TPU v7x, 32 devices: a whole 2x2x4 slice. The times are simulated.
32 devices in a mesh: grp: 2 (over y), row: 4 (over x, core), col: 4 (over z).
Axes of the slice: x: 2, y: 2, z: 4, core: 2. Of those that a mesh axis runs over, the one named last changes fastest.
Arguments:
- values: bfloat16 [8, 4, 2, 27, 128, 128], P(('grp', 'row'), 'col'), parts along dimension 0, may hold values from -0.59765625 to 0.59765625
- pattern: int32 [8, 4, 2, 27], P(('grp', 'row'), 'col'), parts along dimension 0, may hold values from 0 to 1, as said below
Outputs:
- purified: bfloat16 [8, 4, 2, 27, 128, 128], P(('grp', 'row'), 'col'), parts along dimension 0
There are 2 independent parts, one for each index of `grp`. A program takes and returns all parts, laid end to end along the dimension named above; each array names one. Nothing has to cross between parts.
Inputs may be any that keep to these rules, and one draw needn't show every extreme that they name: pattern[x, y, z, 13] = 1 (the cell's own block) everywhere; pattern[x, y, z, k] = 0 wherever z plus the z offset of slot k leaves 0 to 1; every other entry is 0 or 1.
All inputs are finite; a program needn't handle non-finite values.
Results may differ from a plain program's by a relative error of at most 0.005.
Values may be sent and summed in bfloat16 or wider, within the bound.
No kernel may reach another device: no remote copies, remote signals or barrier semaphores. Data moves between devices by JAX's collectives and lax.ppermute only.
A program may use at most 64 MiB of HBM per device.

v0:
```python
import jax
import jax.numpy as jnp
from jax import lax
from jax.sharding import PartitionSpec as P


def with_halo(block, sides, width):
    for axis, dim in sides:
        count = lax.axis_size(axis)
        forward = [(i, i + 1) for i in range(count - 1)]
        forward.append((count - 1, 0))
        backward = [(target, source) for source, target in forward]
        low = lax.ppermute(
            lax.slice_in_dim(block, block.shape[dim] - width, None, axis=dim), axis, forward
        )
        high = lax.ppermute(lax.slice_in_dim(block, 0, width, axis=dim), axis, backward)
        block = jnp.concatenate([low, block, high], axis=dim)
    return block


def slot_offsets():
    offset_list = []
    for along_x in (-1, 0, 1):
        for along_y in (-1, 0, 1):
            for along_z in (-1, 0, 1):
                offset_list.append((along_x, along_y, along_z))
    return offset_list


def pair_groups():
    offset_list = slot_offsets()
    position = {}
    for slot_id, offset in enumerate(offset_list):
        position[offset] = slot_id
    groups = []
    for wanted in offset_list:
        members = []
        for left_slot, shift_vector in enumerate(offset_list):
            remainder = tuple((wanted[axis_id] - shift_vector[axis_id] for axis_id in range(3)))
            if remainder in position:
                members.append((left_slot, position[remainder]))
        groups.append(members)
    return groups


def restricted(left_side, neighbours, presence):
    offset_list = slot_offsets()
    groups = pair_groups()
    thickness = left_side.shape[0]
    width = left_side.shape[2]
    cell_rows = []
    for depth in range(thickness):
        blocks = []
        for target_slot, members in enumerate(groups):
            target_depth = depth + offset_list[target_slot][2]
            valid = []
            if target_depth >= 0 and target_depth < thickness:
                for left_slot, right_slot in members:
                    middle = depth + offset_list[left_slot][2]
                    if middle >= 0 and middle < thickness:
                        valid.append((left_slot, right_slot))
            if not valid:
                blocks.append(jnp.zeros((width, width), jnp.float32))
                continue
            left_joined = jnp.concatenate(
                [left_side[depth, left_slot] for left_slot, right_slot in valid], axis=1
            )
            right_joined = jnp.concatenate(
                [
                    neighbours[offset_list[left_slot][0], offset_list[left_slot][1]][
                        depth + offset_list[left_slot][2], right_slot
                    ]
                    for left_slot, right_slot in valid
                ],
                axis=0,
            )
            blocks.append(jnp.dot(left_joined, right_joined, preferred_element_type=jnp.float32))
        cell_rows.append(jnp.stack(blocks, axis=0))
    stacked = jnp.stack(cell_rows, axis=0)
    return stacked * presence[:, :, None, None].astype(jnp.float32)


def local(values, pattern):
    own_blocks = values[0, 0]
    presence = pattern[0, 0]
    matrix = own_blocks * presence[:, :, None, None].astype(own_blocks.dtype)
    extended = with_halo(matrix[None, None], (("row", 0), ("col", 1)), 1)
    neighbours = {}
    for step_x in (-1, 0, 1):
        for step_y in (-1, 0, 1):
            neighbours[step_x, step_y] = extended[step_x + 1, step_y + 1]
    square = restricted(matrix, neighbours, presence).astype(jnp.bfloat16)
    cubic = restricted(square, neighbours, presence)
    combined = (3.0 * square.astype(jnp.float32) - 2.0 * cubic) * presence[:, :, None, None].astype(
        jnp.float32
    )
    return combined.astype(jnp.bfloat16)[None, None]


def solution(mesh):
    return jax.shard_map(
        local,
        mesh=mesh,
        in_specs=(
            P(("grp", "row"), "col", None, None, None, None),
            P(("grp", "row"), "col", None, None),
        ),
        out_specs=P(("grp", "row"), "col", None, None, None, None),
        check_vma=False,
    )
```

profile of v0, /device:TPU:0, one launch (start us, length us, event | category | flops | bytes accessed | tf_op | source)
XLA Modules:
  0.0 312.1 jit_solution(288815423385075735)
XLA Ops:
  0.0 0.8 convert_bitcast_fusion
  0.8 1.7 broadcast_multiply_fusion
  2.4 0.5 collective-permute-start
  2.9 2.0 collective-permute-start.1
  4.9 36.4 %collective-permute-done = bf16[1,1,2,27,128,128]{5,4,3,2,1,0:T(8,128)(2,1)S(1)} collective-permute-done((bf16[1,1,2,27,128,128]{5,4,3,2,1,0:T(8,128)(2,1)S(1)}, bf16[1,1,2,27,128,128]{5,4,3,2,1,0:T(8,128)(2,1)S(1)}, u32[]{:S(2)}, u32[]{:S(2)}) %collective-permute-start) | collective-permute-done | bytes 1769504 | tf_op jit(solution)/shard_map/ppermute | solution.py:13
  41.4 2.5 collective-permute-done.1
  43.9 0.6 pad_maximum_fusion
  44.5 1.6 collective-permute-start.2
  46.1 2.2 collective-permute-start.3
  48.5 0.6 constant_dynamic-update-slice_fusion.137
  49.2 0.7 constant_dynamic-update-slice_fusion.136
  49.8 0.6 constant_dynamic-update-slice_fusion.277
  50.5 0.7 constant_dynamic-update-slice_fusion.276
  51.2 0.6 constant_dynamic-update-slice_fusion.570
  51.8 0.7 constant_dynamic-update-slice_fusion.135
  52.5 111.2 %collective-permute-done.2 = bf16[3,1,2,27,128,128]{5,4,3,2,1,0:T(8,128)(2,1)S(1)} collective-permute-done((bf16[3,1,2,27,128,128]{5,4,3,2,1,0:T(8,128)(2,1)S(1)}, bf16[3,1,2,27,128,128]{5,4,3,2,1,0:T(8,128)(2,1)S(1)}, u32[]{:S(2)}, u32[]{:S(2)}) %collective-permute-start.2) | collective-permute-done | bytes 5308448 | tf_op jit(solution)/shard_map/ppermute | solution.py:13
  163.7 3.0 slice_bitcast_fusion.1
  166.7 0.9 constant_dynamic-update-slice_fusion.173
  167.6 0.9 constant_dynamic-update-slice_fusion.172
  168.7 108.1 %collective-permute-done.3 = bf16[3,1,2,27,128,128]{5,4,3,2,1,0:T(8,128)(2,1)S(1)} collective-permute-done((bf16[3,1,2,27,128,128]{5,4,3,2,1,0:T(8,128)(2,1)S(1)}, bf16[3,1,2,27,128,128]{5,4,3,2,1,0:T(8,128)(2,1)S(1)}, u32[]{:S(2)}, u32[]{:S(2)}) %collective-permute-start.3) | collective-permute-done | bytes 5308448 | tf_op jit(solution)/shard_map/ppermute | solution.py:16
  276.7 2.1 slice_bitcast_fusion
  279.3 0.7 copy-done.1
  282.9 0.3 constant_dynamic-update-slice_fusion.316
  283.2 0.3 constant_dynamic-update-slice_fusion.315
  284.3 0.3 constant_dynamic-update-slice_fusion.310
  285.2 0.4 constant_dynamic-update-slice_fusion.307
  285.6 0.4 constant_dynamic-update-slice_fusion.306
  286.3 0.3 constant_dynamic-update-slice_fusion.303
  287.2 0.3 constant_dynamic-update-slice_fusion.298
  287.6 0.3 constant_dynamic-update-slice_fusion.297
  288.5 0.3 constant_dynamic-update-slice_fusion.442
  290.0 0.3 constant_dynamic-update-slice_fusion.435
  290.4 0.4 constant_dynamic-update-slice_fusion.433
  290.8 0.4 constant_dynamic-update-slice_fusion.432
  291.5 0.3 constant_dynamic-update-slice_fusion.429
  292.4 0.3 constant_dynamic-update-slice_fusion.424
  292.7 0.5 constant_dynamic-update-slice_fusion.423
  294.4 0.4 fusion.1
  295.4 0.9 copy-done.2
  299.9 0.4 constant_dynamic-update-slice_fusion.557
  300.3 0.4 constant_dynamic-update-slice_fusion.556
  302.2 0.3 constant_dynamic-update-slice_fusion.547
  303.7 0.3 constant_dynamic-update-slice_fusion.692
  305.6 0.4 constant_dynamic-update-slice_fusion.683
  306.0 0.4 constant_dynamic-update-slice_fusion.682
  308.0 0.3 constant_dynamic-update-slice_fusion.673
  308.9 1.0 fusion.5
  309.9 2.2 copy.39
  (221 shorter events, 19.3 us)
Async XLA Ops:
  2.4 45.9 %copy-start = (bf16[1,1,2,27,128,128]{5,4,3,2,1,0:T(8,128)(2,1)S(1)}, bf16[1,1,2,27,128,128]{5,4,3,2,1,0:T(8,128)(2,1)}, u32[]{:S(2)}) copy-start(bf16[1,1,2,27,128,128]{5,4,3,2,1,0:T(8,128)(2,1)} %param.2) | copy-start | bytes 5308420
  2.4 38.9 %collective-permute-start = (bf16[1,1,2,27,128,128]{5,4,3,2,1,0:T(8,128)(2,1)S(1)}, bf16[1,1,2,27,128,128]{5,4,3,2,1,0:T(8,128)(2,1)S(1)}, u32[]{:S(2)}, u32[]{:S(2)}) collective-permute-start(bf16[1,1,2,27,128,128]{5,4,3,2,1,0:T(8,128)(2,1)S(1)} %broadcast_multiply_fusion), channel_id=1, source_target_pairs={{0,4},{4,8},{8,12},{12,0},{1,5},{5,9},{9,13},{13,1},{2,6},{6,10},{... | collective-permute-start | bytes 5308424 | tf_op jit(solution)/shard_map/ppermute | solution.py:13
  2.9 40.9 %collective-permute-start.1 = (bf16[1,1,2,27,128,128]{5,4,3,2,1,0:T(8,128)(2,1)S(1)}, bf16[1,1,2,27,128,128]{5,4,3,2,1,0:T(8,128)(2,1)S(1)}, u32[]{:S(2)}, u32[]{:S(2)}) collective-permute-start(bf16[1,1,2,27,128,128]{5,4,3,2,1,0:T(8,128)(2,1)S(1)} %broadcast_multiply_fusion), channel_id=1, source_target_pairs={{4,0},{8,4},{12,8},{0,12},{5,1},{9,5},{13,9},{1,13},{6,2},{10,6},{... | collective-permute-start | bytes 5308424 | tf_op jit(solution)/shard_map/ppermute | solution.py:16
  44.5 119.2 %collective-permute-start.2 = (bf16[3,1,2,27,128,128]{5,4,3,2,1,0:T(8,128)(2,1)S(1)}, bf16[3,1,2,27,128,128]{5,4,3,2,1,0:T(8,128)(2,1)S(1)}, u32[]{:S(2)}, u32[]{:S(2)}) collective-permute-start(bf16[3,1,2,27,128,128]{5,4,3,2,1,0:T(8,128)(2,1)S(1)} %pad_maximum_fusion), channel_id=1, source_target_pairs={{0,1},{1,2},{2,3},{3,0},{4,5},{5,6},{6,7},{7,4},{8,9},{9,10},{10,1... | collective-permute-start | bytes 15925256 | tf_op jit(solution)/shard_map/ppermute | solution.py:13
  46.1 230.6 %collective-permute-start.3 = (bf16[3,1,2,27,128,128]{5,4,3,2,1,0:T(8,128)(2,1)S(1)}, bf16[3,1,2,27,128,128]{5,4,3,2,1,0:T(8,128)(2,1)S(1)}, u32[]{:S(2)}, u32[]{:S(2)}) collective-permute-start(bf16[3,1,2,27,128,128]{5,4,3,2,1,0:T(8,128)(2,1)S(1)} %pad_maximum_fusion), channel_id=1, source_target_pairs={{1,0},{2,1},{3,2},{0,3},{5,4},{6,5},{7,6},{4,7},{9,8},{10,9},{11,1... | collective-permute-start | bytes 15925256 | tf_op jit(solution)/shard_map/ppermute | solution.py:16
  278.9 1.1 copy-start.1
  279.0 1.1 copy-start.3
  279.0 1.2 copy-start.4
  294.9 1.5 copy-start.2
where the time goes:
time: 315 us; the launch traced here: 312 us
  waiting for transfers between devices  258 us (82%)
  matrix products  22.3 us (7%)
  local copies, waits for them, and re-layouts  19.2 us (6%)
  starting transfers between devices  6.37 us (2%)
  other arithmetic  4.56 us (1%)
    ppermute x2, waiting for transfers between devices, with_halo(): lax.ppermute(lax.slice_in_dim(block, block.shape[dim] - width, None, axis...  148 us
    ppermute x2, waiting for transfers between devices, with_halo(): lax.ppermute(lax.slice_in_dim(block, 0, width, axis=dim), axis, backward)  111 us
    dot_general x72, matrix products, restricted(): jnp.dot(left_joined, right_joined, preferred_element_type=jnp.float32)  22.3 us
    unnamed x168, local copies, waits for them, and re-layouts  11.3 us
  transfers between devices with their start and end apart: 4, of which 4 were waited for; matrix products, arithmetic and copies ran while one was open for 3% of the time, Pallas kernels for 0%

commit v1 on v0

v1 whole, which is shorter than its diff:
```python
import functools

import jax
import jax.numpy as jnp
from jax import lax
from jax.experimental import pallas as pl
from jax.experimental.pallas import tpu as pltpu
from jax.sharding import PartitionSpec as P

STEPS = (-1, 0, 1)


def tile_index(along_u, along_y):
    return (along_u + 1) * 3 + along_y + 1


def pack_kernel(flip, keep, values, mat, x_out, n_out, *z_out):
    width = values.shape[-1]
    sign = flip[0]
    z_up = dict(zip((0, 1, -1), z_out[:3]))
    z_down = dict(zip((0, 1, -1), z_out[3:]))
    for along_u in (0, 1, -1):
        for along_y in STEPS:
            base = 3 * ((sign * along_u + 1) * 3 + along_y + 1) + 1
            targets = [mat.at[tile_index(along_u, along_y)]]
            if along_u >= 0:
                targets.append(x_out.at[along_u * 3 + along_y + 1])
            if along_u <= 0:
                targets.append(n_out.at[-along_u * 3 + along_y + 1])
            if along_y >= 0:
                targets.append(z_up[along_u].at[along_y])
            if along_y <= 0:
                targets.append(z_down[along_u].at[along_y + 1])
            for low in range(2):
                for high in range(2):
                    slot = base + high - low
                    block = values[low, slot] * keep[low, slot].astype(jnp.float32).astype(values.dtype)
                    for target in targets:
                        target[pl.ds(low * width, width), pl.ds(high * width, width)] = block


def product_kernel(flip, keep, mat, x_in, n_in, *rest):
    zu = dict(zip((0, 1, -1), rest[0:3]))
    zd = dict(zip((0, 1, -1), rest[3:6]))
    xu = dict(zip((0, 1), rest[6:8]))
    xd = dict(zip((0, 1), rest[8:10]))
    nu = dict(zip((0, -1), rest[10:12]))
    nd = dict(zip((0, -1), rest[12:14]))
    out, square = rest[14:]
    width = out.shape[-1]
    sign = flip[0]

    def factor(a, c):
        (au, ay), (cu, cy) = a, c
        if au == 0 and ay == 0:
            return mat[tile_index(cu, cy)]
        if ay == 0:
            return (x_in if au > 0 else n_in)[abs(cu) * 3 + cy + 1]
        if au == 0:
            return (zu if ay < 0 else zd)[cu][cy if ay < 0 else cy + 1]
        if au > 0:
            return (xu if ay < 0 else xd)[-cu][cy if ay < 0 else cy + 1]
        return (nu if ay < 0 else nd)[-cu][cy if ay < 0 else cy + 1]

    def total(left, b):
        lefts, rights = [], []
        for au in STEPS:
            for ay in STEPS:
                c = (b[0] - au, b[1] - ay)
                if abs(c[0]) <= 1 and abs(c[1]) <= 1:
                    lefts.append(left[tile_index(au, ay)])
                    rights.append(factor((au, ay), c))
        return jnp.dot(
            jnp.concatenate(lefts, axis=1), jnp.concatenate(rights, axis=0), preferred_element_type=jnp.float32
        )

    def slots(b):
        base = 3 * ((sign * b[0] + 1) * 3 + b[1] + 1) + 1
        for low in range(2):
            for high in range(2):
                slot = base + high - low
                yield low, high, slot, keep[low, slot].astype(jnp.float32)

    cells = [(bu, by) for bu in STEPS for by in STEPS]
    for b in cells:
        summed = total(mat, b)
        for low, high, slot, kept in slots(b):
            quarter = summed[low * width : (low + 1) * width, high * width : (high + 1) * width] * kept
            square[tile_index(*b), pl.ds(low * width, width), pl.ds(high * width, width)] = quarter.astype(jnp.bfloat16)
    for b in cells:
        summed = total(square, b)
        own = square[tile_index(*b)].astype(jnp.float32)
        for low, high, slot, kept in slots(b):
            rows, columns = slice(low * width, (low + 1) * width), slice(high * width, (high + 1) * width)
            mixed = (3.0 * own[rows, columns] - 2.0 * summed[rows, columns]) * kept
            out[low, slot] = mixed.astype(out.dtype)
    empty = jnp.zeros((width, width), out.dtype)
    for m in range(9):
        out[0, 3 * m] = empty
        out[1, 3 * m + 2] = empty


def local(values, pattern):
    blocks, keep = values[0, 0], pattern[0, 0]
    dtype, width = blocks.dtype, blocks.shape[-1]
    side = 2 * width
    rows, cols = lax.axis_size("row"), lax.axis_size("col")
    flip = (2 * lax.rem(lax.axis_index("row"), 2) - 1).reshape(1)

    near, far = [], []
    for i in range(0, rows, 2):
        near += [(i, i + 1), (i + 1, i)]
        far += [(i + 1, (i + 2) % rows), ((i + 2) % rows, i + 1)]
    up = [(i, (i + 1) % cols) for i in range(cols)]
    down = [(i, (i - 1) % cols) for i in range(cols)]

    def tiles(count):
        return jax.ShapeDtypeStruct((count, side, side), dtype)

    smem = pl.BlockSpec(memory_space=pltpu.SMEM)
    vmem = pl.BlockSpec(memory_space=pltpu.VMEM)
    mat, x_out, n_out, *z_out = pl.pallas_call(
        pack_kernel,
        out_shape=[tiles(9), tiles(6), tiles(6)] + [tiles(2)] * 6,
        in_specs=[smem, smem, vmem],
        out_specs=[vmem] * 9,
        compiler_params=pltpu.CompilerParams(vmem_limit_bytes=16 << 20),
        name="pack",
    )(flip, keep, blocks)

    x_in = lax.ppermute(x_out, "row", far)
    zu0 = lax.ppermute(z_out[0], "col", up)
    zd0 = lax.ppermute(z_out[3], "col", down)
    zu1 = lax.ppermute(z_out[1], "col", up)
    zd1 = lax.ppermute(z_out[4], "col", down)
    xu0 = lax.ppermute(zu0, "row", far)
    xd0 = lax.ppermute(zd0, "row", far)
    zu2 = lax.ppermute(z_out[2], "col", up)
    zd2 = lax.ppermute(z_out[5], "col", down)
    xu1 = lax.ppermute(zu1, "row", far)
    xd1 = lax.ppermute(zd1, "row", far)
    n_in = lax.ppermute(n_out, "row", near)
    nu0 = lax.ppermute(zu0, "row", near)
    nd0 = lax.ppermute(zd0, "row", near)
    nu2 = lax.ppermute(zu2, "row", near)
    nd2 = lax.ppermute(zd2, "row", near)

    purified = pl.pallas_call(
        product_kernel,
        out_shape=jax.ShapeDtypeStruct(blocks.shape, dtype),
        in_specs=[smem, smem] + [vmem] * 17,
        out_specs=vmem,
        scratch_shapes=[pltpu.VMEM((9, side, side), dtype)],
        compiler_params=pltpu.CompilerParams(vmem_limit_bytes=24 << 20),
        name="product",
    )(flip, keep, mat, x_in, n_in, zu0, zu1, zu2, zd0, zd1, zd2, xu0, xu1, xd0, xd1, nu0, nu2, nd0, nd2)
    return purified[None, None]


def solution(mesh):
    return jax.shard_map(
        local,
        mesh=mesh,
        in_specs=(
            P(("grp", "row"), "col", None, None, None, None),
            P(("grp", "row"), "col", None, None),
        ),
        out_specs=P(("grp", "row"), "col", None, None, None, None),
        check_vma=False,
    )
```

time: 315 us -> 90.4 us (0.29)
  the two profiles are of different devices: /device:TPU:0 before, /device:TPU:17 now
where the time goes in v1:
time: 90.4 us; the launch traced here: 90.2 us
  waiting for transfers between devices  50.1 us (55%)
  starting transfers between devices  31.3 us (35%)
  Pallas kernels  6.56 us (7%)
  local copies, waits for them, and re-layouts  2.17 us (2%)
    ppermute x1, waiting for transfers between devices, local(): xu1 = lax.ppermute(zu1, 'row', far)  22.1 us
    ppermute x1, starting transfers between devices, local(): xu0 = lax.ppermute(zu0, 'row', far)  19.4 us
    ppermute x1, waiting for transfers between devices, local(): xd0 = lax.ppermute(zd0, 'row', far)  6.71 us
    ppermute x1, waiting for transfers between devices, local(): zu1 = lax.ppermute(z_out[1], 'col', up)  5.45 us
    pallas_call x1, Pallas kernels, local(): pl.pallas_call(product_kernel, out_shape=jax.ShapeDtypeStruct(blocks.shap...  5.45 us
    ppermute x1, waiting for transfers between devices, local(): xd1 = lax.ppermute(zd1, 'row', far)  5.03 us
    ppermute x1, waiting for transfers between devices, local(): xu0 = lax.ppermute(zu0, 'row', far)  4.88 us
    ppermute x1, waiting for transfers between devices, local(): zu2 = lax.ppermute(z_out[2], 'col', up)  3.03 us
  transfers between devices with their start and end apart: 16, of which 7 were waited for; matrix products, arithmetic and copies ran while one was open for 0% of the time, Pallas kernels for 0%

profile of v1, /device:TPU:17, one launch (start us, length us, event | category | flops | bytes accessed | tf_op | source)
XLA Modules:
  0.0 90.2 jit_solution(70732944253179996)
XLA Ops:
  0.0 0.0 copy-start.2
  0.0 0.0 copy-start
  0.0 1.5 %copy-done = bf16[1,1,2,27,128,128]{5,4,3,2,1,0:T(8,128)(2,1)S(1)} copy-done((bf16[1,1,2,27,128,128]{5,4,3,2,1,0:T(8,128)(2,1)S(1)}, bf16[1,1,2,27,128,128]{5,4,3,2,1,0:T(8,128)(2,1)}, u32[]{:S(2)}) %copy-start) | copy-done | bytes 1769496
  1.5 0.0 copy-start.1
  1.5 0.7 copy-done.1
  2.2 1.1 %pack.1 = (bf16[9,256,256]{2,1,0:T(8,128)(2,1)S(1)}, bf16[6,256,256]{2,1,0:T(8,128)(2,1)S(1)}, bf16[6,256,256]{2,1,0:T(8,128)(2,1)S(1)}, bf16[2,256,256]{2,1,0:T...) custom-call(s32[1]{0:T(128)} %bitcast.flip, ...), custom_call_target="tpu_custom_call" | custom-call | tf_op jit(solution)/shard_map/pack/pallas_call | solution.py:122
  3.3 1.3 %collective-permute-start.2 = (bf16[2,256,256]{2,1,0:T(8,128)(2,1)S(1)}, bf16[2,256,256]{2,1,0:T(8,128)(2,1)S(1)}, u32[]{:S(2)}, u32[]{:S(2)}) collective-permute-start(bf16[2,256,256]{2,1,0:T(8,128)(2,1)S(1)} %get-tuple-element.17), channel_id=1, source_target_pairs={{0,1},{1,2},{2,3},{3,0},{4,5},{5,6},{6,7},{7,4},{8,9},{9,10},{10,1... | collective-permute-start | bytes 786440 | tf_op jit(solution)/shard_map/ppermute | solution.py:132
  4.6 0.1 collective-permute-start.3
  4.7 1.2 %collective-permute-start.4 = (bf16[2,256,256]{2,1,0:T(8,128)(2,1)S(1)}, bf16[2,256,256]{2,1,0:T(8,128)(2,1)S(1)}, u32[]{:S(2)}, u32[]{:S(2)}) collective-permute-start(bf16[2,256,256]{2,1,0:T(8,128)(2,1)S(1)} %get-tuple-element.19), channel_id=1, source_target_pairs={{0,1},{1,2},{2,3},{3,0},{4,5},{5,6},{6,7},{7,4},{8,9},{9,10},{10,1... | collective-permute-start | bytes 786440 | tf_op jit(solution)/shard_map/ppermute | solution.py:138
  5.9 0.3 collective-permute-start.5
  6.2 1.4 %collective-permute-start.6 = (bf16[2,256,256]{2,1,0:T(8,128)(2,1)S(1)}, bf16[2,256,256]{2,1,0:T(8,128)(2,1)S(1)}, u32[]{:S(2)}, u32[]{:S(2)}) collective-permute-start(bf16[2,256,256]{2,1,0:T(8,128)(2,1)S(1)} %get-tuple-element.21), channel_id=1, source_target_pairs={{0,3},{1,0},{2,1},{3,2},{4,7},{5,4},{6,5},{7,6},{8,11},{9,8},{10,9... | collective-permute-start | bytes 786440 | tf_op jit(solution)/shard_map/ppermute | solution.py:135
  7.6 2.9 %collective-permute-done.2.rest_0_ = bf16[2,256,256]{2,1,0:T(8,128)(2,1)S(1)} collective-permute-done((bf16[2,256,256]{2,1,0:T(8,128)(2,1)S(1)}, bf16[2,256,256]{2,1,0:T(8,128)(2,1)S(1)}, u32[]{:S(2)}, u32[]{:S(2)}) %collective-permute-start.2) | collective-permute-done | bytes 262176 | tf_op jit(solution)/shard_map/ppermute | solution.py:132
  10.5 0.2 collective-permute-start.7
  10.7 5.4 %collective-permute-done.3.rest_1_ = bf16[2,256,256]{2,1,0:T(8,128)(2,1)S(1)} collective-permute-done((bf16[2,256,256]{2,1,0:T(8,128)(2,1)S(1)}, bf16[2,256,256]{2,1,0:T(8,128)(2,1)S(1)}, u32[]{:S(2)}, u32[]{:S(2)}) %collective-permute-start.3) | collective-permute-done | bytes 262176 | tf_op jit(solution)/shard_map/ppermute | solution.py:134
  16.1 2.7 %collective-permute-start.12 = (bf16[2,256,256]{2,1,0:T(8,128)(2,1)S(1)}, bf16[2,256,256]{2,1,0:T(8,128)(2,1)S(1)}, u32[]{:S(2)}, u32[]{:S(2)}) collective-permute-start(bf16[2,256,256]{2,1,0:T(8,128)(2,1)S(1)} %collective-permute-done.2.rest_0_), channel_id=1, source_target_pairs={{0,4},{4,0},{8,12},{12,8},{1,5},{5,1},{9,13},{13,9},{2,6},{6,2},{1... | collective-permute-start | bytes 786440 | tf_op jit(solution)/shard_map/ppermute | solution.py:143
  18.8 3.0 %collective-permute-done.4.rest_2_ = bf16[2,256,256]{2,1,0:T(8,128)(2,1)S(1)} collective-permute-done((bf16[2,256,256]{2,1,0:T(8,128)(2,1)S(1)}, bf16[2,256,256]{2,1,0:T(8,128)(2,1)S(1)}, u32[]{:S(2)}, u32[]{:S(2)}) %collective-permute-start.4) | collective-permute-done | bytes 262176 | tf_op jit(solution)/shard_map/ppermute | solution.py:138
  21.9 19.4 %collective-permute-start.8 = (bf16[2,256,256]{2,1,0:T(8,128)(2,1)S(1)}, bf16[2,256,256]{2,1,0:T(8,128)(2,1)S(1)}, u32[]{:S(2)}, u32[]{:S(2)}) collective-permute-start(bf16[2,256,256]{2,1,0:T(8,128)(2,1)S(1)} %collective-permute-done.2.rest_0_), channel_id=1, source_target_pairs={{4,8},{8,4},{12,0},{0,12},{5,9},{9,5},{13,1},{1,13},{6,10},{10,6},... | collective-permute-start | bytes 786440 | tf_op jit(solution)/shard_map/ppermute | solution.py:136
  41.3 0.0 collective-permute-done.5.rest_3_
  41.3 0.0 collective-permute-start
  41.3 0.0 collective-permute-done.6.rest_4_
  41.3 0.6 collective-permute-start.1
  41.9 0.0 collective-permute-done.7.rest_5_
  41.9 1.2 %collective-permute-start.9 = (bf16[2,256,256]{2,1,0:T(8,128)(2,1)S(1)}, bf16[2,256,256]{2,1,0:T(8,128)(2,1)S(1)}, u32[]{:S(2)}, u32[]{:S(2)}) collective-permute-start(bf16[2,256,256]{2,1,0:T(8,128)(2,1)S(1)} %collective-permute-done.3.rest_1_), channel_id=1, source_target_pairs={{4,8},{8,4},{12,0},{0,12},{5,9},{9,5},{13,1},{1,13},{6,10},{10,6},... | collective-permute-start | bytes 786440 | tf_op jit(solution)/shard_map/ppermute | solution.py:140
  43.1 0.0 collective-permute-done.12.rest_10_
  43.1 0.4 collective-permute-start.13
  43.5 4.9 %collective-permute-done.8.rest_6_ = bf16[2,256,256]{2,1,0:T(8,128)(2,1)S(1)} collective-permute-done((bf16[2,256,256]{2,1,0:T(8,128)(2,1)S(1)}, bf16[2,256,256]{2,1,0:T(8,128)(2,1)S(1)}, u32[]{:S(2)}, u32[]{:S(2)}) %collective-permute-start.8) | collective-permute-done | bytes 262176 | tf_op jit(solution)/shard_map/ppermute | solution.py:136
  48.4 0.3 collective-permute-start.14
  48.7 22.1 %collective-permute-done.9.rest_7_ = bf16[2,256,256]{2,1,0:T(8,128)(2,1)S(1)} collective-permute-done((bf16[2,256,256]{2,1,0:T(8,128)(2,1)S(1)}, bf16[2,256,256]{2,1,0:T(8,128)(2,1)S(1)}, u32[]{:S(2)}, u32[]{:S(2)}) %collective-permute-start.9) | collective-permute-done | bytes 262176 | tf_op jit(solution)/shard_map/ppermute | solution.py:140
  70.8 0.6 collective-permute-start.10
  71.4 0.0 collective-permute-done.13.rest_11_
  71.4 1.1 %collective-permute-start.11 = (bf16[2,256,256]{2,1,0:T(8,128)(2,1)S(1)}, bf16[2,256,256]{2,1,0:T(8,128)(2,1)S(1)}, u32[]{:S(2)}, u32[]{:S(2)}) collective-permute-start(bf16[2,256,256]{2,1,0:T(8,128)(2,1)S(1)} %collective-permute-done.6.rest_4_), channel_id=1, source_target_pairs={{4,8},{8,4},{12,0},{0,12},{5,9},{9,5},{13,1},{1,13},{6,10},{10,6},... | collective-permute-start | bytes 786440 | tf_op jit(solution)/shard_map/ppermute | solution.py:141
  72.5 0.0 collective-permute-done.14.rest_12_
  72.5 0.4 collective-permute-start.15
  73.0 6.7 %collective-permute-done.10.rest_8_ = bf16[2,256,256]{2,1,0:T(8,128)(2,1)S(1)} collective-permute-done((bf16[2,256,256]{2,1,0:T(8,128)(2,1)S(1)}, bf16[2,256,256]{2,1,0:T(8,128)(2,1)S(1)}, u32[]{:S(2)}, u32[]{:S(2)}) %collective-permute-start.10) | collective-permute-done | bytes 262176 | tf_op jit(solution)/shard_map/ppermute | solution.py:137
  79.7 5.0 %collective-permute-done.11.rest_9_ = bf16[2,256,256]{2,1,0:T(8,128)(2,1)S(1)} collective-permute-done((bf16[2,256,256]{2,1,0:T(8,128)(2,1)S(1)}, bf16[2,256,256]{2,1,0:T(8,128)(2,1)S(1)}, u32[]{:S(2)}, u32[]{:S(2)}) %collective-permute-start.11) | collective-permute-done | bytes 262176 | tf_op jit(solution)/shard_map/ppermute | solution.py:141
  84.7 0.0 collective-permute-done.15.rest_13_
  84.7 0.0 collective-permute-done.x_in
  84.7 0.0 collective-permute-done.1.n_in
  84.7 0.0 copy-done.2
  84.7 5.4 %product.1 = bf16[2,27,128,128]{3,2,1,0:T(8,128)(2,1)} custom-call(s32[1]{0:T(128)} %bitcast.flip, s32[2,27]{1,0:T(2,128)S(1)} %bitcast.6, bf16[9,256,256]{2,1,0:T(8,128)(2,1)S(1)} %get-tuple-element.14.mat, bf16[6,256,256]{2,1,0:T(8,128)(2,1)S(1)} %collective-permute-done.x_in, bf16[6,256,256]{2,1,0:T(8,128)(2,1)S(1)} %collective-permute-done.1.n_in, ...), custom_call_target="tpu_custom_call" | custom-call | tf_op jit(solution)/shard_map/product/pallas_call | solution.py:148
Async XLA Ops:
  0.0 84.7 %copy-start.2 = (s32[1,1,2,27]{3,2,1,0:T(2,128)S(1)}, s32[1,1,2,27]{3,2,1,0:T(2,128)}, u32[]{:S(2)}) copy-start(s32[1,1,2,27]{3,2,1,0:T(2,128)} %param.3) | copy-start | bytes 652
  0.0 1.5 %copy-start = (bf16[1,1,2,27,128,128]{5,4,3,2,1,0:T(8,128)(2,1)S(1)}, bf16[1,1,2,27,128,128]{5,4,3,2,1,0:T(8,128)(2,1)}, u32[]{:S(2)}) copy-start(bf16[1,1,2,27,128,128]{5,4,3,2,1,0:T(8,128)(2,1)} %param.2) | copy-start | bytes 5308420
  1.5 0.7 copy-start.1
  3.3 7.2 %collective-permute-start.2 = (bf16[2,256,256]{2,1,0:T(8,128)(2,1)S(1)}, bf16[2,256,256]{2,1,0:T(8,128)(2,1)S(1)}, u32[]{:S(2)}, u32[]{:S(2)}) collective-permute-start(bf16[2,256,256]{2,1,0:T(8,128)(2,1)S(1)} %get-tuple-element.17), channel_id=1, source_target_pairs={{0,1},{1,2},{2,3},{3,0},{4,5},{5,6},{6,7},{7,4},{8,9},{9,10},{10,1... | collective-permute-start | bytes 786440 | tf_op jit(solution)/shard_map/ppermute | solution.py:132
  4.6 11.5 %collective-permute-start.3 = (bf16[2,256,256]{2,1,0:T(8,128)(2,1)S(1)}, bf16[2,256,256]{2,1,0:T(8,128)(2,1)S(1)}, u32[]{:S(2)}, u32[]{:S(2)}) collective-permute-start(bf16[2,256,256]{2,1,0:T(8,128)(2,1)S(1)} %get-tuple-element.18), channel_id=1, source_target_pairs={{0,1},{1,2},{2,3},{3,0},{4,5},{5,6},{6,7},{7,4},{8,9},{9,10},{10,1... | collective-permute-start | bytes 786440 | tf_op jit(solution)/shard_map/ppermute | solution.py:134
  4.7 17.2 %collective-permute-start.4 = (bf16[2,256,256]{2,1,0:T(8,128)(2,1)S(1)}, bf16[2,256,256]{2,1,0:T(8,128)(2,1)S(1)}, u32[]{:S(2)}, u32[]{:S(2)}) collective-permute-start(bf16[2,256,256]{2,1,0:T(8,128)(2,1)S(1)} %get-tuple-element.19), channel_id=1, source_target_pairs={{0,1},{1,2},{2,3},{3,0},{4,5},{5,6},{6,7},{7,4},{8,9},{9,10},{10,1... | collective-permute-start | bytes 786440 | tf_op jit(solution)/shard_map/ppermute | solution.py:138
  5.9 35.4 %collective-permute-start.5 = (bf16[2,256,256]{2,1,0:T(8,128)(2,1)S(1)}, bf16[2,256,256]{2,1,0:T(8,128)(2,1)S(1)}, u32[]{:S(2)}, u32[]{:S(2)}) collective-permute-start(bf16[2,256,256]{2,1,0:T(8,128)(2,1)S(1)} %get-tuple-element.20), channel_id=1, source_target_pairs={{0,3},{1,0},{2,1},{3,2},{4,7},{5,4},{6,5},{7,6},{8,11},{9,8},{10,9... | collective-permute-start | bytes 786440 | tf_op jit(solution)/shard_map/ppermute | solution.py:133
  6.2 35.1 %collective-permute-start.6 = (bf16[2,256,256]{2,1,0:T(8,128)(2,1)S(1)}, bf16[2,256,256]{2,1,0:T(8,128)(2,1)S(1)}, u32[]{:S(2)}, u32[]{:S(2)}) collective-permute-start(bf16[2,256,256]{2,1,0:T(8,128)(2,1)S(1)} %get-tuple-element.21), channel_id=1, source_target_pairs={{0,3},{1,0},{2,1},{3,2},{4,7},{5,4},{6,5},{7,6},{8,11},{9,8},{10,9... | collective-permute-start | bytes 786440 | tf_op jit(solution)/shard_map/ppermute | solution.py:135
  10.5 31.4 %collective-permute-start.7 = (bf16[2,256,256]{2,1,0:T(8,128)(2,1)S(1)}, bf16[2,256,256]{2,1,0:T(8,128)(2,1)S(1)}, u32[]{:S(2)}, u32[]{:S(2)}) collective-permute-start(bf16[2,256,256]{2,1,0:T(8,128)(2,1)S(1)} %get-tuple-element.22), channel_id=1, source_target_pairs={{0,3},{1,0},{2,1},{3,2},{4,7},{5,4},{6,5},{7,6},{8,11},{9,8},{10,9... | collective-permute-start | bytes 786440 | tf_op jit(solution)/shard_map/ppermute | solution.py:139
  16.1 26.9 %collective-permute-start.12 = (bf16[2,256,256]{2,1,0:T(8,128)(2,1)S(1)}, bf16[2,256,256]{2,1,0:T(8,128)(2,1)S(1)}, u32[]{:S(2)}, u32[]{:S(2)}) collective-permute-start(bf16[2,256,256]{2,1,0:T(8,128)(2,1)S(1)} %collective-permute-done.2.rest_0_), channel_id=1, source_target_pairs={{0,4},{4,0},{8,12},{12,8},{1,5},{5,1},{9,13},{13,9},{2,6},{6,2},{1... | collective-permute-start | bytes 786440 | tf_op jit(solution)/shard_map/ppermute | solution.py:143
  21.9 26.5 %collective-permute-start.8 = (bf16[2,256,256]{2,1,0:T(8,128)(2,1)S(1)}, bf16[2,256,256]{2,1,0:T(8,128)(2,1)S(1)}, u32[]{:S(2)}, u32[]{:S(2)}) collective-permute-start(bf16[2,256,256]{2,1,0:T(8,128)(2,1)S(1)} %collective-permute-done.2.rest_0_), channel_id=1, source_target_pairs={{4,8},{8,4},{12,0},{0,12},{5,9},{9,5},{13,1},{1,13},{6,10},{10,6},... | collective-permute-start | bytes 786440 | tf_op jit(solution)/shard_map/ppermute | solution.py:136
  41.3 43.5 %collective-permute-start = (bf16[6,256,256]{2,1,0:T(8,128)(2,1)S(1)}, bf16[6,256,256]{2,1,0:T(8,128)(2,1)S(1)}, u32[]{:S(2)}, u32[]{:S(2)}) collective-permute-start(bf16[6,256,256]{2,1,0:T(8,128)(2,1)S(1)} %get-tuple-element.15), channel_id=1, source_target_pairs={{4,8},{8,4},{12,0},{0,12},{5,9},{9,5},{13,1},{1,13},{6,10},{10,6},... | collective-permute-start | bytes 2359304 | tf_op jit(solution)/shard_map/ppermute | solution.py:131
  41.3 43.4 %collective-permute-start.1 = (bf16[6,256,256]{2,1,0:T(8,128)(2,1)S(1)}, bf16[6,256,256]{2,1,0:T(8,128)(2,1)S(1)}, u32[]{:S(2)}, u32[]{:S(2)}) collective-permute-start(bf16[6,256,256]{2,1,0:T(8,128)(2,1)S(1)} %get-tuple-element.16), channel_id=1, source_target_pairs={{0,4},{4,0},{8,12},{12,8},{1,5},{5,1},{9,13},{13,9},{2,6},{6,2},{1... | collective-permute-start | bytes 2359304 | tf_op jit(solution)/shard_map/ppermute | solution.py:142
  41.9 28.9 %collective-permute-start.9 = (bf16[2,256,256]{2,1,0:T(8,128)(2,1)S(1)}, bf16[2,256,256]{2,1,0:T(8,128)(2,1)S(1)}, u32[]{:S(2)}, u32[]{:S(2)}) collective-permute-start(bf16[2,256,256]{2,1,0:T(8,128)(2,1)S(1)} %collective-permute-done.3.rest_1_), channel_id=1, source_target_pairs={{4,8},{8,4},{12,0},{0,12},{5,9},{9,5},{13,1},{1,13},{6,10},{10,6},... | collective-permute-start | bytes 786440 | tf_op jit(solution)/shard_map/ppermute | solution.py:140
  43.1 28.3 %collective-permute-start.13 = (bf16[2,256,256]{2,1,0:T(8,128)(2,1)S(1)}, bf16[2,256,256]{2,1,0:T(8,128)(2,1)S(1)}, u32[]{:S(2)}, u32[]{:S(2)}) collective-permute-start(bf16[2,256,256]{2,1,0:T(8,128)(2,1)S(1)} %collective-permute-done.4.rest_2_), channel_id=1, source_target_pairs={{0,4},{4,0},{8,12},{12,8},{1,5},{5,1},{9,13},{13,9},{2,6},{6,2},{1... | collective-permute-start | bytes 786440 | tf_op jit(solution)/shard_map/ppermute | solution.py:145
  48.4 24.1 %collective-permute-start.14 = (bf16[2,256,256]{2,1,0:T(8,128)(2,1)S(1)}, bf16[2,256,256]{2,1,0:T(8,128)(2,1)S(1)}, u32[]{:S(2)}, u32[]{:S(2)}) collective-permute-start(bf16[2,256,256]{2,1,0:T(8,128)(2,1)S(1)} %collective-permute-done.5.rest_3_), channel_id=1, source_target_pairs={{0,4},{4,0},{8,12},{12,8},{1,5},{5,1},{9,13},{13,9},{2,6},{6,2},{1... | collective-permute-start | bytes 786440 | tf_op jit(solution)/shard_map/ppermute | solution.py:144
  70.8 8.9 %collective-permute-start.10 = (bf16[2,256,256]{2,1,0:T(8,128)(2,1)S(1)}, bf16[2,256,256]{2,1,0:T(8,128)(2,1)S(1)}, u32[]{:S(2)}, u32[]{:S(2)}) collective-permute-start(bf16[2,256,256]{2,1,0:T(8,128)(2,1)S(1)} %collective-permute-done.5.rest_3_), channel_id=1, source_target_pairs={{4,8},{8,4},{12,0},{0,12},{5,9},{9,5},{13,1},{1,13},{6,10},{10,6},... | collective-permute-start | bytes 786440 | tf_op jit(solution)/shard_map/ppermute | solution.py:137
  71.4 13.3 %collective-permute-start.11 = (bf16[2,256,256]{2,1,0:T(8,128)(2,1)S(1)}, bf16[2,256,256]{2,1,0:T(8,128)(2,1)S(1)}, u32[]{:S(2)}, u32[]{:S(2)}) collective-permute-start(bf16[2,256,256]{2,1,0:T(8,128)(2,1)S(1)} %collective-permute-done.6.rest_4_), channel_id=1, source_target_pairs={{4,8},{8,4},{12,0},{0,12},{5,9},{9,5},{13,1},{1,13},{6,10},{10,6},... | collective-permute-start | bytes 786440 | tf_op jit(solution)/shard_map/ppermute | solution.py:141
  72.5 12.2 %collective-permute-start.15 = (bf16[2,256,256]{2,1,0:T(8,128)(2,1)S(1)}, bf16[2,256,256]{2,1,0:T(8,128)(2,1)S(1)}, u32[]{:S(2)}, u32[]{:S(2)}) collective-permute-start(bf16[2,256,256]{2,1,0:T(8,128)(2,1)S(1)} %collective-permute-done.7.rest_5_), channel_id=1, source_target_pairs={{0,4},{4,0},{8,12},{12,8},{1,5},{5,1},{9,13},{13,9},{2,6},{6,2},{1... | collective-permute-start | bytes 786440 | tf_op jit(solution)/shard_map/ppermute | solution.py:146

commit v2 on v1

--- a/solution.py
+++ b/solution.py
@@ -14,11 +14,9 @@
     return (along_u + 1) * 3 + along_y + 1
 
 
-def pack_kernel(flip, keep, values, mat, x_out, n_out, *z_out):
+def pack_kernel(flip, keep, values, mat, x_out, n_out, up_out, up_last, *down_out):
     width = values.shape[-1]
     sign = flip[0]
-    z_up = dict(zip((0, 1, -1), z_out[:3]))
-    z_down = dict(zip((0, 1, -1), z_out[3:]))
     for along_u in (0, 1, -1):
         for along_y in STEPS:
             base = 3 * ((sign * along_u + 1) * 3 + along_y + 1) + 1
@@ -28,9 +26,9 @@
             if along_u <= 0:
                 targets.append(n_out.at[-along_u * 3 + along_y + 1])
             if along_y >= 0:
-                targets.append(z_up[along_u].at[along_y])
+                targets.append(up_last.at[along_y] if along_u < 0 else up_out.at[along_u * 2 + along_y])
             if along_y <= 0:
-                targets.append(z_down[along_u].at[along_y + 1])
+                targets.append(down_out[along_u % 3].at[along_y + 1])
             for low in range(2):
                 for high in range(2):
                     slot = base + high - low
@@ -39,14 +37,9 @@
                         target[pl.ds(low * width, width), pl.ds(high * width, width)] = block
 
 
-def product_kernel(flip, keep, mat, x_in, n_in, *rest):
-    zu = dict(zip((0, 1, -1), rest[0:3]))
-    zd = dict(zip((0, 1, -1), rest[3:6]))
-    xu = dict(zip((0, 1), rest[6:8]))
-    xd = dict(zip((0, 1), rest[8:10]))
-    nu = dict(zip((0, -1), rest[10:12]))
-    nd = dict(zip((0, -1), rest[12:14]))
-    out, square = rest[14:]
+def product_kernel(flip, keep, mat, x_in, n_in, up_in, up_rest, x_up, n_up, n_up_rest, *rest):
+    down_in, x_down, n_down = rest[0:3], rest[3:5], rest[5:7]
+    out, square = rest[7:]
     width = out.shape[-1]
     sign = flip[0]
 
@@ -56,11 +49,14 @@
             return mat[tile_index(cu, cy)]
         if ay == 0:
             return (x_in if au > 0 else n_in)[abs(cu) * 3 + cy + 1]
-        if au == 0:
-            return (zu if ay < 0 else zd)[cu][cy if ay < 0 else cy + 1]
+        if ay > 0:
+            source = down_in[cu % 3] if au == 0 else x_down[-cu] if au > 0 else n_down[cu]
+            return source[cy + 1]
         if au > 0:
-            return (xu if ay < 0 else xd)[-cu][cy if ay < 0 else cy + 1]
-        return (nu if ay < 0 else nd)[-cu][cy if ay < 0 else cy + 1]
+            return x_up[-cu * 2 + cy]
+        if cu * (1 + au) < 0 or cu > 0 > au:
+            return (up_rest if au == 0 else n_up_rest)[cy]
+        return (up_in if au == 0 else n_up)[cu * (1 + au) * 2 + cy]
 
     def total(left, b):
         lefts, rights = [], []
@@ -119,41 +115,51 @@
 
     smem = pl.BlockSpec(memory_space=pltpu.SMEM)
     vmem = pl.BlockSpec(memory_space=pltpu.VMEM)
-    mat, x_out, n_out, *z_out = pl.pallas_call(
+    mat, x_out, n_out, up_out, up_last, down0, down1, down2 = pl.pallas_call(
         pack_kernel,
-        out_shape=[tiles(9), tiles(6), tiles(6)] + [tiles(2)] * 6,
+        out_shape=[tiles(9), tiles(6), tiles(6), tiles(4)] + [tiles(2)] * 4,
         in_specs=[smem, smem, vmem],
-        out_specs=[vmem] * 9,
+        out_specs=[vmem] * 8,
         compiler_params=pltpu.CompilerParams(vmem_limit_bytes=16 << 20),
         name="pack",
     )(flip, keep, blocks)
 
-    x_in = lax.ppermute(x_out, "row", far)
-    zu0 = lax.ppermute(z_out[0], "col", up)
-    zd0 = lax.ppermute(z_out[3], "col", down)
-    zu1 = lax.ppermute(z_out[1], "col", up)
-    zd1 = lax.ppermute(z_out[4], "col", down)
-    xu0 = lax.ppermute(zu0, "row", far)
-    xd0 = lax.ppermute(zd0, "row", far)
-    zu2 = lax.ppermute(z_out[2], "col", up)
-    zd2 = lax.ppermute(z_out[5], "col", down)
-    xu1 = lax.ppermute(zu1, "row", far)
-    xd1 = lax.ppermute(zd1, "row", far)
-    n_in = lax.ppermute(n_out, "row", near)
-    nu0 = lax.ppermute(zu0, "row", near)
-    nd0 = lax.ppermute(zd0, "row", near)
-    nu2 = lax.ppermute(zu2, "row", near)
-    nd2 = lax.ppermute(zd2, "row", near)
+    def along_col(tile, towards):
+        return lax.ppermute(tile, "col", towards)
+
+    def along_row(tile, towards):
+        return lax.ppermute(tile, "row", towards)
+
+    after = lax.optimization_barrier
+    x_in = along_row(x_out, far)
+    up_in, up_rest = along_col(up_out, up), along_col(up_last, up)
+    up_in, down0, down1 = after((up_in, down0, down1))
+    x_up = along_row(up_in, far)
+    down0, down1 = along_col(down0, down), along_col(down1, down)
+    x_in, down2 = after((x_in, down2))
+    down2 = along_col(down2, down)
+    x_down0 = along_row(down0, far)
+    x_up, down1 = after((x_up, down1))
+    x_down1 = along_row(down1, far)
+    down0, n_out, up_in = after((down0, n_out, up_in))
+    n_in, n_up = along_row(n_out, near), along_row(up_in, near)
+    down1, down0 = after((down1, down0))
+    n_down0 = along_row(down0, near)
+    x_down0, down2, up_rest = after((x_down0, down2, up_rest))
+    n_down2, n_up_rest = along_row(down2, near), along_row(up_rest, near)
 
     purified = pl.pallas_call(
         product_kernel,
         out_shape=jax.ShapeDtypeStruct(blocks.shape, dtype),
-        in_specs=[smem, smem] + [vmem] * 17,
+        in_specs=[smem, smem] + [vmem] * 15,
         out_specs=vmem,
         scratch_shapes=[pltpu.VMEM((9, side, side), dtype)],
         compiler_params=pltpu.CompilerParams(vmem_limit_bytes=24 << 20),
         name="product",
-    )(flip, keep, mat, x_in, n_in, zu0, zu1, zu2, zd0, zd1, zd2, xu0, xu1, xd0, xd1, nu0, nu2, nd0, nd2)
+    )(
+        flip, keep, mat, x_in, n_in, up_in, up_rest, x_up, n_up, n_up_rest,
+        down0, down1, down2, x_down0, x_down1, n_down0, n_down2,
+    )
     return purified[None, None]
 
 

time: 90.4 us -> 55.2 us (0.61)
  the two profiles are of different devices: /device:TPU:17 before, /device:TPU:0 now
where the time goes in v2:
time: 55.2 us; the launch traced here: 55.1 us
  waiting for transfers between devices  34.9 us (63%)
  starting transfers between devices  11.4 us (21%)
  Pallas kernels  6.56 us (12%)
  local copies, waits for them, and re-layouts  2.17 us (4%)
    ppermute x5, waiting for transfers between devices, along_col(): return lax.ppermute(tile, 'col', towards)  29.3 us
    ppermute x5, starting transfers between devices, along_col(): return lax.ppermute(tile, 'col', towards)  7.16 us
    ppermute x9, waiting for transfers between devices, along_row(): return lax.ppermute(tile, 'row', towards)  5.63 us
    pallas_call x1, Pallas kernels, local(): pl.pallas_call(product_kernel, out_shape=jax.ShapeDtypeStruct(blocks.shap...  5.45 us
    ppermute x9, starting transfers between devices, along_row(): return lax.ppermute(tile, 'row', towards)  4.23 us
    unnamed x6, local copies, waits for them, and re-layouts  2.17 us
    pallas_call x1, Pallas kernels, local(): pl.pallas_call(pack_kernel, out_shape=[tiles(9), tiles(6), tiles(6), tile...  1.11 us
  transfers between devices with their start and end apart: 14, of which 8 were waited for; matrix products, arithmetic and copies ran while one was open for 0% of the time, Pallas kernels for 0%

profile of v2, /device:TPU:0, one launch (start us, length us, event | category | flops | bytes accessed | tf_op | source)
XLA Modules:
  0.0 55.1 jit_solution(8865716794405773522)
XLA Ops:
  0.0 0.0 copy-start.2
  0.0 0.0 copy-start
  0.0 1.5 %copy-done = bf16[1,1,2,27,128,128]{5,4,3,2,1,0:T(8,128)(2,1)S(1)} copy-done((bf16[1,1,2,27,128,128]{5,4,3,2,1,0:T(8,128)(2,1)S(1)}, bf16[1,1,2,27,128,128]{5,4,3,2,1,0:T(8,128)(2,1)}, u32[]{:S(2)}) %copy-start) | copy-done | bytes 1769496
  1.5 0.0 copy-start.1
  1.5 0.7 %copy-done.1 = s32[1,1,2,27]{3,2,1,0:T(2,128)S(1)} copy-done((s32[1,1,2,27]{3,2,1,0:T(2,128)S(1)}, s32[1,1,2,27]{3,2,1,0:T(2,128)}, u32[]{:S(2)}) %copy-start.1) | copy-done | bytes 240
  2.2 1.1 %pack.1 = (bf16[9,256,256]{2,1,0:T(8,128)(2,1)S(1)}, bf16[6,256,256]{2,1,0:T(8,128)(2,1)S(1)}, bf16[6,256,256]{2,1,0:T(8,128)(2,1)S(1)}, bf16[4,256,256]{2,1,0:T...) custom-call(s32[1]{0:T(128)} %bitcast.flip, ...), custom_call_target="tpu_custom_call" | custom-call | tf_op jit(solution)/shard_map/pack/pallas_call | solution.py:118
  3.3 3.1 %collective-permute-start.1 = (bf16[4,256,256]{2,1,0:T(8,128)(2,1)S(1)}, bf16[4,256,256]{2,1,0:T(8,128)(2,1)S(1)}, u32[]{:S(2)}, u32[]{:S(2)}) collective-permute-start(bf16[4,256,256]{2,1,0:T(8,128)(2,1)S(1)} %get-tuple-element.32), channel_id=1, source_target_pairs={{0,1},{1,2},{2,3},{3,0},{4,5},{5,6},{6,7},{7,4},{8,9},{9,10},{10,1... | collective-permute-start | bytes 1572872 | tf_op jit(solution)/shard_map/ppermute | solution.py:128
  6.4 0.7 %collective-permute-start = (bf16[6,256,256]{2,1,0:T(8,128)(2,1)S(1)}, bf16[6,256,256]{2,1,0:T(8,128)(2,1)S(1)}, u32[]{:S(2)}, u32[]{:S(2)}) collective-permute-start(bf16[6,256,256]{2,1,0:T(8,128)(2,1)S(1)} %get-tuple-element.29), channel_id=1, source_target_pairs={{4,8},{8,4},{12,0},{0,12},{5,9},{9,5},{13,1},{1,13},{6,10},{10,6},... | collective-permute-start | bytes 2359304 | tf_op jit(solution)/shard_map/ppermute | solution.py:131
  7.0 13.3 %collective-permute-done.1.up_in = bf16[4,256,256]{2,1,0:T(8,128)(2,1)S(1)} collective-permute-done((bf16[4,256,256]{2,1,0:T(8,128)(2,1)S(1)}, bf16[4,256,256]{2,1,0:T(8,128)(2,1)S(1)}, u32[]{:S(2)}, u32[]{:S(2)}) %collective-permute-start.1) | collective-permute-done | bytes 524320 | tf_op jit(solution)/shard_map/ppermute | solution.py:128
  20.3 0.1 collective-permute-start.7
  20.5 1.7 %collective-permute-start.2 = (bf16[2,256,256]{2,1,0:T(8,128)(2,1)S(1)}, bf16[2,256,256]{2,1,0:T(8,128)(2,1)S(1)}, u32[]{:S(2)}, u32[]{:S(2)}) collective-permute-start(bf16[2,256,256]{2,1,0:T(8,128)(2,1)S(1)} %get-tuple-element.35), channel_id=1, source_target_pairs={{0,3},{1,0},{2,1},{3,2},{4,7},{5,4},{6,5},{7,6},{8,11},{9,8},{10,9... | collective-permute-start | bytes 786440 | tf_op jit(solution)/shard_map/ppermute | solution.py:128
  22.1 0.4 collective-permute-start.8
  22.6 6.6 %collective-permute-done.2.rest_0_ = bf16[2,256,256]{2,1,0:T(8,128)(2,1)S(1)} collective-permute-done((bf16[2,256,256]{2,1,0:T(8,128)(2,1)S(1)}, bf16[2,256,256]{2,1,0:T(8,128)(2,1)S(1)}, u32[]{:S(2)}, u32[]{:S(2)}) %collective-permute-start.2) | collective-permute-done | bytes 262176 | tf_op jit(solution)/shard_map/ppermute | solution.py:128
  29.2 1.0 %collective-permute-start.9 = (bf16[4,256,256]{2,1,0:T(8,128)(2,1)S(1)}, bf16[4,256,256]{2,1,0:T(8,128)(2,1)S(1)}, u32[]{:S(2)}, u32[]{:S(2)}) collective-permute-start(bf16[4,256,256]{2,1,0:T(8,128)(2,1)S(1)} %collective-permute-done.1.up_in), channel_id=1, source_target_pairs={{0,4},{4,0},{8,12},{12,8},{1,5},{5,1},{9,13},{13,9},{2,6},{6,2},{1... | collective-permute-start | bytes 1572872 | tf_op jit(solution)/shard_map/ppermute | solution.py:131
  30.2 0.0 collective-permute-start.3
  30.2 0.0 collective-permute-done.x_in
  30.2 0.0 collective-permute-start.6
  30.2 4.6 %collective-permute-done.8.rest_1_ = bf16[2,256,256]{2,1,0:T(8,128)(2,1)S(1)} collective-permute-done((bf16[2,256,256]{2,1,0:T(8,128)(2,1)S(1)}, bf16[2,256,256]{2,1,0:T(8,128)(2,1)S(1)}, u32[]{:S(2)}, u32[]{:S(2)}) %collective-permute-start.8) | collective-permute-done | bytes 262176 | tf_op jit(solution)/shard_map/ppermute | solution.py:128
  34.8 0.9 %collective-permute-start.4 = (bf16[2,256,256]{2,1,0:T(8,128)(2,1)S(1)}, bf16[2,256,256]{2,1,0:T(8,128)(2,1)S(1)}, u32[]{:S(2)}, u32[]{:S(2)}) collective-permute-start(bf16[2,256,256]{2,1,0:T(8,128)(2,1)S(1)} %collective-permute-done.2.rest_0_), channel_id=1, source_target_pairs={{4,8},{8,4},{12,0},{0,12},{5,9},{9,5},{13,1},{1,13},{6,10},{10,6},... | collective-permute-start | bytes 786440 | tf_op jit(solution)/shard_map/ppermute | solution.py:131
  35.7 1.7 %collective-permute-done.7.x_up = bf16[4,256,256]{2,1,0:T(8,128)(2,1)S(1)} collective-permute-done((bf16[4,256,256]{2,1,0:T(8,128)(2,1)S(1)}, bf16[4,256,256]{2,1,0:T(8,128)(2,1)S(1)}, u32[]{:S(2)}, u32[]{:S(2)}) %collective-permute-start.7) | collective-permute-done | bytes 524320 | tf_op jit(solution)/shard_map/ppermute | solution.py:131
  37.4 2.0 %collective-permute-start.5 = (bf16[2,256,256]{2,1,0:T(8,128)(2,1)S(1)}, bf16[2,256,256]{2,1,0:T(8,128)(2,1)S(1)}, u32[]{:S(2)}, u32[]{:S(2)}) collective-permute-start(bf16[2,256,256]{2,1,0:T(8,128)(2,1)S(1)} %get-tuple-element.40), channel_id=1, source_target_pairs={{0,3},{1,0},{2,1},{3,2},{4,7},{5,4},{6,5},{7,6},{8,11},{9,8},{10,9... | collective-permute-start | bytes 786440 | tf_op jit(solution)/shard_map/ppermute | solution.py:128
  39.4 1.7 %collective-permute-done.6.up_rest = bf16[2,256,256]{2,1,0:T(8,128)(2,1)S(1)} collective-permute-done((bf16[2,256,256]{2,1,0:T(8,128)(2,1)S(1)}, bf16[2,256,256]{2,1,0:T(8,128)(2,1)S(1)}, u32[]{:S(2)}, u32[]{:S(2)}) %collective-permute-start.6) | collective-permute-done | bytes 262176 | tf_op jit(solution)/shard_map/ppermute | solution.py:128
  41.0 0.3 collective-permute-start.11
  41.3 1.4 %collective-permute-done.4.rest_3_ = bf16[2,256,256]{2,1,0:T(8,128)(2,1)S(1)} collective-permute-done((bf16[2,256,256]{2,1,0:T(8,128)(2,1)S(1)}, bf16[2,256,256]{2,1,0:T(8,128)(2,1)S(1)}, u32[]{:S(2)}, u32[]{:S(2)}) %collective-permute-start.4) | collective-permute-done | bytes 262176 | tf_op jit(solution)/shard_map/ppermute | solution.py:131
  42.7 0.8 %collective-permute-start.12 = (bf16[2,256,256]{2,1,0:T(8,128)(2,1)S(1)}, bf16[2,256,256]{2,1,0:T(8,128)(2,1)S(1)}, u32[]{:S(2)}, u32[]{:S(2)}) collective-permute-start(bf16[2,256,256]{2,1,0:T(8,128)(2,1)S(1)} %collective-permute-done.2.rest_0_), channel_id=1, source_target_pairs={{0,4},{4,0},{8,12},{12,8},{1,5},{5,1},{9,13},{13,9},{2,6},{6,2},{1... | collective-permute-start | bytes 786440 | tf_op jit(solution)/shard_map/ppermute | solution.py:131
  43.5 3.0 %collective-permute-done.5.rest_2_ = bf16[2,256,256]{2,1,0:T(8,128)(2,1)S(1)} collective-permute-done((bf16[2,256,256]{2,1,0:T(8,128)(2,1)S(1)}, bf16[2,256,256]{2,1,0:T(8,128)(2,1)S(1)}, u32[]{:S(2)}, u32[]{:S(2)}) %collective-permute-start.5) | collective-permute-done | bytes 262176 | tf_op jit(solution)/shard_map/ppermute | solution.py:128
  46.6 0.0 collective-permute-start.10
  46.6 0.0 collective-permute-done.9.n_up
  46.6 0.5 collective-permute-start.13
  47.1 0.0 collective-permute-done.12.rest_5_
  47.1 2.5 %collective-permute-done.11.rest_4_ = bf16[2,256,256]{2,1,0:T(8,128)(2,1)S(1)} collective-permute-done((bf16[2,256,256]{2,1,0:T(8,128)(2,1)S(1)}, bf16[2,256,256]{2,1,0:T(8,128)(2,1)S(1)}, u32[]{:S(2)}, u32[]{:S(2)}) %collective-permute-start.11) | collective-permute-done | bytes 262176 | tf_op jit(solution)/shard_map/ppermute | solution.py:131
  49.6 0.0 collective-permute-done.10.n_up_rest
  49.6 0.0 collective-permute-done.13.rest_6_
  49.6 0.0 collective-permute-done.3.n_in
  49.6 0.0 copy-done.2
  49.6 5.4 %product.1 = bf16[2,27,128,128]{3,2,1,0:T(8,128)(2,1)} custom-call(s32[1]{0:T(128)} %bitcast.flip, s32[2,27]{1,0:T(2,128)S(1)} %bitcast.6, bf16[9,256,256]{2,1,0:T(8,128)(2,1)S(1)} %get-tuple-element.28.mat, bf16[6,256,256]{2,1,0:T(8,128)(2,1)S(1)} %collective-permute-done.x_in, bf16[6,256,256]{2,1,0:T(8,128)(2,1)S(1)} %collective-permute-done.3.n_in, ...), custom_call_target="tpu_custom_call" | custom-call | tf_op jit(solution)/shard_map/product/pallas_call | solution.py:151
Async XLA Ops:
  0.0 49.6 %copy-start.2 = (s32[1,1,2,27]{3,2,1,0:T(2,128)S(1)}, s32[1,1,2,27]{3,2,1,0:T(2,128)}, u32[]{:S(2)}) copy-start(s32[1,1,2,27]{3,2,1,0:T(2,128)} %param.3) | copy-start | bytes 652
  0.0 1.5 %copy-start = (bf16[1,1,2,27,128,128]{5,4,3,2,1,0:T(8,128)(2,1)S(1)}, bf16[1,1,2,27,128,128]{5,4,3,2,1,0:T(8,128)(2,1)}, u32[]{:S(2)}) copy-start(bf16[1,1,2,27,128,128]{5,4,3,2,1,0:T(8,128)(2,1)} %param.2) | copy-start | bytes 5308420
  1.5 0.7 %copy-start.1 = (s32[1,1,2,27]{3,2,1,0:T(2,128)S(1)}, s32[1,1,2,27]{3,2,1,0:T(2,128)}, u32[]{:S(2)}) copy-start(s32[1,1,2,27]{3,2,1,0:T(2,128)} %param.3) | copy-start | bytes 652
  3.3 17.0 %collective-permute-start.1 = (bf16[4,256,256]{2,1,0:T(8,128)(2,1)S(1)}, bf16[4,256,256]{2,1,0:T(8,128)(2,1)S(1)}, u32[]{:S(2)}, u32[]{:S(2)}) collective-permute-start(bf16[4,256,256]{2,1,0:T(8,128)(2,1)S(1)} %get-tuple-element.32), channel_id=1, source_target_pairs={{0,1},{1,2},{2,3},{3,0},{4,5},{5,6},{6,7},{7,4},{8,9},{9,10},{10,1... | collective-permute-start | bytes 1572872 | tf_op jit(solution)/shard_map/ppermute | solution.py:128
  6.4 23.8 %collective-permute-start = (bf16[6,256,256]{2,1,0:T(8,128)(2,1)S(1)}, bf16[6,256,256]{2,1,0:T(8,128)(2,1)S(1)}, u32[]{:S(2)}, u32[]{:S(2)}) collective-permute-start(bf16[6,256,256]{2,1,0:T(8,128)(2,1)S(1)} %get-tuple-element.29), channel_id=1, source_target_pairs={{4,8},{8,4},{12,0},{0,12},{5,9},{9,5},{13,1},{1,13},{6,10},{10,6},... | collective-permute-start | bytes 2359304 | tf_op jit(solution)/shard_map/ppermute | solution.py:131
  20.3 17.1 %collective-permute-start.7 = (bf16[4,256,256]{2,1,0:T(8,128)(2,1)S(1)}, bf16[4,256,256]{2,1,0:T(8,128)(2,1)S(1)}, u32[]{:S(2)}, u32[]{:S(2)}) collective-permute-start(bf16[4,256,256]{2,1,0:T(8,128)(2,1)S(1)} %collective-permute-done.1.up_in), channel_id=1, source_target_pairs={{4,8},{8,4},{12,0},{0,12},{5,9},{9,5},{13,1},{1,13},{6,10},{10,6},... | collective-permute-start | bytes 1572872 | tf_op jit(solution)/shard_map/ppermute | solution.py:131
  20.5 8.7 %collective-permute-start.2 = (bf16[2,256,256]{2,1,0:T(8,128)(2,1)S(1)}, bf16[2,256,256]{2,1,0:T(8,128)(2,1)S(1)}, u32[]{:S(2)}, u32[]{:S(2)}) collective-permute-start(bf16[2,256,256]{2,1,0:T(8,128)(2,1)S(1)} %get-tuple-element.35), channel_id=1, source_target_pairs={{0,3},{1,0},{2,1},{3,2},{4,7},{5,4},{6,5},{7,6},{8,11},{9,8},{10,9... | collective-permute-start | bytes 786440 | tf_op jit(solution)/shard_map/ppermute | solution.py:128
  22.1 12.7 %collective-permute-start.8 = (bf16[2,256,256]{2,1,0:T(8,128)(2,1)S(1)}, bf16[2,256,256]{2,1,0:T(8,128)(2,1)S(1)}, u32[]{:S(2)}, u32[]{:S(2)}) collective-permute-start(bf16[2,256,256]{2,1,0:T(8,128)(2,1)S(1)} %get-tuple-element.43), channel_id=1, source_target_pairs={{0,3},{1,0},{2,1},{3,2},{4,7},{5,4},{6,5},{7,6},{8,11},{9,8},{10,9... | collective-permute-start | bytes 786440 | tf_op jit(solution)/shard_map/ppermute | solution.py:128
  29.2 17.4 %collective-permute-start.9 = (bf16[4,256,256]{2,1,0:T(8,128)(2,1)S(1)}, bf16[4,256,256]{2,1,0:T(8,128)(2,1)S(1)}, u32[]{:S(2)}, u32[]{:S(2)}) collective-permute-start(bf16[4,256,256]{2,1,0:T(8,128)(2,1)S(1)} %collective-permute-done.1.up_in), channel_id=1, source_target_pairs={{0,4},{4,0},{8,12},{12,8},{1,5},{5,1},{9,13},{13,9},{2,6},{6,2},{1... | collective-permute-start | bytes 1572872 | tf_op jit(solution)/shard_map/ppermute | solution.py:131
  30.2 19.4 %collective-permute-start.3 = (bf16[6,256,256]{2,1,0:T(8,128)(2,1)S(1)}, bf16[6,256,256]{2,1,0:T(8,128)(2,1)S(1)}, u32[]{:S(2)}, u32[]{:S(2)}) collective-permute-start(bf16[6,256,256]{2,1,0:T(8,128)(2,1)S(1)} %get-tuple-element.38), channel_id=1, source_target_pairs={{0,4},{4,0},{8,12},{12,8},{1,5},{5,1},{9,13},{13,9},{2,6},{6,2},{1... | collective-permute-start | bytes 2359304 | tf_op jit(solution)/shard_map/ppermute | solution.py:131
  30.2 10.9 %collective-permute-start.6 = (bf16[2,256,256]{2,1,0:T(8,128)(2,1)S(1)}, bf16[2,256,256]{2,1,0:T(8,128)(2,1)S(1)}, u32[]{:S(2)}, u32[]{:S(2)}) collective-permute-start(bf16[2,256,256]{2,1,0:T(8,128)(2,1)S(1)} %get-tuple-element.41), channel_id=1, source_target_pairs={{0,1},{1,2},{2,3},{3,0},{4,5},{5,6},{6,7},{7,4},{8,9},{9,10},{10,1... | collective-permute-start | bytes 786440 | tf_op jit(solution)/shard_map/ppermute | solution.py:128
  34.8 7.9 %collective-permute-start.4 = (bf16[2,256,256]{2,1,0:T(8,128)(2,1)S(1)}, bf16[2,256,256]{2,1,0:T(8,128)(2,1)S(1)}, u32[]{:S(2)}, u32[]{:S(2)}) collective-permute-start(bf16[2,256,256]{2,1,0:T(8,128)(2,1)S(1)} %collective-permute-done.2.rest_0_), channel_id=1, source_target_pairs={{4,8},{8,4},{12,0},{0,12},{5,9},{9,5},{13,1},{1,13},{6,10},{10,6},... | collective-permute-start | bytes 786440 | tf_op jit(solution)/shard_map/ppermute | solution.py:131
  37.4 9.2 %collective-permute-start.5 = (bf16[2,256,256]{2,1,0:T(8,128)(2,1)S(1)}, bf16[2,256,256]{2,1,0:T(8,128)(2,1)S(1)}, u32[]{:S(2)}, u32[]{:S(2)}) collective-permute-start(bf16[2,256,256]{2,1,0:T(8,128)(2,1)S(1)} %get-tuple-element.40), channel_id=1, source_target_pairs={{0,3},{1,0},{2,1},{3,2},{4,7},{5,4},{6,5},{7,6},{8,11},{9,8},{10,9... | collective-permute-start | bytes 786440 | tf_op jit(solution)/shard_map/ppermute | solution.py:128
  41.0 8.5 %collective-permute-start.11 = (bf16[2,256,256]{2,1,0:T(8,128)(2,1)S(1)}, bf16[2,256,256]{2,1,0:T(8,128)(2,1)S(1)}, u32[]{:S(2)}, u32[]{:S(2)}) collective-permute-start(bf16[2,256,256]{2,1,0:T(8,128)(2,1)S(1)} %collective-permute-done.8.rest_1_), channel_id=1, source_target_pairs={{4,8},{8,4},{12,0},{0,12},{5,9},{9,5},{13,1},{1,13},{6,10},{10,6},... | collective-permute-start | bytes 786440 | tf_op jit(solution)/shard_map/ppermute | solution.py:131
  42.7 4.4 %collective-permute-start.12 = (bf16[2,256,256]{2,1,0:T(8,128)(2,1)S(1)}, bf16[2,256,256]{2,1,0:T(8,128)(2,1)S(1)}, u32[]{:S(2)}, u32[]{:S(2)}) collective-permute-start(bf16[2,256,256]{2,1,0:T(8,128)(2,1)S(1)} %collective-permute-done.2.rest_0_), channel_id=1, source_target_pairs={{0,4},{4,0},{8,12},{12,8},{1,5},{5,1},{9,13},{13,9},{2,6},{6,2},{1... | collective-permute-start | bytes 786440 | tf_op jit(solution)/shard_map/ppermute | solution.py:131
  46.6 3.0 %collective-permute-start.10 = (bf16[2,256,256]{2,1,0:T(8,128)(2,1)S(1)}, bf16[2,256,256]{2,1,0:T(8,128)(2,1)S(1)}, u32[]{:S(2)}, u32[]{:S(2)}) collective-permute-start(bf16[2,256,256]{2,1,0:T(8,128)(2,1)S(1)} %collective-permute-done.6.up_rest), channel_id=1, source_target_pairs={{0,4},{4,0},{8,12},{12,8},{1,5},{5,1},{9,13},{13,9},{2,6},{6,2},{1... | collective-permute-start | bytes 786440 | tf_op jit(solution)/shard_map/ppermute | solution.py:131
  46.6 3.0 %collective-permute-start.13 = (bf16[2,256,256]{2,1,0:T(8,128)(2,1)S(1)}, bf16[2,256,256]{2,1,0:T(8,128)(2,1)S(1)}, u32[]{:S(2)}, u32[]{:S(2)}) collective-permute-start(bf16[2,256,256]{2,1,0:T(8,128)(2,1)S(1)} %collective-permute-done.5.rest_2_), channel_id=1, source_target_pairs={{0,4},{4,0},{8,12},{12,8},{1,5},{5,1},{9,13},{13,9},{2,6},{6,2},{1... | collective-permute-start | bytes 786440 | tf_op jit(solution)/shard_map/ppermute | solution.py:131

commit v3 on v0

v3 whole, which is shorter than its diff:
```python
import jax
import jax.numpy as jnp
from jax import lax
from jax.experimental import pallas as pl
from jax.experimental.pallas import tpu as pltpu
from jax.sharding import PartitionSpec as P

STEPS = (-1, 0, 1)
CELLS = [(along_u, along_y) for along_u in STEPS for along_y in STEPS]
EDGES = {
    1: {"in": [(u, y) for u in (0, 1) for y in STEPS]},
    -1: {"in": [(u, y) for u in (0, -1) for y in STEPS]},
}
PIECES = {
    1: {"up": [(0, 0), (0, 1), (1, 0), (1, 1)], "up_rest": [(-1, 0), (-1, 1)]},
    -1: {"down0": [(0, -1), (0, 0)], "down1": [(1, -1), (1, 0)], "down2": [(-1, -1), (-1, 0)]},
}
STAGES = [['mat', 'x_in', 'up', 'x_up', 'down1'],
 ['up_rest', 'down2', 'x_down0', 'x_down1', 'n_in', 'n_up', 'n_down0', 'n_down2', 'n_up_rest', 'down0']]
SCHEDULE = [('x_in', []), ('up', []), ('x_up', []), ('down0', ['up']), ('down1', ['up']), (0, []), ('up_rest', ['x_in']),
 ('down2', ['x_in']), ('x_down0', []), ('x_down1', ['x_up']), ('n_in', ['down0']), ('n_up', ['down0']),
 ('n_down0', ['sum_0']), ('n_down2', ['sum_0']), ('n_up_rest', ['down1', 'n_up', 'sum_0', 'x_down0']),
 (1, [])]
FLOPS = [1, 1]


def holder(a, c):
    (au, ay), (cu, cy) = a, c
    if au == 0 and ay == 0:
        return "mat", CELLS.index(c)
    prefix = {0: "", 1: "x_", -1: "n_"}[au]
    wanted = (cu if au == 0 else -cu, cy)
    for name, tiles in (EDGES[au] if ay == 0 else PIECES[-ay]).items():
        if wanted in tiles:
            return prefix + name, tiles.index(wanted)


def pairs(b):
    for a in CELLS:
        c = (b[0] - a[0], b[1] - a[1])
        if abs(c[0]) <= 1 and abs(c[1]) <= 1:
            yield a, holder(a, c)


def stage_plan():
    stage_of = {name: k for k, names in enumerate(STAGES) for name in names}
    whole = {b: max(stage_of[name] for _, (name, _) in pairs(b)) for b in CELLS}
    plan = []
    for k in range(len(STAGES)):
        squares = {b: [p for p in pairs(b) if stage_of[p[1][0]] == k] for b in CELLS}
        cubics = {b: [p for p in pairs(b) if max(stage_of[p[1][0]], whole[p[0]]) == k] for b in CELLS}
        plan.append(
            (
                {b: chosen for b, chosen in squares.items() if chosen},
                [b for b in CELLS if whole[b] == k],
                {b: chosen for b, chosen in cubics.items() if chosen},
            )
        )
    return plan


def total(lefts, rights, base):
    summed = jnp.dot(
        jnp.concatenate(lefts, axis=1), jnp.concatenate(rights, axis=0), preferred_element_type=jnp.float32
    )
    return summed if base is None else base + summed


def first_slot(b, sign):
    return 3 * ((sign * b[0] + 1) * 3 + b[1] + 1)


def quarters(b, sign, keep, width):
    for low in range(2):
        for high in range(2):
            rows, columns = slice(low * width, (low + 1) * width), slice(high * width, (high + 1) * width)
            yield low, high, rows, columns, keep[low, first_slot(b, sign) + 1 + high - low].astype(jnp.float32)


def pack_kernel(layout, flip, keep, values, *outs):
    width = values.shape[-1]
    sign = flip[0]
    for b in CELLS:
        targets = [out.at[tiles.index(b)] for out, tiles in zip(outs, layout) if b in tiles]
        for low, high, rows, columns, kept in quarters(b, sign, keep, width):
            block = values[low, first_slot(b, sign) + 1 + high - low] * kept.astype(values.dtype)
            for target in targets:
                target[rows, columns] = block


def product_kernel(work, names, found, made, flip, keep, *refs):
    squares, finished, cubics, final = work
    inputs, refs = dict(zip(names, refs)), refs[len(names) :]
    outputs = dict(zip(made["arrays"], refs))
    sign = flip[0]

    def put(kind, b, value):
        name, place = made[kind, b]
        outputs[name][place] = value.astype(outputs[name].dtype)

    def get(kind, b):
        name, place = made[kind, b] if kind == "square" and ("square", b) in made else found[kind, b]
        return (outputs if name in outputs else inputs)[name][place]

    for b in CELLS:
        if b in squares or b in finished:
            base = get("sum", b) if ("sum", b) in found else None
            chosen = squares.get(b, [])
            value = base
            if chosen:
                lefts = [inputs["mat"][CELLS.index(a)] for a, _ in chosen]
                value = total(lefts, [inputs[name][place] for _, (name, place) in chosen], base)
            if b not in finished:
                put("sum", b, value)
                continue
            name, place = made["square", b]
            width = value.shape[-1] // 2
            for _, _, rows, columns, kept in quarters(b, sign, keep, width):
                outputs[name][place, rows, columns] = (value[rows, columns] * kept).astype(outputs[name].dtype)
    if final:
        out, stage, copied = refs[len(outputs) :]
        width = out.shape[-1]
        empty = jnp.zeros((width, width), out.dtype)
        copies = []
    for b in CELLS:
        chosen = cubics.get(b, [])
        if not chosen and not final:
            continue
        value = get("cubic", b) if ("cubic", b) in found else None
        if chosen:
            lefts = [get("square", a) for a, _ in chosen]
            value = total(lefts, [inputs[name][place] for _, (name, place) in chosen], value)
        if not final:
            put("cubic", b, value)
            continue
        own = get("square", b).astype(jnp.float32)
        cell = CELLS.index(b)
        for low, high, rows, columns, kept in quarters(b, sign, keep, width):
            mixed = (3.0 * own[rows, columns] - 2.0 * value[rows, columns]) * kept
            stage[cell, low, 1 + high - low] = mixed.astype(out.dtype)
        for low in range(2):
            stage[cell, low, 2 * low] = empty
            copies.append(
                pltpu.make_async_copy(
                    stage.at[cell, low], out.at[low, pl.ds(first_slot(b, sign), 3)], copied.at[cell, low]
                )
            )
            copies[-1].start()
    if final:
        for copy in copies:
            copy.wait()


def local(values, pattern):
    blocks, keep = values[0, 0], pattern[0, 0]
    dtype, width = blocks.dtype, blocks.shape[-1]
    side = 2 * width
    rows, cols = lax.axis_size("row"), lax.axis_size("col")
    flip = (2 * lax.rem(lax.axis_index("row"), 2) - 1).reshape(1)

    near, far = [], []
    for i in range(0, rows, 2):
        near += [(i, i + 1), (i + 1, i)]
        far += [(i + 1, (i + 2) % rows), ((i + 2) % rows, i + 1)]
    up = [(i, (i + 1) % cols) for i in range(cols)]
    down = [(i, (i - 1) % cols) for i in range(cols)]

    def tiles(count, kind=dtype):
        return jax.ShapeDtypeStruct((count, side, side), kind)

    smem = pl.BlockSpec(memory_space=pltpu.SMEM)
    vmem = pl.BlockSpec(memory_space=pltpu.VMEM)
    hbm = pl.BlockSpec(memory_space=pltpu.HBM)

    sent = {name: (held, "col", up) for name, held in PIECES[1].items()}
    sent |= {name: (held, "col", down) for name, held in PIECES[-1].items()}
    sent |= {"x_" + name: (held, "row", far) for name, held in EDGES[1].items()}
    sent |= {"n_" + name: (held, "row", near) for name, held in EDGES[-1].items()}
    layout = [CELLS] + [held for held, _, _ in sent.values()]
    packed = pl.pallas_call(
        lambda *refs: pack_kernel(layout, *refs),
        out_shape=[tiles(len(held)) for held in layout],
        in_specs=[smem, smem, vmem],
        out_specs=[vmem] * len(layout),
        compiler_params=pltpu.CompilerParams(vmem_limit_bytes=16 << 20),
        name="pack",
    )(flip, keep, blocks)
    ready = dict(zip(sent, packed[1:]))
    arrays = {"mat": packed[0]}
    plan, found = stage_plan(), {}

    def move(name, gates):
        if name in sent:
            operand, (_, axis, towards) = ready[name], sent[name]
        else:
            operand, axis, towards = arrays[name[2:]], "row", far if name[0] == "x" else near
        gates = [gate for gate in gates if name in sent or gate != name[2:]]
        if gates:
            operand, *held = lax.optimization_barrier((operand, *(arrays[gate] for gate in gates)))
            arrays.update(zip(gates, held))
            if name not in sent:
                arrays[name[2:]] = operand
        arrays[name] = lax.ppermute(operand, axis, towards)

    def multiply(k):
        squares, finished, cubics = plan[k]
        final = k == len(plan) - 1
        names = {"mat"} | {name for chosen in (*squares.values(), *cubics.values()) for _, (name, _) in chosen}
        used = [("sum", b) for b in CELLS if b in squares or b in finished]
        used += [("square", a) for chosen in cubics.values() for a, _ in chosen]
        used += [("square", b) for b in CELLS if final] + [("cubic", b) for b in CELLS if b in cubics or final]
        names |= {found[key][0] for key in used if key in found}
        names = sorted(names)
        made, shapes = {"arrays": []}, []
        for kind, members, number in (
            ("sum", [b for b in CELLS if b in squares and b not in finished], jnp.float32),
            ("square", finished, dtype),
            ("cubic", [b for b in CELLS if b in cubics and not final], jnp.float32),
        ):
            if members:
                made["arrays"].append(f"{kind}_{k}")
                shapes.append(tiles(len(members), number))
                made.update({(kind, b): (f"{kind}_{k}", place) for place, b in enumerate(members)})
        work, before = (squares, finished, cubics, final), dict(found)
        scratch = []
        if final:
            scratch = [pltpu.VMEM(shape.shape, shape.dtype) for shape in shapes]
            scratch += [pltpu.VMEM((9, 2, 3, width, width), dtype), pltpu.SemaphoreType.DMA((9, 2))]
        count = len(shapes)

        def body(*refs):
            if final:
                ins, out, rest = refs[: 2 + len(names)], refs[2 + len(names)], refs[3 + len(names) :]
                refs = (*ins, *rest[:count], out, *rest[count:])
            product_kernel(work, names, before, made, *refs)

        results = pl.pallas_call(
            body,
            out_shape=jax.ShapeDtypeStruct(blocks.shape, dtype) if final else shapes,
            in_specs=[smem, smem] + [vmem] * len(names),
            out_specs=hbm if final else [vmem] * count,
            scratch_shapes=scratch,
            compiler_params=pltpu.CompilerParams(vmem_limit_bytes=24 << 20),
            cost_estimate=pl.CostEstimate(flops=FLOPS[k], bytes_accessed=1, transcendentals=0),
            name=f"product{k}",
        )(flip, keep, *(arrays[name] for name in names))
        if final:
            return results
        arrays.update(zip(made["arrays"], results))
        found.update({key: place for key, place in made.items() if key != "arrays"})

    for event, gates in SCHEDULE:
        if isinstance(event, int):
            purified = multiply(event)
        else:
            move(event, gates)
    return purified[None, None]


def solution(mesh):
    return jax.shard_map(
        local,
        mesh=mesh,
        in_specs=(
            P(("grp", "row"), "col", None, None, None, None),
            P(("grp", "row"), "col", None, None),
        ),
        out_specs=P(("grp", "row"), "col", None, None, None, None),
        check_vma=False,
    )
```

time: 315 us -> 53.8 us (0.17)
  waiting for transfers between devices: 258 us -> 31.5 us
  matrix products: 22.3 us -> 0 us
  local copies, waits for them, and re-layouts: 19.2 us -> 2.17 us
  Pallas kernels: 0 us -> 6.91 us
  starting transfers between devices: 6.37 us -> 13 us
  other arithmetic: 4.56 us -> 0 us
    ppermute x4 -> x14, waiting for transfers between devices: 258 us -> 31.5 us  [move(): arrays[name] = lax.ppermute(operand, axis, towards)]
    dot_general x72 -> x0, matrix products: 22.3 us -> none  [restricted(): jnp.dot(left_joined, right_joined, preferred_element_type=jnp.float32)]
    unnamed x168 -> x6, local copies, waits for them, and re-layouts: 11.3 us -> 2.17 us
    pallas_call x0 -> x3, Pallas kernels: none -> 6.91 us  [the longest x2 5.79 us: multiply(): pl.pallas_call(body, out_shape=jax.ShapeDtypeStruct(blocks.shape, dtype)...]
    ppermute x4 -> x14, starting transfers between devices: 6.37 us -> 13 us  [move(): arrays[name] = lax.ppermute(operand, axis, towards)]
    squeeze x2 -> x0, local copies, waits for them, and re-layouts: 5.11 us -> none  [local(): neighbours[step_x, step_y] = extended[step_x + 1, step_y + 1]]
  transfers between devices with their start and end apart: 4 -> 14, of which waited for: 4 -> 8; matrix products, arithmetic and copies ran while one was open for 3% -> 0% of each run, Pallas kernels for 0% -> 3%
where the time goes in v3:
time: 53.8 us; the launch traced here: 53.6 us
  waiting for transfers between devices  31.5 us (59%)
  starting transfers between devices  13 us (24%)
  Pallas kernels  6.91 us (13%)
  local copies, waits for them, and re-layouts  2.17 us (4%)
    ppermute x14, waiting for transfers between devices, move(): arrays[name] = lax.ppermute(operand, axis, towards)  31.5 us
    ppermute x14, starting transfers between devices, move(): arrays[name] = lax.ppermute(operand, axis, towards)  13 us
    pallas_call x2, Pallas kernels, multiply(): pl.pallas_call(body, out_shape=jax.ShapeDtypeStruct(blocks.shape, dtype)...  5.79 us
    unnamed x6, local copies, waits for them, and re-layouts  2.17 us
    pallas_call x1, Pallas kernels, local(): pl.pallas_call(lambda *refs: pack_kernel(layout, *refs), out_shape=[tiles...  1.12 us
  transfers between devices with their start and end apart: 14, of which 8 were waited for; matrix products, arithmetic and copies ran while one was open for 0% of the time, Pallas kernels for 3%

profile of v3, /device:TPU:0, one launch (start us, length us, event | category | flops | bytes accessed | tf_op | source)
XLA Modules:
  0.0 53.6 jit_solution(3265822711620772248)
XLA Ops:
  0.0 0.0 copy-start.2
  0.0 0.0 copy-start
  0.0 1.5 %copy-done = bf16[1,1,2,27,128,128]{5,4,3,2,1,0:T(8,128)(2,1)S(1)} copy-done((bf16[1,1,2,27,128,128]{5,4,3,2,1,0:T(8,128)(2,1)S(1)}, bf16[1,1,2,27,128,128]{5,4,3,2,1,0:T(8,128)(2,1)}, u32[]{:S(2)}) %copy-start) | copy-done | bytes 1769496
  1.5 0.0 copy-start.1
  1.5 0.7 %copy-done.1 = s32[1,1,2,27]{3,2,1,0:T(2,128)S(1)} copy-done((s32[1,1,2,27]{3,2,1,0:T(2,128)S(1)}, s32[1,1,2,27]{3,2,1,0:T(2,128)}, u32[]{:S(2)}) %copy-start.1) | copy-done | bytes 240
  2.2 1.1 %pack.1 = (bf16[9,256,256]{2,1,0:T(8,128)(2,1)S(1)}, bf16[4,256,256]{2,1,0:T(8,128)(2,1)S(1)}, bf16[2,256,256]{2,1,0:T(8,128)(2,1)S(1)}, bf16[2,256,256]{2,1,0:T...) custom-call(s32[1]{0:T(128)} %bitcast.refs_0_, ...), custom_call_target="tpu_custom_call" | custom-call | tf_op jit(solution)/shard_map/pack/pallas_call | solution.py:180
  3.3 3.1 %collective-permute-start = (bf16[4,256,256]{2,1,0:T(8,128)(2,1)S(1)}, bf16[4,256,256]{2,1,0:T(8,128)(2,1)S(1)}, u32[]{:S(2)}, u32[]{:S(2)}) collective-permute-start(bf16[4,256,256]{2,1,0:T(8,128)(2,1)S(1)} %get-tuple-element.40), channel_id=1, source_target_pairs={{0,1},{1,2},{2,3},{3,0},{4,5},{5,6},{6,7},{7,4},{8,9},{9,10},{10,1... | collective-permute-start | bytes 1572872 | tf_op jit(solution)/shard_map/ppermute | solution.py:203
  6.4 0.7 %collective-permute-start.2 = (bf16[6,256,256]{2,1,0:T(8,128)(2,1)S(1)}, bf16[6,256,256]{2,1,0:T(8,128)(2,1)S(1)}, u32[]{:S(2)}, u32[]{:S(2)}) collective-permute-start(bf16[6,256,256]{2,1,0:T(8,128)(2,1)S(1)} %get-tuple-element.45), channel_id=1, source_target_pairs={{4,8},{8,4},{12,0},{0,12},{5,9},{9,5},{13,1},{1,13},{6,10},{10,6},... | collective-permute-start | bytes 2359304 | tf_op jit(solution)/shard_map/ppermute | solution.py:203
  7.0 13.3 %collective-permute-done.refs_4_.refs_14_ = bf16[4,256,256]{2,1,0:T(8,128)(2,1)S(1)} collective-permute-done((bf16[4,256,256]{2,1,0:T(8,128)(2,1)S(1)}, bf16[4,256,256]{2,1,0:T(8,128)(2,1)S(1)}, u32[]{:S(2)}, u32[]{:S(2)}) %collective-permute-start) | collective-permute-done | bytes 524320 | tf_op jit(solution)/shard_map/ppermute | solution.py:203
  20.3 1.7 %collective-permute-start.4 = (bf16[2,256,256]{2,1,0:T(8,128)(2,1)S(1)}, bf16[2,256,256]{2,1,0:T(8,128)(2,1)S(1)}, u32[]{:S(2)}, u32[]{:S(2)}) collective-permute-start(bf16[2,256,256]{2,1,0:T(8,128)(2,1)S(1)} %get-tuple-element.48), channel_id=1, source_target_pairs={{0,3},{1,0},{2,1},{3,2},{4,7},{5,4},{6,5},{7,6},{8,11},{9,8},{10,9... | collective-permute-start | bytes 786440 | tf_op jit(solution)/shard_map/ppermute | solution.py:203
  22.1 0.0 collective-permute-start.3
  22.1 0.4 collective-permute-start.1
  22.5 6.8 %collective-permute-done.4.refs_3_ = bf16[2,256,256]{2,1,0:T(8,128)(2,1)S(1)} collective-permute-done((bf16[2,256,256]{2,1,0:T(8,128)(2,1)S(1)}, bf16[2,256,256]{2,1,0:T(8,128)(2,1)S(1)}, u32[]{:S(2)}, u32[]{:S(2)}) %collective-permute-start.4) | collective-permute-done | bytes 262176 | tf_op jit(solution)/shard_map/ppermute | solution.py:203
  29.3 0.0 collective-permute-start.6
  29.3 0.5 collective-permute-start.11
  29.8 0.0 collective-permute-done.2.refs_5_.refs_18_
  29.8 3.8 %collective-permute-start.7 = (bf16[2,256,256]{2,1,0:T(8,128)(2,1)S(1)}, bf16[2,256,256]{2,1,0:T(8,128)(2,1)S(1)}, u32[]{:S(2)}, u32[]{:S(2)}) collective-permute-start(bf16[2,256,256]{2,1,0:T(8,128)(2,1)S(1)} %get-tuple-element.59), channel_id=1, source_target_pairs={{0,3},{1,0},{2,1},{3,2},{4,7},{5,4},{6,5},{7,6},{8,11},{9,8},{10,9... | collective-permute-start | bytes 786440 | tf_op jit(solution)/shard_map/ppermute | solution.py:203
  33.6 0.8 %collective-permute-done.1.refs_2_.refs_4_ = bf16[2,256,256]{2,1,0:T(8,128)(2,1)S(1)} collective-permute-done((bf16[2,256,256]{2,1,0:T(8,128)(2,1)S(1)}, bf16[2,256,256]{2,1,0:T(8,128)(2,1)S(1)}, u32[]{:S(2)}, u32[]{:S(2)}) %collective-permute-start.1) | collective-permute-done | bytes 262176 | tf_op jit(solution)/shard_map/ppermute | solution.py:203
  34.4 0.1 collective-permute-start.8
  34.4 3.0 %collective-permute-done.3.refs_6_ = bf16[4,256,256]{2,1,0:T(8,128)(2,1)S(1)} collective-permute-done((bf16[4,256,256]{2,1,0:T(8,128)(2,1)S(1)}, bf16[4,256,256]{2,1,0:T(8,128)(2,1)S(1)}, u32[]{:S(2)}, u32[]{:S(2)}) %collective-permute-start.3) | collective-permute-done | bytes 524320 | tf_op jit(solution)/shard_map/ppermute | solution.py:203
  37.4 1.6 %collective-permute-start.5 = (bf16[2,256,256]{2,1,0:T(8,128)(2,1)S(1)}, bf16[2,256,256]{2,1,0:T(8,128)(2,1)S(1)}, u32[]{:S(2)}, u32[]{:S(2)}) collective-permute-start(bf16[2,256,256]{2,1,0:T(8,128)(2,1)S(1)} %get-tuple-element.54), channel_id=1, source_target_pairs={{0,1},{1,2},{2,3},{3,0},{4,5},{5,6},{6,7},{7,4},{8,9},{9,10},{10,1... | collective-permute-start | bytes 786440 | tf_op jit(solution)/shard_map/ppermute | solution.py:203
  39.0 0.0 copy-done.2
  39.0 1.7 %product0.1 = (f32[8,256,256]{2,1,0:T(8,128)S(1)}, bf16[1,256,256]{2,1,0:T(8,128)(2,1)S(1)}, f32[4,256,256]{2,1,0:T(8,128)S(1)}) custom-call(s32[1]{0:T(128)} %bitcast.refs_0_, s32[2,27]{1,0:T(2,128)S(1)} %bitcast.6, bf16[2,256,256]{2,1,0:T(8,128)(2,1)S(1)} %collective-permute-done.1.refs_2_.refs_4_, ...), custom_call_target="tpu_custom_call" | custom-call | flops 1 | bytes 1 | tf_op jit(solution)/shard_map/product0/pallas_call | solution.py:237
  40.7 0.0 collective-permute-done.7.refs_5_
  40.7 0.5 collective-permute-start.13
  41.2 1.8 %collective-permute-done.8.refs_16_ = bf16[2,256,256]{2,1,0:T(8,128)(2,1)S(1)} collective-permute-done((bf16[2,256,256]{2,1,0:T(8,128)(2,1)S(1)}, bf16[2,256,256]{2,1,0:T(8,128)(2,1)S(1)}, u32[]{:S(2)}, u32[]{:S(2)}) %collective-permute-start.8) | collective-permute-done | bytes 262176 | tf_op jit(solution)/shard_map/ppermute | solution.py:203
  43.0 0.2 collective-permute-start.10
  43.2 4.4 %collective-permute-done.5.refs_15_ = bf16[2,256,256]{2,1,0:T(8,128)(2,1)S(1)} collective-permute-done((bf16[2,256,256]{2,1,0:T(8,128)(2,1)S(1)}, bf16[2,256,256]{2,1,0:T(8,128)(2,1)S(1)}, u32[]{:S(2)}, u32[]{:S(2)}) %collective-permute-start.5) | collective-permute-done | bytes 262176 | tf_op jit(solution)/shard_map/ppermute | solution.py:203
  47.6 0.0 collective-permute-start.9
  47.6 0.0 collective-permute-done.6.refs_10_
  47.6 0.5 collective-permute-start.12
  48.1 1.1 %collective-permute-done.13.refs_17_ = bf16[2,256,256]{2,1,0:T(8,128)(2,1)S(1)} collective-permute-done((bf16[2,256,256]{2,1,0:T(8,128)(2,1)S(1)}, bf16[2,256,256]{2,1,0:T(8,128)(2,1)S(1)}, u32[]{:S(2)}, u32[]{:S(2)}) %collective-permute-start.13) | collective-permute-done | bytes 262176 | tf_op jit(solution)/shard_map/ppermute | solution.py:203
  49.3 0.0 collective-permute-done.10.refs_8_
  49.3 0.0 collective-permute-done.9.refs_7_
  49.3 0.0 collective-permute-done.11.refs_9_
  49.3 0.2 collective-permute-done.12.refs_11_
  49.5 4.1 %product1.1 = bf16[2,27,128,128]{3,2,1,0:T(8,128)(2,1)} custom-call(s32[1]{0:T(128)} %bitcast.refs_0_, s32[2,27]{1,0:T(2,128)S(1)} %bitcast.7, f32[4,256,256]{2,1,0:T(8,128)S(1)} %get-tuple-element.46.refs_2_, bf16[2,256,256]{2,1,0:T(8,128)(2,1)S(1)} %collective-permute-done.4.refs_3_, bf16[2,256,256]{2,1,0:T(8,128)(2,1)S(1)} %collective-permute-done.1.refs_2_.refs_4_, ...), custom_call_target="tpu_custom_call" | custom-call | flops 1 | bytes 1 | tf_op jit(solution)/shard_map/product1/pallas_call | solution.py:237
Async XLA Ops:
  0.0 39.0 %copy-start.2 = (s32[1,1,2,27]{3,2,1,0:T(2,128)S(1)}, s32[1,1,2,27]{3,2,1,0:T(2,128)}, u32[]{:S(2)}) copy-start(s32[1,1,2,27]{3,2,1,0:T(2,128)} %param.3) | copy-start | bytes 652
  0.0 1.5 %copy-start = (bf16[1,1,2,27,128,128]{5,4,3,2,1,0:T(8,128)(2,1)S(1)}, bf16[1,1,2,27,128,128]{5,4,3,2,1,0:T(8,128)(2,1)}, u32[]{:S(2)}) copy-start(bf16[1,1,2,27,128,128]{5,4,3,2,1,0:T(8,128)(2,1)} %param.2) | copy-start | bytes 5308420
  1.5 0.7 %copy-start.1 = (s32[1,1,2,27]{3,2,1,0:T(2,128)S(1)}, s32[1,1,2,27]{3,2,1,0:T(2,128)}, u32[]{:S(2)}) copy-start(s32[1,1,2,27]{3,2,1,0:T(2,128)} %param.3) | copy-start | bytes 652
  3.3 17.0 %collective-permute-start = (bf16[4,256,256]{2,1,0:T(8,128)(2,1)S(1)}, bf16[4,256,256]{2,1,0:T(8,128)(2,1)S(1)}, u32[]{:S(2)}, u32[]{:S(2)}) collective-permute-start(bf16[4,256,256]{2,1,0:T(8,128)(2,1)S(1)} %get-tuple-element.40), channel_id=1, source_target_pairs={{0,1},{1,2},{2,3},{3,0},{4,5},{5,6},{6,7},{7,4},{8,9},{9,10},{10,1... | collective-permute-start | bytes 1572872 | tf_op jit(solution)/shard_map/ppermute | solution.py:203
  6.4 23.4 %collective-permute-start.2 = (bf16[6,256,256]{2,1,0:T(8,128)(2,1)S(1)}, bf16[6,256,256]{2,1,0:T(8,128)(2,1)S(1)}, u32[]{:S(2)}, u32[]{:S(2)}) collective-permute-start(bf16[6,256,256]{2,1,0:T(8,128)(2,1)S(1)} %get-tuple-element.45), channel_id=1, source_target_pairs={{4,8},{8,4},{12,0},{0,12},{5,9},{9,5},{13,1},{1,13},{6,10},{10,6},... | collective-permute-start | bytes 2359304 | tf_op jit(solution)/shard_map/ppermute | solution.py:203
  20.3 9.0 %collective-permute-start.4 = (bf16[2,256,256]{2,1,0:T(8,128)(2,1)S(1)}, bf16[2,256,256]{2,1,0:T(8,128)(2,1)S(1)}, u32[]{:S(2)}, u32[]{:S(2)}) collective-permute-start(bf16[2,256,256]{2,1,0:T(8,128)(2,1)S(1)} %get-tuple-element.48), channel_id=1, source_target_pairs={{0,3},{1,0},{2,1},{3,2},{4,7},{5,4},{6,5},{7,6},{8,11},{9,8},{10,9... | collective-permute-start | bytes 786440 | tf_op jit(solution)/shard_map/ppermute | solution.py:203
  22.1 15.3 %collective-permute-start.3 = (bf16[4,256,256]{2,1,0:T(8,128)(2,1)S(1)}, bf16[4,256,256]{2,1,0:T(8,128)(2,1)S(1)}, u32[]{:S(2)}, u32[]{:S(2)}) collective-permute-start(bf16[4,256,256]{2,1,0:T(8,128)(2,1)S(1)} %collective-permute-done.refs_4_.refs_14_), channel_id=1, source_target_pairs={{4,8},{8,4},{12,0},{0,12},{5,9},{9,5},{13,1},{1,13},{6,10},{10,6},... | collective-permute-start | bytes 1572872 | tf_op jit(solution)/shard_map/ppermute | solution.py:203
  22.1 12.3 %collective-permute-start.1 = (bf16[2,256,256]{2,1,0:T(8,128)(2,1)S(1)}, bf16[2,256,256]{2,1,0:T(8,128)(2,1)S(1)}, u32[]{:S(2)}, u32[]{:S(2)}) collective-permute-start(bf16[2,256,256]{2,1,0:T(8,128)(2,1)S(1)} %get-tuple-element.42), channel_id=1, source_target_pairs={{0,3},{1,0},{2,1},{3,2},{4,7},{5,4},{6,5},{7,6},{8,11},{9,8},{10,9... | collective-permute-start | bytes 786440 | tf_op jit(solution)/shard_map/ppermute | solution.py:203
  29.3 18.3 %collective-permute-start.6 = (bf16[4,256,256]{2,1,0:T(8,128)(2,1)S(1)}, bf16[4,256,256]{2,1,0:T(8,128)(2,1)S(1)}, u32[]{:S(2)}, u32[]{:S(2)}) collective-permute-start(bf16[4,256,256]{2,1,0:T(8,128)(2,1)S(1)} %collective-permute-done.refs_4_.refs_14_), channel_id=1, source_target_pairs={{0,4},{4,0},{8,12},{12,8},{1,5},{5,1},{9,13},{13,9},{2,6},{6,2},{1... | collective-permute-start | bytes 1572872 | tf_op jit(solution)/shard_map/ppermute | solution.py:203
  29.3 20.0 %collective-permute-start.11 = (bf16[6,256,256]{2,1,0:T(8,128)(2,1)S(1)}, bf16[6,256,256]{2,1,0:T(8,128)(2,1)S(1)}, u32[]{:S(2)}, u32[]{:S(2)}) collective-permute-start(bf16[6,256,256]{2,1,0:T(8,128)(2,1)S(1)} %get-tuple-element.64), channel_id=1, source_target_pairs={{0,4},{4,0},{8,12},{12,8},{1,5},{5,1},{9,13},{13,9},{2,6},{6,2},{1... | collective-permute-start | bytes 2359304 | tf_op jit(solution)/shard_map/ppermute | solution.py:203
  29.8 10.9 %collective-permute-start.7 = (bf16[2,256,256]{2,1,0:T(8,128)(2,1)S(1)}, bf16[2,256,256]{2,1,0:T(8,128)(2,1)S(1)}, u32[]{:S(2)}, u32[]{:S(2)}) collective-permute-start(bf16[2,256,256]{2,1,0:T(8,128)(2,1)S(1)} %get-tuple-element.59), channel_id=1, source_target_pairs={{0,3},{1,0},{2,1},{3,2},{4,7},{5,4},{6,5},{7,6},{8,11},{9,8},{10,9... | collective-permute-start | bytes 786440 | tf_op jit(solution)/shard_map/ppermute | solution.py:203
  34.4 8.6 %collective-permute-start.8 = (bf16[2,256,256]{2,1,0:T(8,128)(2,1)S(1)}, bf16[2,256,256]{2,1,0:T(8,128)(2,1)S(1)}, u32[]{:S(2)}, u32[]{:S(2)}) collective-permute-start(bf16[2,256,256]{2,1,0:T(8,128)(2,1)S(1)} %collective-permute-done.4.refs_3_), channel_id=1, source_target_pairs={{4,8},{8,4},{12,0},{0,12},{5,9},{9,5},{13,1},{1,13},{6,10},{10,6},... | collective-permute-start | bytes 786440 | tf_op jit(solution)/shard_map/ppermute | solution.py:203
  37.4 10.2 %collective-permute-start.5 = (bf16[2,256,256]{2,1,0:T(8,128)(2,1)S(1)}, bf16[2,256,256]{2,1,0:T(8,128)(2,1)S(1)}, u32[]{:S(2)}, u32[]{:S(2)}) collective-permute-start(bf16[2,256,256]{2,1,0:T(8,128)(2,1)S(1)} %get-tuple-element.54), channel_id=1, source_target_pairs={{0,1},{1,2},{2,3},{3,0},{4,5},{5,6},{6,7},{7,4},{8,9},{9,10},{10,1... | collective-permute-start | bytes 786440 | tf_op jit(solution)/shard_map/ppermute | solution.py:203
  40.7 8.6 %collective-permute-start.13 = (bf16[2,256,256]{2,1,0:T(8,128)(2,1)S(1)}, bf16[2,256,256]{2,1,0:T(8,128)(2,1)S(1)}, u32[]{:S(2)}, u32[]{:S(2)}) collective-permute-start(bf16[2,256,256]{2,1,0:T(8,128)(2,1)S(1)} %collective-permute-done.1.refs_2_.refs_4_), channel_id=1, source_target_pairs={{4,8},{8,4},{12,0},{0,12},{5,9},{9,5},{13,1},{1,13},{6,10},{10,6},... | collective-permute-start | bytes 786440 | tf_op jit(solution)/shard_map/ppermute | solution.py:203
  43.0 6.3 %collective-permute-start.10 = (bf16[2,256,256]{2,1,0:T(8,128)(2,1)S(1)}, bf16[2,256,256]{2,1,0:T(8,128)(2,1)S(1)}, u32[]{:S(2)}, u32[]{:S(2)}) collective-permute-start(bf16[2,256,256]{2,1,0:T(8,128)(2,1)S(1)} %collective-permute-done.7.refs_5_), channel_id=1, source_target_pairs={{0,4},{4,0},{8,12},{12,8},{1,5},{5,1},{9,13},{13,9},{2,6},{6,2},{1... | collective-permute-start | bytes 786440 | tf_op jit(solution)/shard_map/ppermute | solution.py:203
  47.6 1.7 %collective-permute-start.9 = (bf16[2,256,256]{2,1,0:T(8,128)(2,1)S(1)}, bf16[2,256,256]{2,1,0:T(8,128)(2,1)S(1)}, u32[]{:S(2)}, u32[]{:S(2)}) collective-permute-start(bf16[2,256,256]{2,1,0:T(8,128)(2,1)S(1)} %collective-permute-done.4.refs_3_), channel_id=1, source_target_pairs={{0,4},{4,0},{8,12},{12,8},{1,5},{5,1},{9,13},{13,9},{2,6},{6,2},{1... | collective-permute-start | bytes 786440 | tf_op jit(solution)/shard_map/ppermute | solution.py:203
  47.6 1.9 %collective-permute-start.12 = (bf16[2,256,256]{2,1,0:T(8,128)(2,1)S(1)}, bf16[2,256,256]{2,1,0:T(8,128)(2,1)S(1)}, u32[]{:S(2)}, u32[]{:S(2)}) collective-permute-start(bf16[2,256,256]{2,1,0:T(8,128)(2,1)S(1)} %collective-permute-done.5.refs_15_), channel_id=1, source_target_pairs={{0,4},{4,0},{8,12},{12,8},{1,5},{5,1},{9,13},{13,9},{2,6},{6,2},{1... | collective-permute-start | bytes 786440 | tf_op jit(solution)/shard_map/ppermute | solution.py:203

commit v4 on v3

--- a/solution.py
+++ b/solution.py
@@ -15,13 +15,12 @@
     1: {"up": [(0, 0), (0, 1), (1, 0), (1, 1)], "up_rest": [(-1, 0), (-1, 1)]},
     -1: {"down0": [(0, -1), (0, 0)], "down1": [(1, -1), (1, 0)], "down2": [(-1, -1), (-1, 0)]},
 }
-STAGES = [['mat', 'x_in', 'up', 'x_up', 'down1'],
- ['up_rest', 'down2', 'x_down0', 'x_down1', 'n_in', 'n_up', 'n_down0', 'n_down2', 'n_up_rest', 'down0']]
-SCHEDULE = [('x_in', []), ('up', []), ('x_up', []), ('down0', ['up']), ('down1', ['up']), (0, []), ('up_rest', ['x_in']),
- ('down2', ['x_in']), ('x_down0', []), ('x_down1', ['x_up']), ('n_in', ['down0']), ('n_up', ['down0']),
+STAGES = [['mat', 'x_in', 'up', 'x_up', 'down1', 'down0'],
+ ['up_rest', 'down2', 'x_down0', 'x_down1', 'n_in', 'n_up', 'n_down0', 'n_down2', 'n_up_rest']]
+SCHEDULE = [('x_in', []), ('up', []), ('x_up', []), ('down0', ['up']), ('up_rest', ['x_in']), ('down1', ['up']), (0, []),
+ ('down2', ['x_in']), ('x_down0', []), ('x_down1', ['down1']), ('n_in', ['down0']), ('n_up', ['down0']),
  ('n_down0', ['sum_0']), ('n_down2', ['sum_0']), ('n_up_rest', ['down1', 'n_up', 'sum_0', 'x_down0']),
  (1, [])]
-FLOPS = [1, 1]
 
 
 def holder(a, c):
@@ -66,33 +65,44 @@
     return summed if base is None else base + summed
 
 
+def far_side():
+    return 2 * lax.rem(lax.axis_index("row"), 2) - 1
+
+
 def first_slot(b, sign):
     return 3 * ((sign * b[0] + 1) * 3 + b[1] + 1)
 
 
-def quarters(b, sign, keep, width):
+def masked(block, kept):
+    parts = block.reshape(block.shape[0] // kept.shape[0], *kept.shape)
+    return (parts * kept.astype(block.dtype)[None]).reshape(block.shape)
+
+
+def quarters(b, sign, mask, width):
     for low in range(2):
         for high in range(2):
             rows, columns = slice(low * width, (low + 1) * width), slice(high * width, (high + 1) * width)
-            yield low, high, rows, columns, keep[low, first_slot(b, sign) + 1 + high - low].astype(jnp.float32)
-
-
-def pack_kernel(layout, flip, keep, values, *outs):
+            yield low, high, rows, columns, mask[low, first_slot(b, sign) + 1 + high - low]
+
+
+def pack_kernel(layout, mask, values, *outs):
     width = values.shape[-1]
-    sign = flip[0]
+    sign = far_side()
     for b in CELLS:
         targets = [out.at[tiles.index(b)] for out, tiles in zip(outs, layout) if b in tiles]
-        for low, high, rows, columns, kept in quarters(b, sign, keep, width):
-            block = values[low, first_slot(b, sign) + 1 + high - low] * kept.astype(values.dtype)
+        if not targets:
+            continue
+        for low, high, rows, columns, kept in quarters(b, sign, mask, width):
+            block = masked(values[low, first_slot(b, sign) + 1 + high - low], kept)
             for target in targets:
                 target[rows, columns] = block
 
 
-def product_kernel(work, names, found, made, flip, keep, *refs):
+def product_kernel(work, names, found, made, *refs):
     squares, finished, cubics, final = work
     inputs, refs = dict(zip(names, refs)), refs[len(names) :]
     outputs = dict(zip(made["arrays"], refs))
-    sign = flip[0]
+    sign, mask = far_side(), inputs.get("mask")
 
     def put(kind, b, value):
         name, place = made[kind, b]
@@ -115,8 +125,8 @@
                 continue
             name, place = made["square", b]
             width = value.shape[-1] // 2
-            for _, _, rows, columns, kept in quarters(b, sign, keep, width):
-                outputs[name][place, rows, columns] = (value[rows, columns] * kept).astype(outputs[name].dtype)
+            for _, _, rows, columns, kept in quarters(b, sign, mask, width):
+                outputs[name][place, rows, columns] = masked(value[rows, columns], kept).astype(outputs[name].dtype)
     if final:
         out, stage, copied = refs[len(outputs) :]
         width = out.shape[-1]
@@ -135,8 +145,8 @@
             continue
         own = get("square", b).astype(jnp.float32)
         cell = CELLS.index(b)
-        for low, high, rows, columns, kept in quarters(b, sign, keep, width):
-            mixed = (3.0 * own[rows, columns] - 2.0 * value[rows, columns]) * kept
+        for low, high, rows, columns, kept in quarters(b, sign, mask, width):
+            mixed = masked(3.0 * own[rows, columns] - 2.0 * value[rows, columns], kept)
             stage[cell, low, 1 + high - low] = mixed.astype(out.dtype)
         for low in range(2):
             stage[cell, low, 2 * low] = empty
@@ -156,7 +166,6 @@
     dtype, width = blocks.dtype, blocks.shape[-1]
     side = 2 * width
     rows, cols = lax.axis_size("row"), lax.axis_size("col")
-    flip = (2 * lax.rem(lax.axis_index("row"), 2) - 1).reshape(1)
 
     near, far = [], []
     for i in range(0, rows, 2):
@@ -168,7 +177,6 @@
     def tiles(count, kind=dtype):
         return jax.ShapeDtypeStruct((count, side, side), kind)
 
-    smem = pl.BlockSpec(memory_space=pltpu.SMEM)
     vmem = pl.BlockSpec(memory_space=pltpu.VMEM)
     hbm = pl.BlockSpec(memory_space=pltpu.HBM)
 
@@ -176,17 +184,18 @@
     sent |= {name: (held, "col", down) for name, held in PIECES[-1].items()}
     sent |= {"x_" + name: (held, "row", far) for name, held in EDGES[1].items()}
     sent |= {"n_" + name: (held, "row", near) for name, held in EDGES[-1].items()}
+    mask = jnp.broadcast_to(keep.astype(dtype)[:, :, None, None], (*keep.shape, 16, width))
     layout = [CELLS] + [held for held, _, _ in sent.values()]
     packed = pl.pallas_call(
         lambda *refs: pack_kernel(layout, *refs),
         out_shape=[tiles(len(held)) for held in layout],
-        in_specs=[smem, smem, vmem],
+        in_specs=[vmem, vmem],
         out_specs=[vmem] * len(layout),
         compiler_params=pltpu.CompilerParams(vmem_limit_bytes=16 << 20),
         name="pack",
-    )(flip, keep, blocks)
+    )(mask, blocks)
     ready = dict(zip(sent, packed[1:]))
-    arrays = {"mat": packed[0]}
+    arrays = {"mat": packed[0], "mask": mask}
     plan, found = stage_plan(), {}
 
     def move(name, gates):
@@ -210,6 +219,8 @@
         used += [("square", a) for chosen in cubics.values() for a, _ in chosen]
         used += [("square", b) for b in CELLS if final] + [("cubic", b) for b in CELLS if b in cubics or final]
         names |= {found[key][0] for key in used if key in found}
+        if finished or final:
+            names.add("mask")
         names = sorted(names)
         made, shapes = {"arrays": []}, []
         for kind, members, number in (
@@ -230,20 +241,20 @@
 
         def body(*refs):
             if final:
-                ins, out, rest = refs[: 2 + len(names)], refs[2 + len(names)], refs[3 + len(names) :]
+                ins, out, rest = refs[: len(names)], refs[len(names)], refs[1 + len(names) :]
                 refs = (*ins, *rest[:count], out, *rest[count:])
             product_kernel(work, names, before, made, *refs)
 
         results = pl.pallas_call(
             body,
             out_shape=jax.ShapeDtypeStruct(blocks.shape, dtype) if final else shapes,
-            in_specs=[smem, smem] + [vmem] * len(names),
+            in_specs=[vmem] * len(names),
             out_specs=hbm if final else [vmem] * count,
             scratch_shapes=scratch,
             compiler_params=pltpu.CompilerParams(vmem_limit_bytes=24 << 20),
-            cost_estimate=pl.CostEstimate(flops=FLOPS[k], bytes_accessed=1, transcendentals=0),
+            cost_estimate=pl.CostEstimate(flops=1, bytes_accessed=1, transcendentals=0),
             name=f"product{k}",
-        )(flip, keep, *(arrays[name] for name in names))
+        )(*(arrays[name] for name in names))
         if final:
             return results
         arrays.update(zip(made["arrays"], results))

time: 53.8 us -> 52.8 us (0.981)
  Pallas kernels: 6.91 us -> 5.31 us
  other arithmetic: 0 us -> 0.68 us
  local copies, waits for them, and re-layouts: 2.17 us -> 1.59 us
    pallas_call x2, Pallas kernels: 5.79 us -> 4.75 us  [multiply(): pl.pallas_call(body, out_shape=jax.ShapeDtypeStruct(blocks.shape, dtype)...]
    unnamed x6 -> x2, local copies, waits for them, and re-layouts: 2.17 us -> 1.47 us
    convert_element_type x0 -> x1, other arithmetic: none -> 0.68 us  [local(): keep.astype(dtype)[:, :, None, None]]
    pallas_call x1, Pallas kernels: 1.12 us -> 0.56 us  [local(): pl.pallas_call(lambda *refs: pack_kernel(layout, *refs), out_shape=[tiles...]
  transfers between devices with their start and end apart: 14 -> 14, of which waited for: 8 -> 9; matrix products, arithmetic and copies ran while one was open for 0% -> 0% of each run, Pallas kernels for 3% -> 2%
where the time goes in v4:
time: 52.8 us; the launch traced here: 52.6 us
  waiting for transfers between devices  31.9 us (60%)
  starting transfers between devices  13 us (25%)
  Pallas kernels  5.31 us (10%)
  local copies, waits for them, and re-layouts  1.59 us (3%)
  other arithmetic  0.68 us (1%)
    ppermute x14, waiting for transfers between devices, move(): arrays[name] = lax.ppermute(operand, axis, towards)  31.9 us
    ppermute x14, starting transfers between devices, move(): arrays[name] = lax.ppermute(operand, axis, towards)  13 us
    pallas_call x2, Pallas kernels, multiply(): pl.pallas_call(body, out_shape=jax.ShapeDtypeStruct(blocks.shape, dtype)...  4.75 us
    unnamed x2, local copies, waits for them, and re-layouts  1.47 us
  transfers between devices with their start and end apart: 14, of which 9 were waited for; matrix products, arithmetic and copies ran while one was open for 0% of the time, Pallas kernels for 2%

profile of v4, /device:TPU:0, one launch (start us, length us, event | category | flops | bytes accessed | tf_op | source)
XLA Modules:
  0.0 52.6 jit_solution(3644752704639714949)
XLA Ops:
  0.0 0.7 %convert_bitcast_fusion = bf16[2,27]{1,0:T(2,128)(2,1)S(1)} fusion(s32[1,1,2,27]{3,2,1,0:T(2,128)} %param.3), kind=kLoop, calls=%fused_computation | loop fusion | flops 54 | bytes 324 | tf_op jit(solution)/shard_map/convert_element_type | solution.py:187
  0.7 0.1 broadcast_in_dim.4.refs_0_.refs_2_.refs_4_
  0.8 0.0 copy-start
  0.8 1.5 %copy-done = bf16[1,1,2,27,128,128]{5,4,3,2,1,0:T(8,128)(2,1)S(1)} copy-done((bf16[1,1,2,27,128,128]{5,4,3,2,1,0:T(8,128)(2,1)S(1)}, bf16[1,1,2,27,128,128]{5,4,3,2,1,0:T(8,128)(2,1)}, u32[]{:S(2)}) %copy-start) | copy-done | bytes 1769496
  2.3 0.6 %pack.1 = (bf16[9,256,256]{2,1,0:T(8,128)(2,1)S(1)}, bf16[4,256,256]{2,1,0:T(8,128)(2,1)S(1)}, bf16[2,256,256]{2,1,0:T(8,128)(2,1)S(1)}, bf16[2,256,256]{2,1,0:T...) custom-call(bf16[2,27,16,128]{3,2,1,0:T(8,128)(2,1)S(1)} %broadcast_, ...), custom_call_target="tpu_custom_call" | custom-call | tf_op jit(solution)/shard_map/pack/pallas_call | solution.py:189
  2.9 3.1 %collective-permute-start = (bf16[4,256,256]{2,1,0:T(8,128)(2,1)S(1)}, bf16[4,256,256]{2,1,0:T(8,128)(2,1)S(1)}, u32[]{:S(2)}, u32[]{:S(2)}) collective-permute-start(bf16[4,256,256]{2,1,0:T(8,128)(2,1)S(1)} %get-tuple-element.38), channel_id=1, source_target_pairs={{0,1},{1,2},{2,3},{3,0},{4,5},{5,6},{6,7},{7,4},{8,9},{9,10},{10,1... | collective-permute-start | bytes 1572872 | tf_op jit(solution)/shard_map/ppermute | solution.py:212
  5.9 0.7 %collective-permute-start.3 = (bf16[6,256,256]{2,1,0:T(8,128)(2,1)S(1)}, bf16[6,256,256]{2,1,0:T(8,128)(2,1)S(1)}, u32[]{:S(2)}, u32[]{:S(2)}) collective-permute-start(bf16[6,256,256]{2,1,0:T(8,128)(2,1)S(1)} %get-tuple-element.46), channel_id=1, source_target_pairs={{4,8},{8,4},{12,0},{0,12},{5,9},{9,5},{13,1},{1,13},{6,10},{10,6},... | collective-permute-start | bytes 2359304 | tf_op jit(solution)/shard_map/ppermute | solution.py:212
  6.6 13.3 %collective-permute-done.refs_4_.refs_13_ = bf16[4,256,256]{2,1,0:T(8,128)(2,1)S(1)} collective-permute-done((bf16[4,256,256]{2,1,0:T(8,128)(2,1)S(1)}, bf16[4,256,256]{2,1,0:T(8,128)(2,1)S(1)}, u32[]{:S(2)}, u32[]{:S(2)}) %collective-permute-start) | collective-permute-done | bytes 524320 | tf_op jit(solution)/shard_map/ppermute | solution.py:212
  19.9 1.7 %collective-permute-start.1 = (bf16[2,256,256]{2,1,0:T(8,128)(2,1)S(1)}, bf16[2,256,256]{2,1,0:T(8,128)(2,1)S(1)}, u32[]{:S(2)}, u32[]{:S(2)}) collective-permute-start(bf16[2,256,256]{2,1,0:T(8,128)(2,1)S(1)} %get-tuple-element.39), channel_id=1, source_target_pairs={{0,3},{1,0},{2,1},{3,2},{4,7},{5,4},{6,5},{7,6},{8,11},{9,8},{10,9... | collective-permute-start | bytes 786440 | tf_op jit(solution)/shard_map/ppermute | solution.py:212
  21.6 0.0 collective-permute-start.4
  21.6 0.4 collective-permute-start.2
  22.1 6.8 %collective-permute-done.1.refs_0_.refs_1_ = bf16[2,256,256]{2,1,0:T(8,128)(2,1)S(1)} collective-permute-done((bf16[2,256,256]{2,1,0:T(8,128)(2,1)S(1)}, bf16[2,256,256]{2,1,0:T(8,128)(2,1)S(1)}, u32[]{:S(2)}, u32[]{:S(2)}) %collective-permute-start.1) | collective-permute-done | bytes 262176 | tf_op jit(solution)/shard_map/ppermute | solution.py:212
  28.9 0.0 collective-permute-start.6
  28.9 0.5 collective-permute-start.11
  29.4 0.0 collective-permute-done.3.refs_5_.refs_17_
  29.4 3.8 %collective-permute-start.7 = (bf16[2,256,256]{2,1,0:T(8,128)(2,1)S(1)}, bf16[2,256,256]{2,1,0:T(8,128)(2,1)S(1)}, u32[]{:S(2)}, u32[]{:S(2)}) collective-permute-start(bf16[2,256,256]{2,1,0:T(8,128)(2,1)S(1)} %get-tuple-element.57), channel_id=1, source_target_pairs={{0,3},{1,0},{2,1},{3,2},{4,7},{5,4},{6,5},{7,6},{8,11},{9,8},{10,9... | collective-permute-start | bytes 786440 | tf_op jit(solution)/shard_map/ppermute | solution.py:212
  33.2 0.8 %collective-permute-done.2.refs_1_.refs_2_ = bf16[2,256,256]{2,1,0:T(8,128)(2,1)S(1)} collective-permute-done((bf16[2,256,256]{2,1,0:T(8,128)(2,1)S(1)}, bf16[2,256,256]{2,1,0:T(8,128)(2,1)S(1)}, u32[]{:S(2)}, u32[]{:S(2)}) %collective-permute-start.2) | collective-permute-done | bytes 262176 | tf_op jit(solution)/shard_map/ppermute | solution.py:212
  33.9 0.1 collective-permute-start.8
  34.0 3.0 %collective-permute-done.4.refs_6_ = bf16[4,256,256]{2,1,0:T(8,128)(2,1)S(1)} collective-permute-done((bf16[4,256,256]{2,1,0:T(8,128)(2,1)S(1)}, bf16[4,256,256]{2,1,0:T(8,128)(2,1)S(1)}, u32[]{:S(2)}, u32[]{:S(2)}) %collective-permute-start.4) | collective-permute-done | bytes 524320 | tf_op jit(solution)/shard_map/ppermute | solution.py:212
  37.0 1.6 %collective-permute-start.5 = (bf16[2,256,256]{2,1,0:T(8,128)(2,1)S(1)}, bf16[2,256,256]{2,1,0:T(8,128)(2,1)S(1)}, u32[]{:S(2)}, u32[]{:S(2)}) collective-permute-start(bf16[2,256,256]{2,1,0:T(8,128)(2,1)S(1)} %get-tuple-element.54), channel_id=1, source_target_pairs={{0,1},{1,2},{2,3},{3,0},{4,5},{5,6},{6,7},{7,4},{8,9},{9,10},{10,1... | collective-permute-start | bytes 786440 | tf_op jit(solution)/shard_map/ppermute | solution.py:212
  38.5 1.2 %product0.1 = (f32[8,256,256]{2,1,0:T(8,128)S(1)}, bf16[1,256,256]{2,1,0:T(8,128)(2,1)S(1)}, f32[4,256,256]{2,1,0:T(8,128)S(1)}) custom-call(bf16[2,256,256]{2,1,0:T(8,128)(2,1)S(1)} %collective-permute-done.1.refs_0_.refs_1_, bf16[2,256,256]{2,1,0:T(8,128)(2,1)S(1)} %collective-permute-done.2.refs_1_.refs_2_, ...), custom_call_target="tpu_custom_call" | custom-call | flops 1 | bytes 1 | tf_op jit(solution)/shard_map/product0/pallas_call | solution.py:248
  39.8 0.0 collective-permute-done.7.refs_3_
  39.8 0.5 collective-permute-start.13
  40.3 2.3 %collective-permute-done.8.refs_15_ = bf16[2,256,256]{2,1,0:T(8,128)(2,1)S(1)} collective-permute-done((bf16[2,256,256]{2,1,0:T(8,128)(2,1)S(1)}, bf16[2,256,256]{2,1,0:T(8,128)(2,1)S(1)}, u32[]{:S(2)}, u32[]{:S(2)}) %collective-permute-start.8) | collective-permute-done | bytes 262176 | tf_op jit(solution)/shard_map/ppermute | solution.py:212
  42.6 0.2 collective-permute-start.10
  42.7 4.4 %collective-permute-done.5.refs_14_ = bf16[2,256,256]{2,1,0:T(8,128)(2,1)S(1)} collective-permute-done((bf16[2,256,256]{2,1,0:T(8,128)(2,1)S(1)}, bf16[2,256,256]{2,1,0:T(8,128)(2,1)S(1)}, u32[]{:S(2)}, u32[]{:S(2)}) %collective-permute-start.5) | collective-permute-done | bytes 262176 | tf_op jit(solution)/shard_map/ppermute | solution.py:212
  47.2 0.0 collective-permute-start.9
  47.2 0.0 collective-permute-done.6.refs_9_
  47.2 0.5 collective-permute-start.12
  47.7 0.7 %collective-permute-done.13.refs_16_ = bf16[2,256,256]{2,1,0:T(8,128)(2,1)S(1)} collective-permute-done((bf16[2,256,256]{2,1,0:T(8,128)(2,1)S(1)}, bf16[2,256,256]{2,1,0:T(8,128)(2,1)S(1)}, u32[]{:S(2)}, u32[]{:S(2)}) %collective-permute-start.13) | collective-permute-done | bytes 262176 | tf_op jit(solution)/shard_map/ppermute | solution.py:212
  48.4 0.0 collective-permute-done.10.refs_7_
  48.4 0.4 collective-permute-done.9.refs_6_
  48.7 0.0 collective-permute-done.11.refs_8_
  48.7 0.4 collective-permute-done.12.refs_10_
  49.1 3.5 %product1.1 = bf16[2,27,128,128]{3,2,1,0:T(8,128)(2,1)} custom-call(f32[4,256,256]{2,1,0:T(8,128)S(1)} %get-tuple-element.48.refs_0_, bf16[2,256,256]{2,1,0:T(8,128)(2,1)S(1)} %collective-permute-done.1.refs_0_.refs_1_, bf16[2,256,256]{2,1,0:T(8,128)(2,1)S(1)} %collective-permute-done.2.refs_1_.refs_2_, ...), custom_call_target="tpu_custom_call" | custom-call | flops 1 | bytes 1 | tf_op jit(solution)/shard_map/product1/pallas_call | solution.py:248
Async XLA Ops:
  0.8 1.5 %copy-start = (bf16[1,1,2,27,128,128]{5,4,3,2,1,0:T(8,128)(2,1)S(1)}, bf16[1,1,2,27,128,128]{5,4,3,2,1,0:T(8,128)(2,1)}, u32[]{:S(2)}) copy-start(bf16[1,1,2,27,128,128]{5,4,3,2,1,0:T(8,128)(2,1)} %param.2) | copy-start | bytes 5308420
  2.9 17.0 %collective-permute-start = (bf16[4,256,256]{2,1,0:T(8,128)(2,1)S(1)}, bf16[4,256,256]{2,1,0:T(8,128)(2,1)S(1)}, u32[]{:S(2)}, u32[]{:S(2)}) collective-permute-start(bf16[4,256,256]{2,1,0:T(8,128)(2,1)S(1)} %get-tuple-element.38), channel_id=1, source_target_pairs={{0,1},{1,2},{2,3},{3,0},{4,5},{5,6},{6,7},{7,4},{8,9},{9,10},{10,1... | collective-permute-start | bytes 1572872 | tf_op jit(solution)/shard_map/ppermute | solution.py:212
  5.9 23.4 %collective-permute-start.3 = (bf16[6,256,256]{2,1,0:T(8,128)(2,1)S(1)}, bf16[6,256,256]{2,1,0:T(8,128)(2,1)S(1)}, u32[]{:S(2)}, u32[]{:S(2)}) collective-permute-start(bf16[6,256,256]{2,1,0:T(8,128)(2,1)S(1)} %get-tuple-element.46), channel_id=1, source_target_pairs={{4,8},{8,4},{12,0},{0,12},{5,9},{9,5},{13,1},{1,13},{6,10},{10,6},... | collective-permute-start | bytes 2359304 | tf_op jit(solution)/shard_map/ppermute | solution.py:212
  19.9 9.0 %collective-permute-start.1 = (bf16[2,256,256]{2,1,0:T(8,128)(2,1)S(1)}, bf16[2,256,256]{2,1,0:T(8,128)(2,1)S(1)}, u32[]{:S(2)}, u32[]{:S(2)}) collective-permute-start(bf16[2,256,256]{2,1,0:T(8,128)(2,1)S(1)} %get-tuple-element.39), channel_id=1, source_target_pairs={{0,3},{1,0},{2,1},{3,2},{4,7},{5,4},{6,5},{7,6},{8,11},{9,8},{10,9... | collective-permute-start | bytes 786440 | tf_op jit(solution)/shard_map/ppermute | solution.py:212
  21.6 15.3 %collective-permute-start.4 = (bf16[4,256,256]{2,1,0:T(8,128)(2,1)S(1)}, bf16[4,256,256]{2,1,0:T(8,128)(2,1)S(1)}, u32[]{:S(2)}, u32[]{:S(2)}) collective-permute-start(bf16[4,256,256]{2,1,0:T(8,128)(2,1)S(1)} %collective-permute-done.refs_4_.refs_13_), channel_id=1, source_target_pairs={{4,8},{8,4},{12,0},{0,12},{5,9},{9,5},{13,1},{1,13},{6,10},{10,6},... | collective-permute-start | bytes 1572872 | tf_op jit(solution)/shard_map/ppermute | solution.py:212
  21.6 12.3 %collective-permute-start.2 = (bf16[2,256,256]{2,1,0:T(8,128)(2,1)S(1)}, bf16[2,256,256]{2,1,0:T(8,128)(2,1)S(1)}, u32[]{:S(2)}, u32[]{:S(2)}) collective-permute-start(bf16[2,256,256]{2,1,0:T(8,128)(2,1)S(1)} %get-tuple-element.42), channel_id=1, source_target_pairs={{0,3},{1,0},{2,1},{3,2},{4,7},{5,4},{6,5},{7,6},{8,11},{9,8},{10,9... | collective-permute-start | bytes 786440 | tf_op jit(solution)/shard_map/ppermute | solution.py:212
  28.9 18.3 %collective-permute-start.6 = (bf16[4,256,256]{2,1,0:T(8,128)(2,1)S(1)}, bf16[4,256,256]{2,1,0:T(8,128)(2,1)S(1)}, u32[]{:S(2)}, u32[]{:S(2)}) collective-permute-start(bf16[4,256,256]{2,1,0:T(8,128)(2,1)S(1)} %collective-permute-done.refs_4_.refs_13_), channel_id=1, source_target_pairs={{0,4},{4,0},{8,12},{12,8},{1,5},{5,1},{9,13},{13,9},{2,6},{6,2},{1... | collective-permute-start | bytes 1572872 | tf_op jit(solution)/shard_map/ppermute | solution.py:212
  28.9 19.9 %collective-permute-start.11 = (bf16[6,256,256]{2,1,0:T(8,128)(2,1)S(1)}, bf16[6,256,256]{2,1,0:T(8,128)(2,1)S(1)}, u32[]{:S(2)}, u32[]{:S(2)}) collective-permute-start(bf16[6,256,256]{2,1,0:T(8,128)(2,1)S(1)} %get-tuple-element.62), channel_id=1, source_target_pairs={{0,4},{4,0},{8,12},{12,8},{1,5},{5,1},{9,13},{13,9},{2,6},{6,2},{1... | collective-permute-start | bytes 2359304 | tf_op jit(solution)/shard_map/ppermute | solution.py:212
  29.4 10.4 %collective-permute-start.7 = (bf16[2,256,256]{2,1,0:T(8,128)(2,1)S(1)}, bf16[2,256,256]{2,1,0:T(8,128)(2,1)S(1)}, u32[]{:S(2)}, u32[]{:S(2)}) collective-permute-start(bf16[2,256,256]{2,1,0:T(8,128)(2,1)S(1)} %get-tuple-element.57), channel_id=1, source_target_pairs={{0,3},{1,0},{2,1},{3,2},{4,7},{5,4},{6,5},{7,6},{8,11},{9,8},{10,9... | collective-permute-start | bytes 786440 | tf_op jit(solution)/shard_map/ppermute | solution.py:212
  33.9 8.6 %collective-permute-start.8 = (bf16[2,256,256]{2,1,0:T(8,128)(2,1)S(1)}, bf16[2,256,256]{2,1,0:T(8,128)(2,1)S(1)}, u32[]{:S(2)}, u32[]{:S(2)}) collective-permute-start(bf16[2,256,256]{2,1,0:T(8,128)(2,1)S(1)} %collective-permute-done.1.refs_0_.refs_1_), channel_id=1, source_target_pairs={{4,8},{8,4},{12,0},{0,12},{5,9},{9,5},{13,1},{1,13},{6,10},{10,6},... | collective-permute-start | bytes 786440 | tf_op jit(solution)/shard_map/ppermute | solution.py:212
  37.0 10.2 %collective-permute-start.5 = (bf16[2,256,256]{2,1,0:T(8,128)(2,1)S(1)}, bf16[2,256,256]{2,1,0:T(8,128)(2,1)S(1)}, u32[]{:S(2)}, u32[]{:S(2)}) collective-permute-start(bf16[2,256,256]{2,1,0:T(8,128)(2,1)S(1)} %get-tuple-element.54), channel_id=1, source_target_pairs={{0,1},{1,2},{2,3},{3,0},{4,5},{5,6},{6,7},{7,4},{8,9},{9,10},{10,1... | collective-permute-start | bytes 786440 | tf_op jit(solution)/shard_map/ppermute | solution.py:212
  39.8 8.6 %collective-permute-start.13 = (bf16[2,256,256]{2,1,0:T(8,128)(2,1)S(1)}, bf16[2,256,256]{2,1,0:T(8,128)(2,1)S(1)}, u32[]{:S(2)}, u32[]{:S(2)}) collective-permute-start(bf16[2,256,256]{2,1,0:T(8,128)(2,1)S(1)} %collective-permute-done.2.refs_1_.refs_2_), channel_id=1, source_target_pairs={{4,8},{8,4},{12,0},{0,12},{5,9},{9,5},{13,1},{1,13},{6,10},{10,6},... | collective-permute-start | bytes 786440 | tf_op jit(solution)/shard_map/ppermute | solution.py:212
  42.6 5.8 %collective-permute-start.10 = (bf16[2,256,256]{2,1,0:T(8,128)(2,1)S(1)}, bf16[2,256,256]{2,1,0:T(8,128)(2,1)S(1)}, u32[]{:S(2)}, u32[]{:S(2)}) collective-permute-start(bf16[2,256,256]{2,1,0:T(8,128)(2,1)S(1)} %collective-permute-done.7.refs_3_), channel_id=1, source_target_pairs={{0,4},{4,0},{8,12},{12,8},{1,5},{5,1},{9,13},{13,9},{2,6},{6,2},{1... | collective-permute-start | bytes 786440 | tf_op jit(solution)/shard_map/ppermute | solution.py:212
  47.2 1.5 %collective-permute-start.9 = (bf16[2,256,256]{2,1,0:T(8,128)(2,1)S(1)}, bf16[2,256,256]{2,1,0:T(8,128)(2,1)S(1)}, u32[]{:S(2)}, u32[]{:S(2)}) collective-permute-start(bf16[2,256,256]{2,1,0:T(8,128)(2,1)S(1)} %collective-permute-done.1.refs_0_.refs_1_), channel_id=1, source_target_pairs={{0,4},{4,0},{8,12},{12,8},{1,5},{5,1},{9,13},{13,9},{2,6},{6,2},{1... | collective-permute-start | bytes 786440 | tf_op jit(solution)/shard_map/ppermute | solution.py:212
  47.2 1.9 %collective-permute-start.12 = (bf16[2,256,256]{2,1,0:T(8,128)(2,1)S(1)}, bf16[2,256,256]{2,1,0:T(8,128)(2,1)S(1)}, u32[]{:S(2)}, u32[]{:S(2)}) collective-permute-start(bf16[2,256,256]{2,1,0:T(8,128)(2,1)S(1)} %collective-permute-done.5.refs_14_), channel_id=1, source_target_pairs={{0,4},{4,0},{8,12},{12,8},{1,5},{5,1},{9,13},{13,9},{2,6},{6,2},{1... | collective-permute-start | bytes 786440 | tf_op jit(solution)/shard_map/ppermute | solution.py:212

commit v5 on v4

--- a/solution.py
+++ b/solution.py
@@ -184,7 +184,7 @@
     sent |= {name: (held, "col", down) for name, held in PIECES[-1].items()}
     sent |= {"x_" + name: (held, "row", far) for name, held in EDGES[1].items()}
     sent |= {"n_" + name: (held, "row", near) for name, held in EDGES[-1].items()}
-    mask = jnp.broadcast_to(keep.astype(dtype)[:, :, None, None], (*keep.shape, 16, width))
+    mask = jnp.broadcast_to(keep.astype(dtype)[:, :, None, None], (*keep.shape, width, width))
     layout = [CELLS] + [held for held, _, _ in sent.values()]
     packed = pl.pallas_call(
         lambda *refs: pack_kernel(layout, *refs),

time: 52.8 us -> 51.8 us (0.981)
  local copies, waits for them, and re-layouts: 1.59 us -> 0.67 us
    unnamed x2, local copies, waits for them, and re-layouts: 1.47 us -> 0.37 us
where the time goes in v5:
time: 51.8 us; the launch traced here: 51.7 us
  waiting for transfers between devices  31.9 us (62%)
  starting transfers between devices  13 us (25%)
  Pallas kernels  5.17 us (10%)
  other arithmetic  0.81 us (2%)
  local copies, waits for them, and re-layouts  0.67 us (1%)
    ppermute x14, waiting for transfers between devices, move(): arrays[name] = lax.ppermute(operand, axis, towards)  31.9 us
    ppermute x14, starting transfers between devices, move(): arrays[name] = lax.ppermute(operand, axis, towards)  13 us
    pallas_call x2, Pallas kernels, multiply(): pl.pallas_call(body, out_shape=jax.ShapeDtypeStruct(blocks.shape, dtype)...  4.59 us
  transfers between devices with their start and end apart: 14, of which 9 were waited for; matrix products, arithmetic and copies ran while one was open for 0% of the time, Pallas kernels for 2%

profile of v5, /device:TPU:0, one launch (start us, length us, event | category | flops | bytes accessed | tf_op | source)
XLA Modules:
  0.0 51.7 jit_solution(7149993008929098900)
XLA Ops:
  0.0 0.0 copy-start
  0.0 0.8 %convert_bitcast_fusion = bf16[2,27]{1,0:T(2,128)(2,1)S(1)} fusion(s32[1,1,2,27]{3,2,1,0:T(2,128)} %param.3), kind=kLoop, calls=%fused_computation | loop fusion | flops 54 | bytes 324 | tf_op jit(solution)/shard_map/convert_element_type | solution.py:187
  0.8 0.3 broadcast_in_dim.4.refs_0_.refs_2_.refs_4_
  1.1 0.4 copy-done
  1.5 0.6 %pack.1 = (bf16[9,256,256]{2,1,0:T(8,128)(2,1)S(1)}, bf16[4,256,256]{2,1,0:T(8,128)(2,1)S(1)}, bf16[2,256,256]{2,1,0:T(8,128)(2,1)S(1)}, bf16[2,256,256]{2,1,0:T...) custom-call(bf16[2,27,128,128]{3,2,1,0:T(8,128)(2,1)S(1)} %broadcast, ...), custom_call_target="tpu_custom_call" | custom-call | tf_op jit(solution)/shard_map/pack/pallas_call | solution.py:189
  2.1 3.1 %collective-permute-start = (bf16[4,256,256]{2,1,0:T(8,128)(2,1)S(1)}, bf16[4,256,256]{2,1,0:T(8,128)(2,1)S(1)}, u32[]{:S(2)}, u32[]{:S(2)}) collective-permute-start(bf16[4,256,256]{2,1,0:T(8,128)(2,1)S(1)} %get-tuple-element.38), channel_id=1, source_target_pairs={{0,1},{1,2},{2,3},{3,0},{4,5},{5,6},{6,7},{7,4},{8,9},{9,10},{10,1... | collective-permute-start | bytes 1572872 | tf_op jit(solution)/shard_map/ppermute | solution.py:212
  5.1 0.7 %collective-permute-start.3 = (bf16[6,256,256]{2,1,0:T(8,128)(2,1)S(1)}, bf16[6,256,256]{2,1,0:T(8,128)(2,1)S(1)}, u32[]{:S(2)}, u32[]{:S(2)}) collective-permute-start(bf16[6,256,256]{2,1,0:T(8,128)(2,1)S(1)} %get-tuple-element.46), channel_id=1, source_target_pairs={{4,8},{8,4},{12,0},{0,12},{5,9},{9,5},{13,1},{1,13},{6,10},{10,6},... | collective-permute-start | bytes 2359304 | tf_op jit(solution)/shard_map/ppermute | solution.py:212
  5.8 13.3 %collective-permute-done.refs_4_.refs_13_ = bf16[4,256,256]{2,1,0:T(8,128)(2,1)S(1)} collective-permute-done((bf16[4,256,256]{2,1,0:T(8,128)(2,1)S(1)}, bf16[4,256,256]{2,1,0:T(8,128)(2,1)S(1)}, u32[]{:S(2)}, u32[]{:S(2)}) %collective-permute-start) | collective-permute-done | bytes 524320 | tf_op jit(solution)/shard_map/ppermute | solution.py:212
  19.1 1.7 %collective-permute-start.1 = (bf16[2,256,256]{2,1,0:T(8,128)(2,1)S(1)}, bf16[2,256,256]{2,1,0:T(8,128)(2,1)S(1)}, u32[]{:S(2)}, u32[]{:S(2)}) collective-permute-start(bf16[2,256,256]{2,1,0:T(8,128)(2,1)S(1)} %get-tuple-element.39), channel_id=1, source_target_pairs={{0,3},{1,0},{2,1},{3,2},{4,7},{5,4},{6,5},{7,6},{8,11},{9,8},{10,9... | collective-permute-start | bytes 786440 | tf_op jit(solution)/shard_map/ppermute | solution.py:212
  20.8 0.0 collective-permute-start.4
  20.8 0.4 collective-permute-start.2
  21.3 6.8 %collective-permute-done.1.refs_0_.refs_1_ = bf16[2,256,256]{2,1,0:T(8,128)(2,1)S(1)} collective-permute-done((bf16[2,256,256]{2,1,0:T(8,128)(2,1)S(1)}, bf16[2,256,256]{2,1,0:T(8,128)(2,1)S(1)}, u32[]{:S(2)}, u32[]{:S(2)}) %collective-permute-start.1) | collective-permute-done | bytes 262176 | tf_op jit(solution)/shard_map/ppermute | solution.py:212
  28.1 0.0 collective-permute-start.6
  28.1 0.5 collective-permute-start.11
  28.6 0.0 collective-permute-done.3.refs_5_.refs_17_
  28.6 3.8 %collective-permute-start.7 = (bf16[2,256,256]{2,1,0:T(8,128)(2,1)S(1)}, bf16[2,256,256]{2,1,0:T(8,128)(2,1)S(1)}, u32[]{:S(2)}, u32[]{:S(2)}) collective-permute-start(bf16[2,256,256]{2,1,0:T(8,128)(2,1)S(1)} %get-tuple-element.57), channel_id=1, source_target_pairs={{0,3},{1,0},{2,1},{3,2},{4,7},{5,4},{6,5},{7,6},{8,11},{9,8},{10,9... | collective-permute-start | bytes 786440 | tf_op jit(solution)/shard_map/ppermute | solution.py:212
  32.4 0.8 %collective-permute-done.2.refs_1_.refs_2_ = bf16[2,256,256]{2,1,0:T(8,128)(2,1)S(1)} collective-permute-done((bf16[2,256,256]{2,1,0:T(8,128)(2,1)S(1)}, bf16[2,256,256]{2,1,0:T(8,128)(2,1)S(1)}, u32[]{:S(2)}, u32[]{:S(2)}) %collective-permute-start.2) | collective-permute-done | bytes 262176 | tf_op jit(solution)/shard_map/ppermute | solution.py:212
  33.2 0.1 collective-permute-start.8
  33.2 3.0 %collective-permute-done.4.refs_6_ = bf16[4,256,256]{2,1,0:T(8,128)(2,1)S(1)} collective-permute-done((bf16[4,256,256]{2,1,0:T(8,128)(2,1)S(1)}, bf16[4,256,256]{2,1,0:T(8,128)(2,1)S(1)}, u32[]{:S(2)}, u32[]{:S(2)}) %collective-permute-start.4) | collective-permute-done | bytes 524320 | tf_op jit(solution)/shard_map/ppermute | solution.py:212
  36.2 1.6 %collective-permute-start.5 = (bf16[2,256,256]{2,1,0:T(8,128)(2,1)S(1)}, bf16[2,256,256]{2,1,0:T(8,128)(2,1)S(1)}, u32[]{:S(2)}, u32[]{:S(2)}) collective-permute-start(bf16[2,256,256]{2,1,0:T(8,128)(2,1)S(1)} %get-tuple-element.54), channel_id=1, source_target_pairs={{0,1},{1,2},{2,3},{3,0},{4,5},{5,6},{6,7},{7,4},{8,9},{9,10},{10,1... | collective-permute-start | bytes 786440 | tf_op jit(solution)/shard_map/ppermute | solution.py:212
  37.8 1.2 %product0.1 = (f32[8,256,256]{2,1,0:T(8,128)S(1)}, bf16[1,256,256]{2,1,0:T(8,128)(2,1)S(1)}, f32[4,256,256]{2,1,0:T(8,128)S(1)}) custom-call(bf16[2,256,256]{2,1,0:T(8,128)(2,1)S(1)} %collective-permute-done.1.refs_0_.refs_1_, bf16[2,256,256]{2,1,0:T(8,128)(2,1)S(1)} %collective-permute-done.2.refs_1_.refs_2_, ...), custom_call_target="tpu_custom_call" | custom-call | flops 1 | bytes 1 | tf_op jit(solution)/shard_map/product0/pallas_call | solution.py:248
  39.0 0.0 collective-permute-done.7.refs_3_
  39.0 0.5 collective-permute-start.13
  39.5 2.3 %collective-permute-done.8.refs_15_ = bf16[2,256,256]{2,1,0:T(8,128)(2,1)S(1)} collective-permute-done((bf16[2,256,256]{2,1,0:T(8,128)(2,1)S(1)}, bf16[2,256,256]{2,1,0:T(8,128)(2,1)S(1)}, u32[]{:S(2)}, u32[]{:S(2)}) %collective-permute-start.8) | collective-permute-done | bytes 262176 | tf_op jit(solution)/shard_map/ppermute | solution.py:212
  41.8 0.2 collective-permute-start.10
  42.0 4.4 %collective-permute-done.5.refs_14_ = bf16[2,256,256]{2,1,0:T(8,128)(2,1)S(1)} collective-permute-done((bf16[2,256,256]{2,1,0:T(8,128)(2,1)S(1)}, bf16[2,256,256]{2,1,0:T(8,128)(2,1)S(1)}, u32[]{:S(2)}, u32[]{:S(2)}) %collective-permute-start.5) | collective-permute-done | bytes 262176 | tf_op jit(solution)/shard_map/ppermute | solution.py:212
  46.4 0.0 collective-permute-start.9
  46.4 0.0 collective-permute-done.6.refs_9_
  46.4 0.5 collective-permute-start.12
  46.9 0.7 %collective-permute-done.13.refs_16_ = bf16[2,256,256]{2,1,0:T(8,128)(2,1)S(1)} collective-permute-done((bf16[2,256,256]{2,1,0:T(8,128)(2,1)S(1)}, bf16[2,256,256]{2,1,0:T(8,128)(2,1)S(1)}, u32[]{:S(2)}, u32[]{:S(2)}) %collective-permute-start.13) | collective-permute-done | bytes 262176 | tf_op jit(solution)/shard_map/ppermute | solution.py:212
  47.6 0.0 collective-permute-done.10.refs_7_
  47.6 0.4 collective-permute-done.9.refs_6_
  47.9 0.0 collective-permute-done.11.refs_8_
  47.9 0.4 collective-permute-done.12.refs_10_
  48.3 3.4 %product1.1 = bf16[2,27,128,128]{3,2,1,0:T(8,128)(2,1)} custom-call(f32[4,256,256]{2,1,0:T(8,128)S(1)} %get-tuple-element.48.refs_0_, bf16[2,256,256]{2,1,0:T(8,128)(2,1)S(1)} %collective-permute-done.1.refs_0_.refs_1_, bf16[2,256,256]{2,1,0:T(8,128)(2,1)S(1)} %collective-permute-done.2.refs_1_.refs_2_, ...), custom_call_target="tpu_custom_call" | custom-call | flops 1 | bytes 1 | tf_op jit(solution)/shard_map/product1/pallas_call | solution.py:248
Async XLA Ops:
  0.0 1.5 %copy-start = (bf16[1,1,2,27,128,128]{5,4,3,2,1,0:T(8,128)(2,1)S(1)}, bf16[1,1,2,27,128,128]{5,4,3,2,1,0:T(8,128)(2,1)}, u32[]{:S(2)}) copy-start(bf16[1,1,2,27,128,128]{5,4,3,2,1,0:T(8,128)(2,1)} %param.2) | copy-start | bytes 5308420
  2.1 17.0 %collective-permute-start = (bf16[4,256,256]{2,1,0:T(8,128)(2,1)S(1)}, bf16[4,256,256]{2,1,0:T(8,128)(2,1)S(1)}, u32[]{:S(2)}, u32[]{:S(2)}) collective-permute-start(bf16[4,256,256]{2,1,0:T(8,128)(2,1)S(1)} %get-tuple-element.38), channel_id=1, source_target_pairs={{0,1},{1,2},{2,3},{3,0},{4,5},{5,6},{6,7},{7,4},{8,9},{9,10},{10,1... | collective-permute-start | bytes 1572872 | tf_op jit(solution)/shard_map/ppermute | solution.py:212
  5.1 23.4 %collective-permute-start.3 = (bf16[6,256,256]{2,1,0:T(8,128)(2,1)S(1)}, bf16[6,256,256]{2,1,0:T(8,128)(2,1)S(1)}, u32[]{:S(2)}, u32[]{:S(2)}) collective-permute-start(bf16[6,256,256]{2,1,0:T(8,128)(2,1)S(1)} %get-tuple-element.46), channel_id=1, source_target_pairs={{4,8},{8,4},{12,0},{0,12},{5,9},{9,5},{13,1},{1,13},{6,10},{10,6},... | collective-permute-start | bytes 2359304 | tf_op jit(solution)/shard_map/ppermute | solution.py:212
  19.1 9.0 %collective-permute-start.1 = (bf16[2,256,256]{2,1,0:T(8,128)(2,1)S(1)}, bf16[2,256,256]{2,1,0:T(8,128)(2,1)S(1)}, u32[]{:S(2)}, u32[]{:S(2)}) collective-permute-start(bf16[2,256,256]{2,1,0:T(8,128)(2,1)S(1)} %get-tuple-element.39), channel_id=1, source_target_pairs={{0,3},{1,0},{2,1},{3,2},{4,7},{5,4},{6,5},{7,6},{8,11},{9,8},{10,9... | collective-permute-start | bytes 786440 | tf_op jit(solution)/shard_map/ppermute | solution.py:212
  20.8 15.3 %collective-permute-start.4 = (bf16[4,256,256]{2,1,0:T(8,128)(2,1)S(1)}, bf16[4,256,256]{2,1,0:T(8,128)(2,1)S(1)}, u32[]{:S(2)}, u32[]{:S(2)}) collective-permute-start(bf16[4,256,256]{2,1,0:T(8,128)(2,1)S(1)} %collective-permute-done.refs_4_.refs_13_), channel_id=1, source_target_pairs={{4,8},{8,4},{12,0},{0,12},{5,9},{9,5},{13,1},{1,13},{6,10},{10,6},... | collective-permute-start | bytes 1572872 | tf_op jit(solution)/shard_map/ppermute | solution.py:212
  20.8 12.3 %collective-permute-start.2 = (bf16[2,256,256]{2,1,0:T(8,128)(2,1)S(1)}, bf16[2,256,256]{2,1,0:T(8,128)(2,1)S(1)}, u32[]{:S(2)}, u32[]{:S(2)}) collective-permute-start(bf16[2,256,256]{2,1,0:T(8,128)(2,1)S(1)} %get-tuple-element.42), channel_id=1, source_target_pairs={{0,3},{1,0},{2,1},{3,2},{4,7},{5,4},{6,5},{7,6},{8,11},{9,8},{10,9... | collective-permute-start | bytes 786440 | tf_op jit(solution)/shard_map/ppermute | solution.py:212
  28.1 18.3 %collective-permute-start.6 = (bf16[4,256,256]{2,1,0:T(8,128)(2,1)S(1)}, bf16[4,256,256]{2,1,0:T(8,128)(2,1)S(1)}, u32[]{:S(2)}, u32[]{:S(2)}) collective-permute-start(bf16[4,256,256]{2,1,0:T(8,128)(2,1)S(1)} %collective-permute-done.refs_4_.refs_13_), channel_id=1, source_target_pairs={{0,4},{4,0},{8,12},{12,8},{1,5},{5,1},{9,13},{13,9},{2,6},{6,2},{1... | collective-permute-start | bytes 1572872 | tf_op jit(solution)/shard_map/ppermute | solution.py:212
  28.1 19.9 %collective-permute-start.11 = (bf16[6,256,256]{2,1,0:T(8,128)(2,1)S(1)}, bf16[6,256,256]{2,1,0:T(8,128)(2,1)S(1)}, u32[]{:S(2)}, u32[]{:S(2)}) collective-permute-start(bf16[6,256,256]{2,1,0:T(8,128)(2,1)S(1)} %get-tuple-element.62), channel_id=1, source_target_pairs={{0,4},{4,0},{8,12},{12,8},{1,5},{5,1},{9,13},{13,9},{2,6},{6,2},{1... | collective-permute-start | bytes 2359304 | tf_op jit(solution)/shard_map/ppermute | solution.py:212
  28.6 10.4 %collective-permute-start.7 = (bf16[2,256,256]{2,1,0:T(8,128)(2,1)S(1)}, bf16[2,256,256]{2,1,0:T(8,128)(2,1)S(1)}, u32[]{:S(2)}, u32[]{:S(2)}) collective-permute-start(bf16[2,256,256]{2,1,0:T(8,128)(2,1)S(1)} %get-tuple-element.57), channel_id=1, source_target_pairs={{0,3},{1,0},{2,1},{3,2},{4,7},{5,4},{6,5},{7,6},{8,11},{9,8},{10,9... | collective-permute-start | bytes 786440 | tf_op jit(solution)/shard_map/ppermute | solution.py:212
  33.2 8.6 %collective-permute-start.8 = (bf16[2,256,256]{2,1,0:T(8,128)(2,1)S(1)}, bf16[2,256,256]{2,1,0:T(8,128)(2,1)S(1)}, u32[]{:S(2)}, u32[]{:S(2)}) collective-permute-start(bf16[2,256,256]{2,1,0:T(8,128)(2,1)S(1)} %collective-permute-done.1.refs_0_.refs_1_), channel_id=1, source_target_pairs={{4,8},{8,4},{12,0},{0,12},{5,9},{9,5},{13,1},{1,13},{6,10},{10,6},... | collective-permute-start | bytes 786440 | tf_op jit(solution)/shard_map/ppermute | solution.py:212
  36.2 10.2 %collective-permute-start.5 = (bf16[2,256,256]{2,1,0:T(8,128)(2,1)S(1)}, bf16[2,256,256]{2,1,0:T(8,128)(2,1)S(1)}, u32[]{:S(2)}, u32[]{:S(2)}) collective-permute-start(bf16[2,256,256]{2,1,0:T(8,128)(2,1)S(1)} %get-tuple-element.54), channel_id=1, source_target_pairs={{0,1},{1,2},{2,3},{3,0},{4,5},{5,6},{6,7},{7,4},{8,9},{9,10},{10,1... | collective-permute-start | bytes 786440 | tf_op jit(solution)/shard_map/ppermute | solution.py:212
  39.0 8.6 %collective-permute-start.13 = (bf16[2,256,256]{2,1,0:T(8,128)(2,1)S(1)}, bf16[2,256,256]{2,1,0:T(8,128)(2,1)S(1)}, u32[]{:S(2)}, u32[]{:S(2)}) collective-permute-start(bf16[2,256,256]{2,1,0:T(8,128)(2,1)S(1)} %collective-permute-done.2.refs_1_.refs_2_), channel_id=1, source_target_pairs={{4,8},{8,4},{12,0},{0,12},{5,9},{9,5},{13,1},{1,13},{6,10},{10,6},... | collective-permute-start | bytes 786440 | tf_op jit(solution)/shard_map/ppermute | solution.py:212
  41.8 5.8 %collective-permute-start.10 = (bf16[2,256,256]{2,1,0:T(8,128)(2,1)S(1)}, bf16[2,256,256]{2,1,0:T(8,128)(2,1)S(1)}, u32[]{:S(2)}, u32[]{:S(2)}) collective-permute-start(bf16[2,256,256]{2,1,0:T(8,128)(2,1)S(1)} %collective-permute-done.7.refs_3_), channel_id=1, source_target_pairs={{0,4},{4,0},{8,12},{12,8},{1,5},{5,1},{9,13},{13,9},{2,6},{6,2},{1... | collective-permute-start | bytes 786440 | tf_op jit(solution)/shard_map/ppermute | solution.py:212
  46.4 1.5 %collective-permute-start.9 = (bf16[2,256,256]{2,1,0:T(8,128)(2,1)S(1)}, bf16[2,256,256]{2,1,0:T(8,128)(2,1)S(1)}, u32[]{:S(2)}, u32[]{:S(2)}) collective-permute-start(bf16[2,256,256]{2,1,0:T(8,128)(2,1)S(1)} %collective-permute-done.1.refs_0_.refs_1_), channel_id=1, source_target_pairs={{0,4},{4,0},{8,12},{12,8},{1,5},{5,1},{9,13},{13,9},{2,6},{6,2},{1... | collective-permute-start | bytes 786440 | tf_op jit(solution)/shard_map/ppermute | solution.py:212
  46.4 1.9 %collective-permute-start.12 = (bf16[2,256,256]{2,1,0:T(8,128)(2,1)S(1)}, bf16[2,256,256]{2,1,0:T(8,128)(2,1)S(1)}, u32[]{:S(2)}, u32[]{:S(2)}) collective-permute-start(bf16[2,256,256]{2,1,0:T(8,128)(2,1)S(1)} %collective-permute-done.5.refs_14_), channel_id=1, source_target_pairs={{0,4},{4,0},{8,12},{12,8},{1,5},{5,1},{9,13},{13,9},{2,6},{6,2},{1... | collective-permute-start | bytes 786440 | tf_op jit(solution)/shard_map/ppermute | solution.py:212

commit v6 on v5

--- a/solution.py
+++ b/solution.py
@@ -15,12 +15,12 @@
     1: {"up": [(0, 0), (0, 1), (1, 0), (1, 1)], "up_rest": [(-1, 0), (-1, 1)]},
     -1: {"down0": [(0, -1), (0, 0)], "down1": [(1, -1), (1, 0)], "down2": [(-1, -1), (-1, 0)]},
 }
-STAGES = [['mat', 'x_in', 'up', 'x_up', 'down1', 'down0'],
- ['up_rest', 'down2', 'x_down0', 'x_down1', 'n_in', 'n_up', 'n_down0', 'n_down2', 'n_up_rest']]
-SCHEDULE = [('x_in', []), ('up', []), ('x_up', []), ('down0', ['up']), ('up_rest', ['x_in']), ('down1', ['up']), (0, []),
- ('down2', ['x_in']), ('x_down0', []), ('x_down1', ['down1']), ('n_in', ['down0']), ('n_up', ['down0']),
- ('n_down0', ['sum_0']), ('n_down2', ['sum_0']), ('n_up_rest', ['down1', 'n_up', 'sum_0', 'x_down0']),
- (1, [])]
+STAGES = [['mat', 'x_in', 'x_up'], ['up', 'down1'],
+ ['up_rest', 'down2', 'x_down0', 'x_down1', 'n_in', 'n_up', 'n_down2', 'down0', 'n_down0', 'n_up_rest']]
+SCHEDULE = [('x_in', []), ('up', []), ('x_up', []), (0, []), ('down0', ['up']), ('down1', ['up']), (1, []),
+ ('up_rest', ['x_in']), ('down2', ['x_in']), ('x_down0', []), ('x_down1', ['x_up']), ('n_in', []),
+ ('n_up', ['down0', 'n_in']), ('n_down0', ['sum_0', 'x_in']), ('n_down2', ['sum_0']),
+ ('n_up_rest', ['down1', 'n_up', 'sum_0', 'x_down0']), (2, [])]
 
 
 def holder(a, c):

time: 51.8 us -> 50.4 us (0.973)
  waiting for transfers between devices: 31.9 us -> 28 us
  starting transfers between devices: 13 us -> 15.4 us
    ppermute x14, waiting for transfers between devices: 31.9 us -> 28 us  [move(): arrays[name] = lax.ppermute(operand, axis, towards)]
    ppermute x14, starting transfers between devices: 13 us -> 15.4 us  [move(): arrays[name] = lax.ppermute(operand, axis, towards)]
    pallas_call x2 -> x3, Pallas kernels: 4.59 us -> 4.77 us  [multiply(): pl.pallas_call(body, out_shape=jax.ShapeDtypeStruct(blocks.shape, dtype)...]
  transfers between devices with their start and end apart: 14 -> 14, of which waited for: 9 -> 6; matrix products, arithmetic and copies ran while one was open for 0% -> 0% of each run, Pallas kernels for 2% -> 3%
where the time goes in v6:
time: 50.4 us; the launch traced here: 50.3 us
  waiting for transfers between devices  28 us (56%)
  starting transfers between devices  15.4 us (31%)
  Pallas kernels  5.34 us (11%)
  other arithmetic  0.81 us (2%)
  local copies, waits for them, and re-layouts  0.67 us (1%)
    ppermute x14, waiting for transfers between devices, move(): arrays[name] = lax.ppermute(operand, axis, towards)  28 us
    ppermute x14, starting transfers between devices, move(): arrays[name] = lax.ppermute(operand, axis, towards)  15.4 us
    pallas_call x3, Pallas kernels, multiply(): pl.pallas_call(body, out_shape=jax.ShapeDtypeStruct(blocks.shape, dtype)...  4.77 us
  transfers between devices with their start and end apart: 14, of which 6 were waited for; matrix products, arithmetic and copies ran while one was open for 0% of the time, Pallas kernels for 3%

profile of v6, /device:TPU:0, one launch (start us, length us, event | category | flops | bytes accessed | tf_op | source)
XLA Modules:
  0.0 50.3 jit_solution(3884647898164994840)
XLA Ops:
  0.0 0.0 copy-start
  0.0 0.8 %convert_bitcast_fusion = bf16[2,27]{1,0:T(2,128)(2,1)S(1)} fusion(s32[1,1,2,27]{3,2,1,0:T(2,128)} %param.3), kind=kLoop, calls=%fused_computation | loop fusion | flops 54 | bytes 324 | tf_op jit(solution)/shard_map/convert_element_type | solution.py:187
  0.8 0.3 broadcast_in_dim.4.refs_0_.refs_1_.refs_4_
  1.1 0.4 copy-done
  1.5 0.6 %pack.1 = (bf16[9,256,256]{2,1,0:T(8,128)(2,1)S(1)}, bf16[4,256,256]{2,1,0:T(8,128)(2,1)S(1)}, bf16[2,256,256]{2,1,0:T(8,128)(2,1)S(1)}, bf16[2,256,256]{2,1,0:T...) custom-call(bf16[2,27,128,128]{3,2,1,0:T(8,128)(2,1)S(1)} %broadcast, ...), custom_call_target="tpu_custom_call" | custom-call | tf_op jit(solution)/shard_map/pack/pallas_call | solution.py:189
  2.1 3.1 %collective-permute-start = (bf16[4,256,256]{2,1,0:T(8,128)(2,1)S(1)}, bf16[4,256,256]{2,1,0:T(8,128)(2,1)S(1)}, u32[]{:S(2)}, u32[]{:S(2)}) collective-permute-start(bf16[4,256,256]{2,1,0:T(8,128)(2,1)S(1)} %get-tuple-element.40), channel_id=1, source_target_pairs={{0,1},{1,2},{2,3},{3,0},{4,5},{5,6},{6,7},{7,4},{8,9},{9,10},{10,1... | collective-permute-start | bytes 1572872 | tf_op jit(solution)/shard_map/ppermute | solution.py:212
  5.1 0.0 collective-permute-start.5
  5.2 1.6 %collective-permute-start.2 = (bf16[6,256,256]{2,1,0:T(8,128)(2,1)S(1)}, bf16[6,256,256]{2,1,0:T(8,128)(2,1)S(1)}, u32[]{:S(2)}, u32[]{:S(2)}) collective-permute-start(bf16[6,256,256]{2,1,0:T(8,128)(2,1)S(1)} %get-tuple-element.44), channel_id=1, source_target_pairs={{4,8},{8,4},{12,0},{0,12},{5,9},{9,5},{13,1},{1,13},{6,10},{10,6},... | collective-permute-start | bytes 2359304 | tf_op jit(solution)/shard_map/ppermute | solution.py:212
  6.8 12.3 %collective-permute-done.refs_4_.refs_14_ = bf16[4,256,256]{2,1,0:T(8,128)(2,1)S(1)} collective-permute-done((bf16[4,256,256]{2,1,0:T(8,128)(2,1)S(1)}, bf16[4,256,256]{2,1,0:T(8,128)(2,1)S(1)}, u32[]{:S(2)}, u32[]{:S(2)}) %collective-permute-start) | collective-permute-done | bytes 524320 | tf_op jit(solution)/shard_map/ppermute | solution.py:212
  19.1 1.7 %collective-permute-start.4 = (bf16[2,256,256]{2,1,0:T(8,128)(2,1)S(1)}, bf16[2,256,256]{2,1,0:T(8,128)(2,1)S(1)}, u32[]{:S(2)}, u32[]{:S(2)}) collective-permute-start(bf16[2,256,256]{2,1,0:T(8,128)(2,1)S(1)} %get-tuple-element.47), channel_id=1, source_target_pairs={{0,3},{1,0},{2,1},{3,2},{4,7},{5,4},{6,5},{7,6},{8,11},{9,8},{10,9... | collective-permute-start | bytes 786440 | tf_op jit(solution)/shard_map/ppermute | solution.py:212
  20.8 0.0 collective-permute-start.3
  20.8 0.4 collective-permute-start.1
  21.3 6.8 %collective-permute-done.4.refs_1_ = bf16[2,256,256]{2,1,0:T(8,128)(2,1)S(1)} collective-permute-done((bf16[2,256,256]{2,1,0:T(8,128)(2,1)S(1)}, bf16[2,256,256]{2,1,0:T(8,128)(2,1)S(1)}, u32[]{:S(2)}, u32[]{:S(2)}) %collective-permute-start.4) | collective-permute-done | bytes 262176 | tf_op jit(solution)/shard_map/ppermute | solution.py:212
  28.1 0.0 collective-permute-done.5.refs_8_
  28.1 0.0 collective-permute-start.7
  28.1 0.0 collective-permute-done.2.refs_1_.refs_18_
  28.1 3.9 %collective-permute-start.8 = (bf16[2,256,256]{2,1,0:T(8,128)(2,1)S(1)}, bf16[2,256,256]{2,1,0:T(8,128)(2,1)S(1)}, u32[]{:S(2)}, u32[]{:S(2)}) collective-permute-start(bf16[2,256,256]{2,1,0:T(8,128)(2,1)S(1)} %get-tuple-element.58), channel_id=1, source_target_pairs={{0,3},{1,0},{2,1},{3,2},{4,7},{5,4},{6,5},{7,6},{8,11},{9,8},{10,9... | collective-permute-start | bytes 786440 | tf_op jit(solution)/shard_map/ppermute | solution.py:212
  31.9 1.3 %collective-permute-start.9 = (bf16[2,256,256]{2,1,0:T(8,128)(2,1)S(1)}, bf16[2,256,256]{2,1,0:T(8,128)(2,1)S(1)}, u32[]{:S(2)}, u32[]{:S(2)}) collective-permute-start(bf16[2,256,256]{2,1,0:T(8,128)(2,1)S(1)} %collective-permute-done.4.refs_1_), channel_id=1, source_target_pairs={{4,8},{8,4},{12,0},{0,12},{5,9},{9,5},{13,1},{1,13},{6,10},{10,6},... | collective-permute-start | bytes 786440 | tf_op jit(solution)/shard_map/ppermute | solution.py:212
  33.2 0.0 collective-permute-done.1.refs_0_.refs_2_
  33.2 0.0 collective-permute-start.6
  33.2 2.7 %collective-permute-done.3.refs_2_.refs_5_ = bf16[4,256,256]{2,1,0:T(8,128)(2,1)S(1)} collective-permute-done((bf16[4,256,256]{2,1,0:T(8,128)(2,1)S(1)}, bf16[4,256,256]{2,1,0:T(8,128)(2,1)S(1)}, u32[]{:S(2)}, u32[]{:S(2)}) %collective-permute-start.3) | collective-permute-done | bytes 524320 | tf_op jit(solution)/shard_map/ppermute | solution.py:212
  35.9 2.2 %collective-permute-start.13 = (bf16[2,256,256]{2,1,0:T(8,128)(2,1)S(1)}, bf16[2,256,256]{2,1,0:T(8,128)(2,1)S(1)}, u32[]{:S(2)}, u32[]{:S(2)}) collective-permute-start(bf16[2,256,256]{2,1,0:T(8,128)(2,1)S(1)} %collective-permute-done.1.refs_0_.refs_2_), channel_id=1, source_target_pairs={{4,8},{8,4},{12,0},{0,12},{5,9},{9,5},{13,1},{1,13},{6,10},{10,6},... | collective-permute-start | bytes 786440 | tf_op jit(solution)/shard_map/ppermute | solution.py:212
  38.1 0.8 %product0.1.refs_3_.refs_12_ = f32[9,256,256]{2,1,0:T(8,128)S(1)} custom-call(bf16[9,256,256]{2,1,0:T(8,128)(2,1)S(1)} %get-tuple-element.43.refs_0_.refs_2_.refs_5_, bf16[6,256,256]{2,1,0:T(8,128)(2,1)S(1)} %collective-permute-done.2.refs_1_.refs_18_, bf16[4,256,256]{2,1,0:T(8,128)(2,1)S(1)} %collective-permute-done.3.refs_2_.refs_5_), custom_call_target="tpu_custom_call" | custom-call | flops 1 | bytes 1 | tf_op jit(solution)/shard_map/product0/pallas_call | solution.py:248
  38.9 0.0 collective-permute-done.8.refs_3_
  38.9 0.1 collective-permute-start.11
  39.0 2.5 %collective-permute-done.9.refs_16_ = bf16[2,256,256]{2,1,0:T(8,128)(2,1)S(1)} collective-permute-done((bf16[2,256,256]{2,1,0:T(8,128)(2,1)S(1)}, bf16[2,256,256]{2,1,0:T(8,128)(2,1)S(1)}, u32[]{:S(2)}, u32[]{:S(2)}) %collective-permute-start.9) | collective-permute-done | bytes 262176 | tf_op jit(solution)/shard_map/ppermute | solution.py:212
  41.5 1.1 %collective-permute-start.10 = (bf16[2,256,256]{2,1,0:T(8,128)(2,1)S(1)}, bf16[2,256,256]{2,1,0:T(8,128)(2,1)S(1)}, u32[]{:S(2)}, u32[]{:S(2)}) collective-permute-start(bf16[2,256,256]{2,1,0:T(8,128)(2,1)S(1)} %collective-permute-done.4.refs_1_), channel_id=1, source_target_pairs={{0,4},{4,0},{8,12},{12,8},{1,5},{5,1},{9,13},{13,9},{2,6},{6,2},{1... | collective-permute-start | bytes 786440 | tf_op jit(solution)/shard_map/ppermute | solution.py:212
  42.6 1.9 %collective-permute-done.6.refs_15_ = bf16[2,256,256]{2,1,0:T(8,128)(2,1)S(1)} collective-permute-done((bf16[2,256,256]{2,1,0:T(8,128)(2,1)S(1)}, bf16[2,256,256]{2,1,0:T(8,128)(2,1)S(1)}, u32[]{:S(2)}, u32[]{:S(2)}) %collective-permute-start.6) | collective-permute-done | bytes 262176 | tf_op jit(solution)/shard_map/ppermute | solution.py:212
  44.5 0.0 collective-permute-done.7.refs_9_
  44.5 0.0 collective-permute-start.12
  44.5 0.5 %product1.1 = (f32[4,256,256]{2,1,0:T(8,128)S(1)}, bf16[1,256,256]{2,1,0:T(8,128)(2,1)S(1)}, f32[4,256,256]{2,1,0:T(8,128)S(1)}) custom-call(bf16[2,256,256]{2,1,0:T(8,128)(2,1)S(1)} %collective-permute-done.1.refs_0_.refs_2_, bf16[2,27,128,128]{3,2,1,0:T(8,128)(2,1)S(1)} %broadcast_in_dim.4.refs_0_.refs_1_.refs_4_, ...), custom_call_target="tpu_custom_call" | custom-call | flops 1 | bytes 1 | tf_op jit(solution)/shard_map/product1/pallas_call | solution.py:248
  45.0 1.8 %collective-permute-done.13.refs_17_ = bf16[2,256,256]{2,1,0:T(8,128)(2,1)S(1)} collective-permute-done((bf16[2,256,256]{2,1,0:T(8,128)(2,1)S(1)}, bf16[2,256,256]{2,1,0:T(8,128)(2,1)S(1)}, u32[]{:S(2)}, u32[]{:S(2)}) %collective-permute-start.13) | collective-permute-done | bytes 262176 | tf_op jit(solution)/shard_map/ppermute | solution.py:212
  46.8 0.0 collective-permute-done.11.refs_7_
  46.8 0.0 collective-permute-done.10.refs_6_
  46.8 0.0 collective-permute-done.12.refs_10_
  46.8 3.5 %product2.1 = bf16[2,27,128,128]{3,2,1,0:T(8,128)(2,1)} custom-call(f32[4,256,256]{2,1,0:T(8,128)S(1)} %get-tuple-element.46.refs_0_, bf16[2,256,256]{2,1,0:T(8,128)(2,1)S(1)} %collective-permute-done.4.refs_1_, bf16[2,256,256]{2,1,0:T(8,128)(2,1)S(1)} %collective-permute-done.1.refs_0_.refs_2_, bf16[2,256,256]{2,1,0:T(8,128)(2,1)S(1)} %collective-permute-done.8.refs_3_, ...), custom_call_target="tpu_custom_call" | custom-call | flops 1 | bytes 1 | tf_op jit(solution)/shard_map/product2/pallas_call | solution.py:248
Async XLA Ops:
  0.0 1.5 %copy-start = (bf16[1,1,2,27,128,128]{5,4,3,2,1,0:T(8,128)(2,1)S(1)}, bf16[1,1,2,27,128,128]{5,4,3,2,1,0:T(8,128)(2,1)}, u32[]{:S(2)}) copy-start(bf16[1,1,2,27,128,128]{5,4,3,2,1,0:T(8,128)(2,1)} %param.2) | copy-start | bytes 5308420
  2.1 17.0 %collective-permute-start = (bf16[4,256,256]{2,1,0:T(8,128)(2,1)S(1)}, bf16[4,256,256]{2,1,0:T(8,128)(2,1)S(1)}, u32[]{:S(2)}, u32[]{:S(2)}) collective-permute-start(bf16[4,256,256]{2,1,0:T(8,128)(2,1)S(1)} %get-tuple-element.40), channel_id=1, source_target_pairs={{0,1},{1,2},{2,3},{3,0},{4,5},{5,6},{6,7},{7,4},{8,9},{9,10},{10,1... | collective-permute-start | bytes 1572872 | tf_op jit(solution)/shard_map/ppermute | solution.py:212
  5.1 22.9 %collective-permute-start.5 = (bf16[6,256,256]{2,1,0:T(8,128)(2,1)S(1)}, bf16[6,256,256]{2,1,0:T(8,128)(2,1)S(1)}, u32[]{:S(2)}, u32[]{:S(2)}) collective-permute-start(bf16[6,256,256]{2,1,0:T(8,128)(2,1)S(1)} %get-tuple-element.48), channel_id=1, source_target_pairs={{0,4},{4,0},{8,12},{12,8},{1,5},{5,1},{9,13},{13,9},{2,6},{6,2},{1... | collective-permute-start | bytes 2359304 | tf_op jit(solution)/shard_map/ppermute | solution.py:212
  5.2 22.9 %collective-permute-start.2 = (bf16[6,256,256]{2,1,0:T(8,128)(2,1)S(1)}, bf16[6,256,256]{2,1,0:T(8,128)(2,1)S(1)}, u32[]{:S(2)}, u32[]{:S(2)}) collective-permute-start(bf16[6,256,256]{2,1,0:T(8,128)(2,1)S(1)} %get-tuple-element.44), channel_id=1, source_target_pairs={{4,8},{8,4},{12,0},{0,12},{5,9},{9,5},{13,1},{1,13},{6,10},{10,6},... | collective-permute-start | bytes 2359304 | tf_op jit(solution)/shard_map/ppermute | solution.py:212
  19.1 9.0 %collective-permute-start.4 = (bf16[2,256,256]{2,1,0:T(8,128)(2,1)S(1)}, bf16[2,256,256]{2,1,0:T(8,128)(2,1)S(1)}, u32[]{:S(2)}, u32[]{:S(2)}) collective-permute-start(bf16[2,256,256]{2,1,0:T(8,128)(2,1)S(1)} %get-tuple-element.47), channel_id=1, source_target_pairs={{0,3},{1,0},{2,1},{3,2},{4,7},{5,4},{6,5},{7,6},{8,11},{9,8},{10,9... | collective-permute-start | bytes 786440 | tf_op jit(solution)/shard_map/ppermute | solution.py:212
  20.8 15.0 %collective-permute-start.3 = (bf16[4,256,256]{2,1,0:T(8,128)(2,1)S(1)}, bf16[4,256,256]{2,1,0:T(8,128)(2,1)S(1)}, u32[]{:S(2)}, u32[]{:S(2)}) collective-permute-start(bf16[4,256,256]{2,1,0:T(8,128)(2,1)S(1)} %collective-permute-done.refs_4_.refs_14_), channel_id=1, source_target_pairs={{4,8},{8,4},{12,0},{0,12},{5,9},{9,5},{13,1},{1,13},{6,10},{10,6},... | collective-permute-start | bytes 1572872 | tf_op jit(solution)/shard_map/ppermute | solution.py:212
  20.8 12.4 %collective-permute-start.1 = (bf16[2,256,256]{2,1,0:T(8,128)(2,1)S(1)}, bf16[2,256,256]{2,1,0:T(8,128)(2,1)S(1)}, u32[]{:S(2)}, u32[]{:S(2)}) collective-permute-start(bf16[2,256,256]{2,1,0:T(8,128)(2,1)S(1)} %get-tuple-element.42), channel_id=1, source_target_pairs={{0,3},{1,0},{2,1},{3,2},{4,7},{5,4},{6,5},{7,6},{8,11},{9,8},{10,9... | collective-permute-start | bytes 786440 | tf_op jit(solution)/shard_map/ppermute | solution.py:212
  28.1 16.4 %collective-permute-start.7 = (bf16[4,256,256]{2,1,0:T(8,128)(2,1)S(1)}, bf16[4,256,256]{2,1,0:T(8,128)(2,1)S(1)}, u32[]{:S(2)}, u32[]{:S(2)}) collective-permute-start(bf16[4,256,256]{2,1,0:T(8,128)(2,1)S(1)} %collective-permute-done.refs_4_.refs_14_), channel_id=1, source_target_pairs={{0,4},{4,0},{8,12},{12,8},{1,5},{5,1},{9,13},{13,9},{2,6},{6,2},{1... | collective-permute-start | bytes 1572872 | tf_op jit(solution)/shard_map/ppermute | solution.py:212
  28.1 10.8 %collective-permute-start.8 = (bf16[2,256,256]{2,1,0:T(8,128)(2,1)S(1)}, bf16[2,256,256]{2,1,0:T(8,128)(2,1)S(1)}, u32[]{:S(2)}, u32[]{:S(2)}) collective-permute-start(bf16[2,256,256]{2,1,0:T(8,128)(2,1)S(1)} %get-tuple-element.58), channel_id=1, source_target_pairs={{0,3},{1,0},{2,1},{3,2},{4,7},{5,4},{6,5},{7,6},{8,11},{9,8},{10,9... | collective-permute-start | bytes 786440 | tf_op jit(solution)/shard_map/ppermute | solution.py:212
  31.9 9.6 %collective-permute-start.9 = (bf16[2,256,256]{2,1,0:T(8,128)(2,1)S(1)}, bf16[2,256,256]{2,1,0:T(8,128)(2,1)S(1)}, u32[]{:S(2)}, u32[]{:S(2)}) collective-permute-start(bf16[2,256,256]{2,1,0:T(8,128)(2,1)S(1)} %collective-permute-done.4.refs_1_), channel_id=1, source_target_pairs={{4,8},{8,4},{12,0},{0,12},{5,9},{9,5},{13,1},{1,13},{6,10},{10,6},... | collective-permute-start | bytes 786440 | tf_op jit(solution)/shard_map/ppermute | solution.py:212
  33.2 11.3 %collective-permute-start.6 = (bf16[2,256,256]{2,1,0:T(8,128)(2,1)S(1)}, bf16[2,256,256]{2,1,0:T(8,128)(2,1)S(1)}, u32[]{:S(2)}, u32[]{:S(2)}) collective-permute-start(bf16[2,256,256]{2,1,0:T(8,128)(2,1)S(1)} %get-tuple-element.55), channel_id=1, source_target_pairs={{0,1},{1,2},{2,3},{3,0},{4,5},{5,6},{6,7},{7,4},{8,9},{9,10},{10,1... | collective-permute-start | bytes 786440 | tf_op jit(solution)/shard_map/ppermute | solution.py:212
  35.9 10.9 %collective-permute-start.13 = (bf16[2,256,256]{2,1,0:T(8,128)(2,1)S(1)}, bf16[2,256,256]{2,1,0:T(8,128)(2,1)S(1)}, u32[]{:S(2)}, u32[]{:S(2)}) collective-permute-start(bf16[2,256,256]{2,1,0:T(8,128)(2,1)S(1)} %collective-permute-done.1.refs_0_.refs_2_), channel_id=1, source_target_pairs={{4,8},{8,4},{12,0},{0,12},{5,9},{9,5},{13,1},{1,13},{6,10},{10,6},... | collective-permute-start | bytes 786440 | tf_op jit(solution)/shard_map/ppermute | solution.py:212
  38.9 7.9 %collective-permute-start.11 = (bf16[2,256,256]{2,1,0:T(8,128)(2,1)S(1)}, bf16[2,256,256]{2,1,0:T(8,128)(2,1)S(1)}, u32[]{:S(2)}, u32[]{:S(2)}) collective-permute-start(bf16[2,256,256]{2,1,0:T(8,128)(2,1)S(1)} %collective-permute-done.8.refs_3_), channel_id=1, source_target_pairs={{0,4},{4,0},{8,12},{12,8},{1,5},{5,1},{9,13},{13,9},{2,6},{6,2},{1... | collective-permute-start | bytes 786440 | tf_op jit(solution)/shard_map/ppermute | solution.py:212
  41.5 5.3 %collective-permute-start.10 = (bf16[2,256,256]{2,1,0:T(8,128)(2,1)S(1)}, bf16[2,256,256]{2,1,0:T(8,128)(2,1)S(1)}, u32[]{:S(2)}, u32[]{:S(2)}) collective-permute-start(bf16[2,256,256]{2,1,0:T(8,128)(2,1)S(1)} %collective-permute-done.4.refs_1_), channel_id=1, source_target_pairs={{0,4},{4,0},{8,12},{12,8},{1,5},{5,1},{9,13},{13,9},{2,6},{6,2},{1... | collective-permute-start | bytes 786440 | tf_op jit(solution)/shard_map/ppermute | solution.py:212
  44.5 2.3 %collective-permute-start.12 = (bf16[2,256,256]{2,1,0:T(8,128)(2,1)S(1)}, bf16[2,256,256]{2,1,0:T(8,128)(2,1)S(1)}, u32[]{:S(2)}, u32[]{:S(2)}) collective-permute-start(bf16[2,256,256]{2,1,0:T(8,128)(2,1)S(1)} %collective-permute-done.6.refs_15_), channel_id=1, source_target_pairs={{0,4},{4,0},{8,12},{12,8},{1,5},{5,1},{9,13},{13,9},{2,6},{6,2},{1... | collective-permute-start | bytes 786440 | tf_op jit(solution)/shard_map/ppermute | solution.py:212

commit v7 on v6

--- a/solution.py
+++ b/solution.py
@@ -15,8 +15,11 @@
     1: {"up": [(0, 0), (0, 1), (1, 0), (1, 1)], "up_rest": [(-1, 0), (-1, 1)]},
     -1: {"down0": [(0, -1), (0, 0)], "down1": [(1, -1), (1, 0)], "down2": [(-1, -1), (-1, 0)]},
 }
-STAGES = [['mat', 'x_in', 'x_up'], ['up', 'down1'],
- ['up_rest', 'down2', 'x_down0', 'x_down1', 'n_in', 'n_up', 'n_down2', 'down0', 'n_down0', 'n_up_rest']]
+STAGES = [
+    ["mat", "x_in", "x_up"],
+    ["up", "down1", "down0"],
+    ["up_rest", "down2", "x_down0", "x_down1", "n_in", "n_up", "n_down2", "n_down0", "n_up_rest"],
+]
 SCHEDULE = [('x_in', []), ('up', []), ('x_up', []), (0, []), ('down0', ['up']), ('down1', ['up']), (1, []),
  ('up_rest', ['x_in']), ('down2', ['x_in']), ('x_down0', []), ('x_down1', ['x_up']), ('n_in', []),
  ('n_up', ['down0', 'n_in']), ('n_down0', ['sum_0', 'x_in']), ('n_down2', ['sum_0']),

time: 50.4 us -> 50.4 us (level)
  no operation moved by 1% of the time
where the time goes in v7:
time: 50.4 us; the launch traced here: 50.2 us
  waiting for transfers between devices  27.9 us (55%)
  starting transfers between devices  15.4 us (31%)
  Pallas kernels  5.35 us (11%)
  other arithmetic  0.81 us (2%)
  local copies, waits for them, and re-layouts  0.67 us (1%)
    ppermute x14, waiting for transfers between devices, move(): arrays[name] = lax.ppermute(operand, axis, towards)  27.9 us
    ppermute x14, starting transfers between devices, move(): arrays[name] = lax.ppermute(operand, axis, towards)  15.4 us
    pallas_call x3, Pallas kernels, multiply(): pl.pallas_call(body, out_shape=jax.ShapeDtypeStruct(blocks.shape, dtype)...  4.77 us
  transfers between devices with their start and end apart: 14, of which 6 were waited for; matrix products, arithmetic and copies ran while one was open for 0% of the time, Pallas kernels for 3%

profile of v7, /device:TPU:0, one launch (start us, length us, event | category | flops | bytes accessed | tf_op | source)
XLA Modules:
  0.0 50.2 jit_solution(4983864149653047297)
XLA Ops:
  0.0 0.0 copy-start
  0.0 0.8 %convert_bitcast_fusion = bf16[2,27]{1,0:T(2,128)(2,1)S(1)} fusion(s32[1,1,2,27]{3,2,1,0:T(2,128)} %param.3), kind=kLoop, calls=%fused_computation | loop fusion | flops 54 | bytes 324 | tf_op jit(solution)/shard_map/convert_element_type | solution.py:190
  0.8 0.3 broadcast_in_dim.4.refs_0_.refs_2_.refs_4_
  1.1 0.4 copy-done
  1.5 0.6 %pack.1 = (bf16[9,256,256]{2,1,0:T(8,128)(2,1)S(1)}, bf16[4,256,256]{2,1,0:T(8,128)(2,1)S(1)}, bf16[2,256,256]{2,1,0:T(8,128)(2,1)S(1)}, bf16[2,256,256]{2,1,0:T...) custom-call(bf16[2,27,128,128]{3,2,1,0:T(8,128)(2,1)S(1)} %broadcast, ...), custom_call_target="tpu_custom_call" | custom-call | tf_op jit(solution)/shard_map/pack/pallas_call | solution.py:192
  2.1 3.1 %collective-permute-start = (bf16[4,256,256]{2,1,0:T(8,128)(2,1)S(1)}, bf16[4,256,256]{2,1,0:T(8,128)(2,1)S(1)}, u32[]{:S(2)}, u32[]{:S(2)}) collective-permute-start(bf16[4,256,256]{2,1,0:T(8,128)(2,1)S(1)} %get-tuple-element.39), channel_id=1, source_target_pairs={{0,1},{1,2},{2,3},{3,0},{4,5},{5,6},{6,7},{7,4},{8,9},{9,10},{10,1... | collective-permute-start | bytes 1572872 | tf_op jit(solution)/shard_map/ppermute | solution.py:215
  5.1 0.0 collective-permute-start.5
  5.2 1.6 %collective-permute-start.3 = (bf16[6,256,256]{2,1,0:T(8,128)(2,1)S(1)}, bf16[6,256,256]{2,1,0:T(8,128)(2,1)S(1)}, u32[]{:S(2)}, u32[]{:S(2)}) collective-permute-start(bf16[6,256,256]{2,1,0:T(8,128)(2,1)S(1)} %get-tuple-element.45), channel_id=1, source_target_pairs={{4,8},{8,4},{12,0},{0,12},{5,9},{9,5},{13,1},{1,13},{6,10},{10,6},... | collective-permute-start | bytes 2359304 | tf_op jit(solution)/shard_map/ppermute | solution.py:215
  6.8 12.3 %collective-permute-done.refs_5_.refs_14_ = bf16[4,256,256]{2,1,0:T(8,128)(2,1)S(1)} collective-permute-done((bf16[4,256,256]{2,1,0:T(8,128)(2,1)S(1)}, bf16[4,256,256]{2,1,0:T(8,128)(2,1)S(1)}, u32[]{:S(2)}, u32[]{:S(2)}) %collective-permute-start) | collective-permute-done | bytes 524320 | tf_op jit(solution)/shard_map/ppermute | solution.py:215
  19.1 1.7 %collective-permute-start.1 = (bf16[2,256,256]{2,1,0:T(8,128)(2,1)S(1)}, bf16[2,256,256]{2,1,0:T(8,128)(2,1)S(1)}, u32[]{:S(2)}, u32[]{:S(2)}) collective-permute-start(bf16[2,256,256]{2,1,0:T(8,128)(2,1)S(1)} %get-tuple-element.40), channel_id=1, source_target_pairs={{0,3},{1,0},{2,1},{3,2},{4,7},{5,4},{6,5},{7,6},{8,11},{9,8},{10,9... | collective-permute-start | bytes 786440 | tf_op jit(solution)/shard_map/ppermute | solution.py:215
  20.8 0.0 collective-permute-start.4
  20.8 0.4 collective-permute-start.2
  21.3 6.8 %collective-permute-done.1.refs_0_.refs_1_ = bf16[2,256,256]{2,1,0:T(8,128)(2,1)S(1)} collective-permute-done((bf16[2,256,256]{2,1,0:T(8,128)(2,1)S(1)}, bf16[2,256,256]{2,1,0:T(8,128)(2,1)S(1)}, u32[]{:S(2)}, u32[]{:S(2)}) %collective-permute-start.1) | collective-permute-done | bytes 262176 | tf_op jit(solution)/shard_map/ppermute | solution.py:215
  28.1 0.0 collective-permute-done.5.refs_8_
  28.1 0.0 collective-permute-start.7
  28.1 0.0 collective-permute-done.3.refs_1_.refs_18_
  28.1 3.9 %collective-permute-start.8 = (bf16[2,256,256]{2,1,0:T(8,128)(2,1)S(1)}, bf16[2,256,256]{2,1,0:T(8,128)(2,1)S(1)}, u32[]{:S(2)}, u32[]{:S(2)}) collective-permute-start(bf16[2,256,256]{2,1,0:T(8,128)(2,1)S(1)} %get-tuple-element.58), channel_id=1, source_target_pairs={{0,3},{1,0},{2,1},{3,2},{4,7},{5,4},{6,5},{7,6},{8,11},{9,8},{10,9... | collective-permute-start | bytes 786440 | tf_op jit(solution)/shard_map/ppermute | solution.py:215
  31.9 1.3 %collective-permute-start.9 = (bf16[2,256,256]{2,1,0:T(8,128)(2,1)S(1)}, bf16[2,256,256]{2,1,0:T(8,128)(2,1)S(1)}, u32[]{:S(2)}, u32[]{:S(2)}) collective-permute-start(bf16[2,256,256]{2,1,0:T(8,128)(2,1)S(1)} %collective-permute-done.1.refs_0_.refs_1_), channel_id=1, source_target_pairs={{4,8},{8,4},{12,0},{0,12},{5,9},{9,5},{13,1},{1,13},{6,10},{10,6},... | collective-permute-start | bytes 786440 | tf_op jit(solution)/shard_map/ppermute | solution.py:215
  33.2 0.0 collective-permute-done.2.refs_1_.refs_2_
  33.2 0.0 collective-permute-start.6
  33.2 2.7 %collective-permute-done.4.refs_2_.refs_6_ = bf16[4,256,256]{2,1,0:T(8,128)(2,1)S(1)} collective-permute-done((bf16[4,256,256]{2,1,0:T(8,128)(2,1)S(1)}, bf16[4,256,256]{2,1,0:T(8,128)(2,1)S(1)}, u32[]{:S(2)}, u32[]{:S(2)}) %collective-permute-start.4) | collective-permute-done | bytes 524320 | tf_op jit(solution)/shard_map/ppermute | solution.py:215
  35.9 2.2 %collective-permute-start.13 = (bf16[2,256,256]{2,1,0:T(8,128)(2,1)S(1)}, bf16[2,256,256]{2,1,0:T(8,128)(2,1)S(1)}, u32[]{:S(2)}, u32[]{:S(2)}) collective-permute-start(bf16[2,256,256]{2,1,0:T(8,128)(2,1)S(1)} %collective-permute-done.2.refs_1_.refs_2_), channel_id=1, source_target_pairs={{4,8},{8,4},{12,0},{0,12},{5,9},{9,5},{13,1},{1,13},{6,10},{10,6},... | collective-permute-start | bytes 786440 | tf_op jit(solution)/shard_map/ppermute | solution.py:215
  38.1 0.8 %product0.1.refs_4_.refs_12_ = f32[9,256,256]{2,1,0:T(8,128)S(1)} custom-call(bf16[9,256,256]{2,1,0:T(8,128)(2,1)S(1)} %get-tuple-element.44.refs_0_.refs_3_.refs_5_, bf16[6,256,256]{2,1,0:T(8,128)(2,1)S(1)} %collective-permute-done.3.refs_1_.refs_18_, bf16[4,256,256]{2,1,0:T(8,128)(2,1)S(1)} %collective-permute-done.4.refs_2_.refs_6_), custom_call_target="tpu_custom_call" | custom-call | flops 1 | bytes 1 | tf_op jit(solution)/shard_map/product0/pallas_call | solution.py:251
  38.9 0.0 collective-permute-done.8.refs_3_
  38.9 0.1 collective-permute-start.11
  39.0 2.5 %collective-permute-done.9.refs_16_ = bf16[2,256,256]{2,1,0:T(8,128)(2,1)S(1)} collective-permute-done((bf16[2,256,256]{2,1,0:T(8,128)(2,1)S(1)}, bf16[2,256,256]{2,1,0:T(8,128)(2,1)S(1)}, u32[]{:S(2)}, u32[]{:S(2)}) %collective-permute-start.9) | collective-permute-done | bytes 262176 | tf_op jit(solution)/shard_map/ppermute | solution.py:215
  41.5 1.1 %collective-permute-start.10 = (bf16[2,256,256]{2,1,0:T(8,128)(2,1)S(1)}, bf16[2,256,256]{2,1,0:T(8,128)(2,1)S(1)}, u32[]{:S(2)}, u32[]{:S(2)}) collective-permute-start(bf16[2,256,256]{2,1,0:T(8,128)(2,1)S(1)} %collective-permute-done.1.refs_0_.refs_1_), channel_id=1, source_target_pairs={{0,4},{4,0},{8,12},{12,8},{1,5},{5,1},{9,13},{13,9},{2,6},{6,2},{1... | collective-permute-start | bytes 786440 | tf_op jit(solution)/shard_map/ppermute | solution.py:215
  42.6 1.9 %collective-permute-done.6.refs_15_ = bf16[2,256,256]{2,1,0:T(8,128)(2,1)S(1)} collective-permute-done((bf16[2,256,256]{2,1,0:T(8,128)(2,1)S(1)}, bf16[2,256,256]{2,1,0:T(8,128)(2,1)S(1)}, u32[]{:S(2)}, u32[]{:S(2)}) %collective-permute-start.6) | collective-permute-done | bytes 262176 | tf_op jit(solution)/shard_map/ppermute | solution.py:215
  44.5 0.0 collective-permute-done.7.refs_9_
  44.5 0.0 collective-permute-start.12
  44.5 0.6 %product1.1 = (f32[5,256,256]{2,1,0:T(8,128)S(1)}, bf16[1,256,256]{2,1,0:T(8,128)(2,1)S(1)}, f32[4,256,256]{2,1,0:T(8,128)S(1)}) custom-call(bf16[2,256,256]{2,1,0:T(8,128)(2,1)S(1)} %collective-permute-done.1.refs_0_.refs_1_, bf16[2,256,256]{2,1,0:T(8,128)(2,1)S(1)} %collective-permute-done.2.refs_1_.refs_2_, ...), custom_call_target="tpu_custom_call" | custom-call | flops 1 | bytes 1 | tf_op jit(solution)/shard_map/product1/pallas_call | solution.py:251
  45.1 1.7 %collective-permute-done.13.refs_17_ = bf16[2,256,256]{2,1,0:T(8,128)(2,1)S(1)} collective-permute-done((bf16[2,256,256]{2,1,0:T(8,128)(2,1)S(1)}, bf16[2,256,256]{2,1,0:T(8,128)(2,1)S(1)}, u32[]{:S(2)}, u32[]{:S(2)}) %collective-permute-start.13) | collective-permute-done | bytes 262176 | tf_op jit(solution)/shard_map/ppermute | solution.py:215
  46.8 0.0 collective-permute-done.11.refs_7_
  46.8 0.0 collective-permute-done.10.refs_6_
  46.8 0.0 collective-permute-done.12.refs_10_
  46.8 3.4 %product2.1 = bf16[2,27,128,128]{3,2,1,0:T(8,128)(2,1)} custom-call(f32[4,256,256]{2,1,0:T(8,128)S(1)} %get-tuple-element.47.refs_0_, bf16[2,256,256]{2,1,0:T(8,128)(2,1)S(1)} %collective-permute-done.1.refs_0_.refs_1_, bf16[2,256,256]{2,1,0:T(8,128)(2,1)S(1)} %collective-permute-done.2.refs_1_.refs_2_, ...), custom_call_target="tpu_custom_call" | custom-call | flops 1 | bytes 1 | tf_op jit(solution)/shard_map/product2/pallas_call | solution.py:251
Async XLA Ops:
  0.0 1.5 %copy-start = (bf16[1,1,2,27,128,128]{5,4,3,2,1,0:T(8,128)(2,1)S(1)}, bf16[1,1,2,27,128,128]{5,4,3,2,1,0:T(8,128)(2,1)}, u32[]{:S(2)}) copy-start(bf16[1,1,2,27,128,128]{5,4,3,2,1,0:T(8,128)(2,1)} %param.2) | copy-start | bytes 5308420
  2.1 17.0 %collective-permute-start = (bf16[4,256,256]{2,1,0:T(8,128)(2,1)S(1)}, bf16[4,256,256]{2,1,0:T(8,128)(2,1)S(1)}, u32[]{:S(2)}, u32[]{:S(2)}) collective-permute-start(bf16[4,256,256]{2,1,0:T(8,128)(2,1)S(1)} %get-tuple-element.39), channel_id=1, source_target_pairs={{0,1},{1,2},{2,3},{3,0},{4,5},{5,6},{6,7},{7,4},{8,9},{9,10},{10,1... | collective-permute-start | bytes 1572872 | tf_op jit(solution)/shard_map/ppermute | solution.py:215
  5.1 22.9 %collective-permute-start.5 = (bf16[6,256,256]{2,1,0:T(8,128)(2,1)S(1)}, bf16[6,256,256]{2,1,0:T(8,128)(2,1)S(1)}, u32[]{:S(2)}, u32[]{:S(2)}) collective-permute-start(bf16[6,256,256]{2,1,0:T(8,128)(2,1)S(1)} %get-tuple-element.48), channel_id=1, source_target_pairs={{0,4},{4,0},{8,12},{12,8},{1,5},{5,1},{9,13},{13,9},{2,6},{6,2},{1... | collective-permute-start | bytes 2359304 | tf_op jit(solution)/shard_map/ppermute | solution.py:215
  5.2 22.9 %collective-permute-start.3 = (bf16[6,256,256]{2,1,0:T(8,128)(2,1)S(1)}, bf16[6,256,256]{2,1,0:T(8,128)(2,1)S(1)}, u32[]{:S(2)}, u32[]{:S(2)}) collective-permute-start(bf16[6,256,256]{2,1,0:T(8,128)(2,1)S(1)} %get-tuple-element.45), channel_id=1, source_target_pairs={{4,8},{8,4},{12,0},{0,12},{5,9},{9,5},{13,1},{1,13},{6,10},{10,6},... | collective-permute-start | bytes 2359304 | tf_op jit(solution)/shard_map/ppermute | solution.py:215
  19.1 9.0 %collective-permute-start.1 = (bf16[2,256,256]{2,1,0:T(8,128)(2,1)S(1)}, bf16[2,256,256]{2,1,0:T(8,128)(2,1)S(1)}, u32[]{:S(2)}, u32[]{:S(2)}) collective-permute-start(bf16[2,256,256]{2,1,0:T(8,128)(2,1)S(1)} %get-tuple-element.40), channel_id=1, source_target_pairs={{0,3},{1,0},{2,1},{3,2},{4,7},{5,4},{6,5},{7,6},{8,11},{9,8},{10,9... | collective-permute-start | bytes 786440 | tf_op jit(solution)/shard_map/ppermute | solution.py:215
  20.8 15.0 %collective-permute-start.4 = (bf16[4,256,256]{2,1,0:T(8,128)(2,1)S(1)}, bf16[4,256,256]{2,1,0:T(8,128)(2,1)S(1)}, u32[]{:S(2)}, u32[]{:S(2)}) collective-permute-start(bf16[4,256,256]{2,1,0:T(8,128)(2,1)S(1)} %collective-permute-done.refs_5_.refs_14_), channel_id=1, source_target_pairs={{4,8},{8,4},{12,0},{0,12},{5,9},{9,5},{13,1},{1,13},{6,10},{10,6},... | collective-permute-start | bytes 1572872 | tf_op jit(solution)/shard_map/ppermute | solution.py:215
  20.8 12.4 %collective-permute-start.2 = (bf16[2,256,256]{2,1,0:T(8,128)(2,1)S(1)}, bf16[2,256,256]{2,1,0:T(8,128)(2,1)S(1)}, u32[]{:S(2)}, u32[]{:S(2)}) collective-permute-start(bf16[2,256,256]{2,1,0:T(8,128)(2,1)S(1)} %get-tuple-element.43), channel_id=1, source_target_pairs={{0,3},{1,0},{2,1},{3,2},{4,7},{5,4},{6,5},{7,6},{8,11},{9,8},{10,9... | collective-permute-start | bytes 786440 | tf_op jit(solution)/shard_map/ppermute | solution.py:215
  28.1 16.4 %collective-permute-start.7 = (bf16[4,256,256]{2,1,0:T(8,128)(2,1)S(1)}, bf16[4,256,256]{2,1,0:T(8,128)(2,1)S(1)}, u32[]{:S(2)}, u32[]{:S(2)}) collective-permute-start(bf16[4,256,256]{2,1,0:T(8,128)(2,1)S(1)} %collective-permute-done.refs_5_.refs_14_), channel_id=1, source_target_pairs={{0,4},{4,0},{8,12},{12,8},{1,5},{5,1},{9,13},{13,9},{2,6},{6,2},{1... | collective-permute-start | bytes 1572872 | tf_op jit(solution)/shard_map/ppermute | solution.py:215
  28.1 10.8 %collective-permute-start.8 = (bf16[2,256,256]{2,1,0:T(8,128)(2,1)S(1)}, bf16[2,256,256]{2,1,0:T(8,128)(2,1)S(1)}, u32[]{:S(2)}, u32[]{:S(2)}) collective-permute-start(bf16[2,256,256]{2,1,0:T(8,128)(2,1)S(1)} %get-tuple-element.58), channel_id=1, source_target_pairs={{0,3},{1,0},{2,1},{3,2},{4,7},{5,4},{6,5},{7,6},{8,11},{9,8},{10,9... | collective-permute-start | bytes 786440 | tf_op jit(solution)/shard_map/ppermute | solution.py:215
  31.9 9.6 %collective-permute-start.9 = (bf16[2,256,256]{2,1,0:T(8,128)(2,1)S(1)}, bf16[2,256,256]{2,1,0:T(8,128)(2,1)S(1)}, u32[]{:S(2)}, u32[]{:S(2)}) collective-permute-start(bf16[2,256,256]{2,1,0:T(8,128)(2,1)S(1)} %collective-permute-done.1.refs_0_.refs_1_), channel_id=1, source_target_pairs={{4,8},{8,4},{12,0},{0,12},{5,9},{9,5},{13,1},{1,13},{6,10},{10,6},... | collective-permute-start | bytes 786440 | tf_op jit(solution)/shard_map/ppermute | solution.py:215
  33.2 11.3 %collective-permute-start.6 = (bf16[2,256,256]{2,1,0:T(8,128)(2,1)S(1)}, bf16[2,256,256]{2,1,0:T(8,128)(2,1)S(1)}, u32[]{:S(2)}, u32[]{:S(2)}) collective-permute-start(bf16[2,256,256]{2,1,0:T(8,128)(2,1)S(1)} %get-tuple-element.55), channel_id=1, source_target_pairs={{0,1},{1,2},{2,3},{3,0},{4,5},{5,6},{6,7},{7,4},{8,9},{9,10},{10,1... | collective-permute-start | bytes 786440 | tf_op jit(solution)/shard_map/ppermute | solution.py:215
  35.9 10.9 %collective-permute-start.13 = (bf16[2,256,256]{2,1,0:T(8,128)(2,1)S(1)}, bf16[2,256,256]{2,1,0:T(8,128)(2,1)S(1)}, u32[]{:S(2)}, u32[]{:S(2)}) collective-permute-start(bf16[2,256,256]{2,1,0:T(8,128)(2,1)S(1)} %collective-permute-done.2.refs_1_.refs_2_), channel_id=1, source_target_pairs={{4,8},{8,4},{12,0},{0,12},{5,9},{9,5},{13,1},{1,13},{6,10},{10,6},... | collective-permute-start | bytes 786440 | tf_op jit(solution)/shard_map/ppermute | solution.py:215
  38.9 7.9 %collective-permute-start.11 = (bf16[2,256,256]{2,1,0:T(8,128)(2,1)S(1)}, bf16[2,256,256]{2,1,0:T(8,128)(2,1)S(1)}, u32[]{:S(2)}, u32[]{:S(2)}) collective-permute-start(bf16[2,256,256]{2,1,0:T(8,128)(2,1)S(1)} %collective-permute-done.8.refs_3_), channel_id=1, source_target_pairs={{0,4},{4,0},{8,12},{12,8},{1,5},{5,1},{9,13},{13,9},{2,6},{6,2},{1... | collective-permute-start | bytes 786440 | tf_op jit(solution)/shard_map/ppermute | solution.py:215
  41.5 5.3 %collective-permute-start.10 = (bf16[2,256,256]{2,1,0:T(8,128)(2,1)S(1)}, bf16[2,256,256]{2,1,0:T(8,128)(2,1)S(1)}, u32[]{:S(2)}, u32[]{:S(2)}) collective-permute-start(bf16[2,256,256]{2,1,0:T(8,128)(2,1)S(1)} %collective-permute-done.1.refs_0_.refs_1_), channel_id=1, source_target_pairs={{0,4},{4,0},{8,12},{12,8},{1,5},{5,1},{9,13},{13,9},{2,6},{6,2},{1... | collective-permute-start | bytes 786440 | tf_op jit(solution)/shard_map/ppermute | solution.py:215
  44.5 2.3 %collective-permute-start.12 = (bf16[2,256,256]{2,1,0:T(8,128)(2,1)S(1)}, bf16[2,256,256]{2,1,0:T(8,128)(2,1)S(1)}, u32[]{:S(2)}, u32[]{:S(2)}) collective-permute-start(bf16[2,256,256]{2,1,0:T(8,128)(2,1)S(1)} %collective-permute-done.6.refs_15_), channel_id=1, source_target_pairs={{0,4},{4,0},{8,12},{12,8},{1,5},{5,1},{9,13},{13,9},{2,6},{6,2},{1... | collective-permute-start | bytes 786440 | tf_op jit(solution)/shard_map/ppermute | solution.py:215
